TPU v7x, 32 devices: a whole 2x2x4 slice. The times are simulated.
32 devices in a mesh: narrow: 4 (over x, core), wide: 8 (over z, y).
Axes of the slice: x: 2, y: 2, z: 4, core: 2. Of those that a mesh axis runs over, the one named last changes fastest.
Arguments:
- tokens: bfloat16 [64, 16384], P('narrow', 'wide'), may hold values from -6 to 6
- w_query: bfloat16 [16384, 8192], P('wide', 'narrow'), may hold values from -0.046875 to 0.046875
- w_keyval: bfloat16 [16384, 1024], P('wide', 'narrow'), may hold values from -0.046875 to 0.046875
- w_output: bfloat16 [8192, 16384], P('narrow', 'wide'), may hold values from -0.0625 to 0.0625
- grad_out: bfloat16 [64, 16384], P('narrow', 'wide'), may hold values from -6 to 6
Outputs:
- output: bfloat16 [64, 16384], P('narrow', 'wide')
- grad_tokens: bfloat16 [64, 16384], P('narrow', 'wide')
- grad_wq: bfloat16 [16384, 8192], P('wide', 'narrow')
- grad_wkv: bfloat16 [16384, 1024], P('wide', 'narrow')
- grad_wo: bfloat16 [8192, 16384], P('narrow', 'wide')
All inputs are finite; a program needn't handle non-finite values.
Results may differ from a plain program's by a relative error of at most 0.015.
Values may be sent and summed in bfloat16 or wider, within the bound.
No kernel may reach another device: no remote copies, remote signals or barrier semaphores. Data moves between devices by JAX's collectives and lax.ppermute only.
A program may use at most 128 MiB of HBM per device.

v0:
```python
import jax
import jax.numpy as jnp
from jax import lax
from jax.sharding import PartitionSpec as P

HD = 128


def contract_rows(left, right):
    return lax.dot_general(
        left, right, (((0,), (0,)), ((), ())), preferred_element_type=jnp.float32
    )


def contract_cols(left, right):
    return lax.dot_general(
        left, right, (((1,), (1,)), ((), ())), preferred_element_type=jnp.float32
    )


def wide_sum(term_fn, all_rows):
    return lax.psum_scatter(
        term_fn(jnp.int32(0), lax.axis_size("wide") * (all_rows // lax.axis_size("wide"))),
        "wide",
        scatter_dimension=0,
        tiled=True,
    )


def shards(tokens, w_query, w_keyval, w_output, grad_out):
    wide_index = lax.axis_index("wide")
    token_panel = lax.all_gather(tokens, "narrow", axis=0, tiled=True)
    all_rows = token_panel.shape[0]
    query_cols = w_query.shape[1]
    pair_cols = w_keyval.shape[1]
    joined = jnp.concatenate([w_query, w_keyval], axis=1)

    def project_all(first_row, row_count):
        return jnp.dot(token_panel, joined, preferred_element_type=jnp.float32)

    projected = wide_sum(project_all, all_rows)
    queries = projected[:, :query_cols].astype(jnp.bfloat16)
    kv_own = projected[:, query_cols:].astype(jnp.bfloat16)
    kv_panel = lax.all_gather(kv_own, "wide", axis=0, tiled=True)
    rows_here = queries.shape[0]
    heads_here = query_cols // HD
    groups_here = pair_cols // (2 * HD)
    group_size = heads_here // groups_here
    score_scale = HD ** (-0.5)
    query_pos = wide_index * rows_here + lax.iota(jnp.int32, rows_here)
    key_pos = lax.iota(jnp.int32, all_rows)
    allowed = key_pos[None, :] <= query_pos[:, None]
    query_heads = queries.reshape(rows_here, groups_here, group_size, HD)
    pair_heads = kv_panel.reshape(all_rows, groups_here, 2, HD)
    key_heads = pair_heads[:, :, 0]
    value_heads = pair_heads[:, :, 1]
    scores = (
        jnp.einsum("rghd,sgd->ghrs", query_heads, key_heads, preferred_element_type=jnp.float32)
        * score_scale
    )
    weights = jnp.where(allowed, jnp.exp(scores), 0.0)
    weights = weights / jnp.sum(weights, axis=3, keepdims=True)
    prob_bf = weights.astype(jnp.bfloat16)
    attended = jnp.einsum(
        "ghrs,sgd->rghd", prob_bf, value_heads, preferred_element_type=jnp.float32
    )
    attended = attended.reshape(rows_here, query_cols).astype(jnp.bfloat16)
    att_panel = lax.all_gather(attended, "wide", axis=0, tiled=True)
    row_block = att_panel
    output = lax.psum_scatter(
        jnp.dot(row_block, w_output, preferred_element_type=jnp.float32).astype(jnp.bfloat16),
        "narrow",
        scatter_dimension=0,
        tiled=True,
    )
    grad_panel = lax.all_gather(grad_out, "narrow", axis=0, tiled=True)
    grad_wo = contract_rows(att_panel, grad_panel).astype(jnp.bfloat16)

    def back_out(first_row, row_count):
        return contract_cols(grad_panel, w_output)

    grad_att = wide_sum(back_out, all_rows).astype(jnp.bfloat16)
    grad_heads = grad_att.reshape(rows_here, groups_here, group_size, HD)
    prob_grad = jnp.einsum(
        "rghd,sgd->ghrs", grad_heads, value_heads, preferred_element_type=jnp.float32
    )
    grad_values = jnp.einsum(
        "ghrs,rghd->sgd", prob_bf, grad_heads, preferred_element_type=jnp.float32
    )
    score_grad = weights * (prob_grad - jnp.sum(weights * prob_grad, axis=3, keepdims=True))
    score_half = score_grad.astype(jnp.bfloat16)
    grad_q = (
        jnp.einsum("ghrs,sgd->rghd", score_half, key_heads, preferred_element_type=jnp.float32)
        * score_scale
    )
    grad_q = grad_q.reshape(rows_here, query_cols).astype(jnp.bfloat16)
    grad_keys = (
        jnp.einsum("ghrs,rghd->sgd", score_half, query_heads, preferred_element_type=jnp.float32)
        * score_scale
    )
    kv_grad = jnp.stack([grad_keys, grad_values], axis=2).reshape(all_rows, pair_cols)
    kv_share = lax.psum_scatter(kv_grad, "wide", scatter_dimension=0, tiled=True).astype(
        jnp.bfloat16
    )
    grad_mixed = jnp.concatenate([grad_q, kv_share], axis=1)
    grad_rows = lax.all_gather(grad_mixed, "wide", axis=0, tiled=True)
    grad_joined = contract_rows(token_panel, grad_rows)
    grad_wq = grad_joined[:, :query_cols].astype(jnp.bfloat16)
    grad_wkv = grad_joined[:, query_cols:].astype(jnp.bfloat16)
    row_block = grad_rows
    grad_tokens = lax.psum_scatter(
        contract_cols(row_block, joined).astype(jnp.bfloat16),
        "narrow",
        scatter_dimension=0,
        tiled=True,
    )
    return (output, grad_tokens, grad_wq, grad_wkv, grad_wo)


def solution(mesh):
    return jax.shard_map(
        shards,
        mesh=mesh,
        in_specs=(
            P("narrow", "wide"),
            P("wide", "narrow"),
            P("wide", "narrow"),
            P("narrow", "wide"),
            P("narrow", "wide"),
        ),
        out_specs=(
            P("narrow", "wide"),
            P("narrow", "wide"),
            P("wide", "narrow"),
            P("wide", "narrow"),
            P("narrow", "wide"),
        ),
        check_vma=False,
    )
```

profile of v0, /device:TPU:0, one launch (start us, length us, event | category | flops | bytes accessed | tf_op | source)
XLA Modules:
  0.0 353.3 jit_solution(4813207071936937951)
XLA Ops:
  7.2 0.0 reduce-scatter.10.cloned.1.call-start
  7.2 7.4 %all_gather.18 = bf16[64,2048]{1,0:T(8,128)(2,1)S(1)} all-gather(bf16[16,2048]{1,0:T(8,128)(2,1)} %param.9), channel_id=1, replica_groups=mesh['narrow'=4,'wide'=8] {'narrow'}, dimensions={0}, use_global_device_ids=true | all-gather | bytes 327680 | tf_op jit(solution)/shard_map/all_gather | solution.py:76
  14.6 6.8 %fusion.16 = f32[64,2048]{1,0:T(8,128)} fusion(bf16[64,2048]{1,0:T(8,128)(2,1)S(1)} %all_gather.18, bf16[2048,2048]{1,0:T(8,128)(2,1)} %param.8), kind=kOutput, calls=%fused_computation.44 | convolution fusion | flops 536870912 | bytes 9175040 | tf_op jit(solution)/shard_map/dot_general | solution.py:16
  21.4 0.0 copy-start.1
  21.4 0.0 copy-start
  21.5 0.0 reduce-scatter.10.cloned.1.call-update
  21.5 0.0 reduce-scatter.6.cloned.1.call-start
  21.5 8.4 %constant_dynamic-update-slice_fusion.1 = bf16[2048,2304]{1,0:T(8,128)(2,1)} fusion(bf16[2048,2048]{1,0:T(8,128)(2,1)} %param.6), kind=kLoop, calls=%fused_computation.39 | loop fusion | bytes 16777216
  30.0 0.0 copy-done.1
  30.0 5.8 %all_gather.15 = bf16[64,2048]{1,0:T(8,128)(2,1)S(1)} all-gather(bf16[16,2048]{1,0:T(8,128)(2,1)S(1)} %copy-done.1), channel_id=1, replica_groups=mesh['narrow'=4,'wide'=8] {'narrow'}, dimensions={0}, use_global_device_ids=true | all-gather | bytes 327680 | tf_op jit(solution)/shard_map/all_gather | solution.py:32
  35.8 0.0 copy-done
  35.8 1.1 constant_dynamic-update-slice_fusion
  36.9 6.3 %convolution_bitcast_fusion = f32[64,2304]{1,0:T(8,128)} fusion(bf16[64,2048]{1,0:T(8,128)(2,1)S(1)} %all_gather.15, bf16[2048,2304]{1,0:T(8,128)(2,1)} %constant_dynamic-update-slice_fusion), kind=kOutput, calls=%fused_computation.3 | convolution fusion | flops 603979776 | bytes 10289152 | tf_op jit(solution)/shard_map/dot_general | solution.py:39
  43.2 0.0 reduce-scatter.6.cloned.1.call-update
  43.2 0.0 reduce-scatter.12.cloned.1.call-start
  43.3 0.1 iota_compare_fusion
  43.3 41.5 %reduce-scatter.10.cloned.1.call-done = f32[8,2048]{1,0:T(8,128)} async-done(((f32[64,2048]{1,0:T(8,128)}), f32[8,2048]{1,0:T(8,128)}) %reduce-scatter.10.cloned.1.call-update) | async-done | bytes 65552 | tf_op jit(solution)/shard_map/reduce_scatter | solution.py:22
  84.9 0.8 convert_bitcast_fusion
  85.7 64.5 %reduce-scatter.6.cloned.1.call-done = f32[8,2304]{1,0:T(8,128)} async-done(((f32[64,2304]{1,0:T(8,128)}), f32[8,2304]{1,0:T(8,128)}) %reduce-scatter.6.cloned.1.call-update) | async-done | bytes 73744 | tf_op jit(solution)/shard_map/reduce_scatter | solution.py:22
  150.2 0.9 convert.8
  151.1 30.4 %all_gather.16 = bf16[64,256]{1,0:T(8,128)(2,1)S(1)} all-gather(bf16[8,256]{1,0:T(8,128)(2,1)S(1)} %slice.28), channel_id=1, replica_groups=mesh['narrow'=4,'wide'=8] {'wide'}, dimensions={0}, use_global_device_ids=true | all-gather | bytes 36864 | tf_op jit(solution)/shard_map/all_gather | solution.py:44
  181.6 0.1 fusion.14
  181.6 0.2 fusion.15
  181.9 0.2 multiply_reduce_fusion
  182.1 0.1 fusion.9
  182.2 0.1 fusion.5
  182.3 0.2 convolution_bitcast_fusion.2
  182.6 30.9 %all_gather.17 = bf16[64,2048]{1,0:T(8,128)(2,1)S(1)} all-gather(bf16[8,2048]{1,0:T(8,128)(2,1)S(1)} %bitcast.101), channel_id=1, replica_groups=mesh['narrow'=4,'wide'=8] {'wide'}, dimensions={0}, use_global_device_ids=true | all-gather | bytes 294912 | tf_op jit(solution)/shard_map/all_gather | solution.py:68
  213.5 0.2 fusion.8
  213.7 0.1 copy.24
  213.7 0.6 copy.61
  214.4 0.0 reduce-scatter.12.cloned.1.call-update
  214.4 0.0 reduce-scatter.8.cloned.1.call-start
  214.4 5.7 %convolution_convert_fusion.3 = bf16[64,2048]{1,0:T(8,128)(2,1)} fusion(bf16[64,2048]{1,0:T(8,128)(2,1)S(1)} %all_gather.17, bf16[2048,2048]{1,0:T(8,128)(2,1)} %param.8), kind=kOutput, calls=%fused_computation.5 | convolution fusion | flops 537001984 | bytes 8912896 | tf_op jit(solution)/shard_map/dot_general | solution.py:71
  220.1 0.1 fusion.6
  220.3 0.0 reduce-scatter.8.cloned.1.call-update
  220.3 0.0 reduce-scatter.14.cloned.1.call-start
  220.3 54.4 %reduce-scatter.12.cloned.1.call-done = f32[8,256]{1,0:T(8,128)} async-done(((f32[64,256]{1,0:T(8,128)}), f32[8,256]{1,0:T(8,128)}) %reduce-scatter.12.cloned.1.call-update) | async-done | bytes 8208 | tf_op jit(solution)/shard_map/reduce_scatter | solution.py:102
  274.8 0.7 convert_element_type.61
  275.5 31.2 %all_gather.19 = bf16[64,2304]{1,0:T(8,128)(2,1)S(1)} all-gather(bf16[8,2304]{1,0:T(8,128)(2,1)S(1)} %pad_maximum_fusion.1), channel_id=1, replica_groups=mesh['narrow'=4,'wide'=8] {'wide'}, dimensions={0}, use_global_device_ids=true | all-gather | bytes 331776 | tf_op jit(solution)/shard_map/all_gather | solution.py:106
  306.6 7.3 %convolution_convert_fusion.2 = bf16[64,2048]{1,0:T(8,128)(2,1)} fusion(bf16[64,2304]{1,0:T(8,128)(2,1)S(1)} %all_gather.19, bf16[2048,2304]{1,0:T(8,128)(2,1)} %constant_dynamic-update-slice_fusion), kind=kOutput, calls=%fused_computation.4 | convolution fusion | flops 604110848 | bytes 9994240 | tf_op jit(solution)/shard_map/dot_general | solution.py:16
  314.0 0.0 reduce-scatter.14.cloned.1.call-update
  314.0 5.8 %convolution_convert_fusion.1 = bf16[2048,2048]{1,0:T(8,128)(2,1)} fusion(bf16[64,2048]{1,0:T(8,128)(2,1)S(1)} %all_gather.17, bf16[64,2048]{1,0:T(8,128)(2,1)S(1)} %all_gather.18), kind=kOutput, calls=%fused_computation.2 | convolution fusion | flops 541065216 | bytes 8912896 | tf_op jit(solution)/shard_map/dot_general | solution.py:10
  319.8 5.0 %fusion = bf16[2048,2304]{0,1:T(8,128)(2,1)} fusion(bf16[64,2304]{1,0:T(8,128)(2,1)S(1)} %all_gather.19, bf16[64,2048]{1,0:T(8,128)(2,1)S(1)} %all_gather.15), kind=kOutput, calls=%fused_computation.1 | convolution fusion | flops 608698368 | bytes 9994240 | tf_op jit(solution)/shard_map/dot_general | solution.py:10
  324.8 8.3 %slice.32 = bf16[2048,2048]{0,1:T(8,128)(2,1)} slice(bf16[2048,2304]{0,1:T(8,128)(2,1)} %fusion), slice={[0:2048], [0:2048]} | slice | bytes 16777216 | tf_op jit(solution)/shard_map/slice | solution.py:108
  333.1 12.3 %copy.25 = bf16[2048,2048]{1,0:T(8,128)(2,1)} copy(bf16[2048,2048]{0,1:T(8,128)(2,1)} %slice.32) | data formatting | bytes 16777216
  345.5 0.0 slice-done
  345.5 1.3 copy.26
  (11 shorter events, 0.1 us)
Async XLA Ops:
  7.2 77.7 %reduce-scatter.10.cloned.1.call-start = ((), (), s32[]{:S(2)}) async-start(), calls=%async_computation.7 | async-start | bytes 589824 | tf_op jit(solution)/shard_map/reduce_scatter | solution.py:22
  21.4 8.5 %copy-start.1 = (bf16[16,2048]{1,0:T(8,128)(2,1)S(1)}, bf16[16,2048]{1,0:T(8,128)(2,1)}, u32[]{:S(2)}) copy-start(bf16[16,2048]{1,0:T(8,128)(2,1)} %param.5) | copy-start | bytes 196612
  21.4 14.4 %copy-start = (bf16[2048,256]{1,0:T(8,128)(2,1)S(1)}, bf16[2048,256]{1,0:T(8,128)(2,1)}, u32[]{:S(2)}) copy-start(bf16[2048,256]{1,0:T(8,128)(2,1)} %param.7) | copy-start | bytes 3145732
  21.5 128.8 %reduce-scatter.6.cloned.1.call-start = ((), (), s32[]{:S(2)}) async-start(), calls=%async_computation.5 | async-start | bytes 663552 | tf_op jit(solution)/shard_map/reduce_scatter | solution.py:22
  43.2 231.6 %reduce-scatter.12.cloned.1.call-start = ((), (), s32[]{:S(2)}) async-start(), calls=%async_computation.8 | async-start | bytes 73728 | tf_op jit(solution)/shard_map/reduce_scatter | solution.py:102
  214.4 132.4 %reduce-scatter.8.cloned.1.call-start = ((), (), s32[]{:S(2)}) async-start(), calls=%async_computation.6 | async-start | bytes 327680 | tf_op jit(solution)/shard_map/reduce_scatter | solution.py:70
  220.3 126.5 %reduce-scatter.14.cloned.1.call-start = ((), (), s32[]{:S(2)}) async-start(), calls=%async_computation.9 | async-start | bytes 327680 | tf_op jit(solution)/shard_map/reduce_scatter | solution.py:111
  333.1 12.3 %slice-start = ((bf16[2048,2304]{0,1:T(8,128)(2,1)}), bf16[2048,256]{0,1:T(8,128)(2,1)S(1)}, s32[]{:S(2)}) async-start(bf16[2048,2304]{0,1:T(8,128)(2,1)} %fusion), calls=%async_computation.10 | async-start | bytes 2097152 | tf_op jit(solution)/shard_map/slice | solution.py:109
Sparse Core Ops, SparseCore 0:
  21.6 63.2 reduce-scatter.9
  89.1 61.1 reduce-scatter.5
  214.5 60.2 reduce-scatter.11
  277.7 19.0 reduce-scatter.7
  314.1 19.0 reduce-scatter.13
where the time goes:
time: 354 us; the launch traced here: 353 us
  waiting for transfers between devices  161 us (45%)
  blocking collectives  106 us (30%)
  matrix products  38 us (11%)
  local copies, waits for them, and re-layouts  32.3 us (9%)
  between operations  13.9 us (4%)
    reduce_scatter x2, waiting for transfers between devices, wide_sum(): lax.psum_scatter(term_fn(jnp.int32(0), lax.axis_size('wide') * (all_rows...  106 us
    reduce_scatter x1, waiting for transfers between devices, shards(): lax.psum_scatter(kv_grad, 'wide', scatter_dimension=0, tiled=True)  54.4 us
    all_gather x1, blocking collectives, shards(): grad_rows = lax.all_gather(grad_mixed, 'wide', axis=0, tiled=True)  31.2 us
    all_gather x1, blocking collectives, shards(): att_panel = lax.all_gather(attended, 'wide', axis=0, tiled=True)  30.9 us
    all_gather x1, blocking collectives, shards(): kv_panel = lax.all_gather(kv_own, 'wide', axis=0, tiled=True)  30.4 us
    unnamed x10, local copies, waits for them, and re-layouts  22.7 us
    dot_general x2, matrix products, contract_cols(): lax.dot_general(left, right, (((1,), (1,)), ((), ())), preferred_element_...  14.2 us
    dot_general x2, matrix products, contract_rows(): lax.dot_general(left, right, (((0,), (0,)), ((), ())), preferred_element_...  10.8 us
  transfers between devices with their start and end apart: 5, of which 3 were waited for; matrix products, arithmetic and copies ran while one was open for 18% of the time, Pallas kernels for 0%

commit v1 on v0

--- a/solution.py
+++ b/solution.py
@@ -1,6 +1,10 @@
+import functools
+
 import jax
 import jax.numpy as jnp
 from jax import lax
+from jax.experimental import pallas as pl
+from jax.experimental.pallas import tpu as pltpu
 from jax.sharding import PartitionSpec as P
 
 HD = 128
@@ -27,7 +31,7 @@
     )
 
 
-def shards(tokens, w_query, w_keyval, w_output, grad_out):
+def row_shards(tokens, w_query, w_keyval, w_output, grad_out):
     wide_index = lax.axis_index("wide")
     token_panel = lax.all_gather(tokens, "narrow", axis=0, tiled=True)
     all_rows = token_panel.shape[0]
@@ -117,9 +121,505 @@
     return (output, grad_tokens, grad_wq, grad_wkv, grad_wo)
 
 
+MIB = 1 << 20
+BF = jnp.bfloat16
+F32 = jnp.float32
+VMEM = pl.BlockSpec(memory_space=pltpu.VMEM)
+ANY = pl.BlockSpec(memory_space=pl.ANY)
+HBM = pl.BlockSpec(memory_space=pltpu.HBM)
+
+
+def swap(value, axis, size, distance):
+    return lax.ppermute(value, axis, [(i, i ^ distance) for i in range(size)])
+
+
+def call(kernel, ins, in_specs, outs, out_specs, scratch, vmem, flops, moved, aliases={}):
+    return pl.pallas_call(
+        kernel,
+        out_shape=outs,
+        in_specs=in_specs,
+        out_specs=out_specs,
+        scratch_shapes=scratch,
+        input_output_aliases=aliases,
+        compiler_params=pltpu.CompilerParams(vmem_limit_bytes=vmem),
+        cost_estimate=pl.CostEstimate(flops=flops, bytes_accessed=moved, transcendentals=0),
+    )(*ins)
+
+
+def block_of(distance, cols):
+    return pl.ds(pl.multiple_of((lax.axis_index("wide") ^ distance) * cols, cols), cols)
+
+
+def load_kernel(source, wq, wo, out, sem):
+    copy = pltpu.make_async_copy(source, out, sem)
+    copy.start()
+    copy.wait()
+
+
+def panels(refs):
+    half = len(refs) // 2
+    return (jnp.concatenate([r[...] for r in part], axis=0) for part in (refs[:half], refs[half:]))
+
+
+def query_block(wq, b, cols):
+    return wq[:, block_of(b, cols)]
+
+
+def output_block(wo, b, cols):
+    return wo[block_of(b, cols), :]
+
+
+def project_blocks(token_panel, grad_panel, blocks, wq, wo, width, out):
+    cols = width // (2 * len(blocks))
+    for at, b in enumerate(blocks):
+        left = 2 * at * cols
+        out[:, left : left + cols] = jnp.dot(token_panel, query_block(wq, b, cols), preferred_element_type=F32).astype(BF)
+        out[:, left + cols : left + 2 * cols] = contract_cols(grad_panel, output_block(wo, b, cols)).astype(BF)
+
+
+def project_far_kernel(blocks, count, *refs):
+    pieces, (wq, wo, wkv, out, kv) = refs[:count], refs[count:]
+    token_panel, grad_panel = panels(pieces)
+    project_blocks(token_panel, grad_panel, blocks, wq, wo, out.shape[1], out)
+    kv[...] = jnp.dot(token_panel, wkv[...], preferred_element_type=F32).astype(BF)
+
+
+def project_kernel(blocks, count, *refs):
+    pieces, (wq, wo, out) = refs[:count], refs[count:]
+    token_panel, grad_panel = panels(pieces)
+    project_blocks(token_panel, grad_panel, blocks, wq, wo, out.shape[1], out)
+
+
+def last_swap_kernel(block, kv, *outs):
+    cols, kv_cols = block.shape[1] // len(outs), kv.shape[1] // len(outs)
+    for at, out in enumerate(outs):
+        out[:, :cols] = block[:, at * cols : (at + 1) * cols]
+        out[:, cols:] = kv[:, at * kv_cols : (at + 1) * kv_cols]
+
+
+def add_kernel(left, right, out):
+    out[...] = plus(left[...], right[...]).astype(BF)
+
+
+def turn_kernel(*refs):
+    refs[-1][...] = jnp.concatenate([r[...] for r in refs[:-1]], axis=0).T
+
+
+def plus(left, right):
+    return left.astype(F32) + right.astype(F32)
+
+
+def total(parts):
+    value = parts[0][...].astype(F32)
+    for part in parts[1:]:
+        value = value + part[...].astype(F32)
+    return value
+
+
+def add_far_kernel(near, far, *outs):
+    width = outs[0].shape[1]
+    for at, out in enumerate(outs):
+        part = slice(at * width, (at + 1) * width)
+        out[...] = plus(near[:, part], far[:, part]).astype(BF)
+
+
+def attend_kernel(narrow, near, kv, far_query, far_grad, *refs):
+    parts, out = refs[:-1], refs[-1]
+    width = parts[0].shape[1]
+    cols, far = width // 2, (far_query, far_grad)
+    block = near[:, near.shape[1] - width :].astype(F32) + jnp.concatenate([r[:, :cols].astype(F32) for r in far], axis=1)
+    block = block + total(parts)
+    pair = kv[...].astype(F32) + jnp.concatenate([r[:, cols:].astype(F32) for r in far], axis=1)
+    value = jnp.concatenate([block, pair], axis=1).astype(BF)
+    rows = value.shape[0]
+    cols = (value.shape[1] - 2 * HD) // 2
+    piece = rows // narrow
+    me = lax.axis_index("narrow")
+
+    def position(dim):
+        at = lax.broadcasted_iota(jnp.int32, (rows, rows), dim)
+        return ((at // piece) ^ me) * piece + at % piece
+
+    allowed = position(1) <= position(0)
+    keys, values = value[:, 2 * cols : 2 * cols + HD], value[:, 2 * cols + HD :]
+    scale = HD ** (-0.5)
+    grad_keys = jnp.zeros((rows, HD), F32)
+    grad_values = jnp.zeros((rows, HD), F32)
+    for at in range(0, cols, HD):
+        queries, grads = value[:, at : at + HD], value[:, cols + at : cols + at + HD]
+        weights = jnp.where(allowed, jnp.exp(contract_cols(queries, keys) * scale), 0.0)
+        weights = weights / jnp.sum(weights, axis=1, keepdims=True)
+        probs = weights.astype(BF)
+        out[:, at : at + HD] = jnp.dot(probs, values, preferred_element_type=F32).astype(BF)
+        prob_grad = contract_cols(grads, values)
+        score_grad = weights * (prob_grad - jnp.sum(weights * prob_grad, axis=1, keepdims=True))
+        score_half = score_grad.astype(BF)
+        out[:, cols + at : cols + at + HD] = (
+            jnp.dot(score_half, keys, preferred_element_type=F32) * scale
+        ).astype(BF)
+        grad_keys = grad_keys + contract_rows(score_half, queries) * scale
+        grad_values = grad_values + contract_rows(probs, grads)
+    out[:, 2 * cols : 2 * cols + HD] = grad_keys.astype(BF)
+    out[:, 2 * cols + HD :] = grad_values.astype(BF)
+
+
+def join_kernel(width, *refs):
+    parts, out = refs[:-1], refs[-1]
+    kv = parts[0][:, width:].astype(F32)
+    for at, part in enumerate(parts):
+        out[:, at * width : (at + 1) * width] = part[:, :width]
+        if at:
+            kv = kv + part[:, width:].astype(F32)
+    out[:, len(parts) * width :] = kv.astype(BF)
+
+
+def accumulate(blocks, cols, parts, wq, wo, before, out_sum, grad_sum):
+    for i, (part, left, b) in enumerate(blocks):
+        out = jnp.dot(parts[part][:, left : left + cols], output_block(wo, b, cols), preferred_element_type=F32)
+        grad = contract_cols(parts[part][:, left + cols : left + 2 * cols], query_block(wq, b, cols))
+        if i == 0 and before:
+            out, grad = out + before[0][...], grad + before[1][...]
+        elif i:
+            out, grad = out + out_sum[...], grad + grad_sum[...]
+        out_sum[...] = out
+        grad_sum[...] = grad
+
+
+def back_kernel(blocks, cols, count, *refs):
+    parts, (wq, wo), rest = refs[:count], refs[count : count + 2], refs[count + 2 :]
+    accumulate(blocks, cols, parts, wq, wo, rest[:-2], *rest[-2:])
+
+
+def kv_total(parts):
+    total = parts[0][:, parts[0].shape[1] - 2 * HD :].astype(F32)
+    for part in parts[1:]:
+        total = total + part[:, part.shape[1] - 2 * HD :].astype(F32)
+    return total.astype(BF)
+
+
+def back_last_kernel(blocks, cols, count, piece, *refs):
+    parts, (wq, wo, wkv, out_before, grad_before, near, far, out_sum, grad_sum) = refs[:count], refs[count:]
+    accumulate(blocks, cols, parts, wq, wo, (out_before, grad_before), out_sum, grad_sum)
+    grad_sum[...] += contract_cols(kv_total(parts), wkv[...])
+    for out, low in ((near, 0), (far, 1)):
+        for at in range(out.shape[0] // (2 * piece)):
+            first = (2 * at + low) * piece
+            out[2 * at * piece : (2 * at + 1) * piece, :] = out_sum[first : first + piece, :].astype(BF)
+            out[(2 * at + 1) * piece : (2 * at + 2) * piece, :] = grad_sum[first : first + piece, :].astype(BF)
+
+
+def send_weight_grads(blocks, cols, turned, grads, parts, gwq, gwo, gwq_v, gwo_v, sems):
+    grad_panel = jnp.concatenate([r[...] for r in grads], axis=0)
+    copies = []
+
+    def send(source, target):
+        copies.append(pltpu.make_async_copy(source, target, sems.at[len(copies)]))
+        copies[-1].start()
+
+    tile = 256
+    for at, (part, left, b) in enumerate(blocks):
+        att = parts[part][:, left : left + cols].T
+        for first in range(0, gwo.shape[1], tile):
+            span = slice(first, first + tile)
+            gwo_v[at, :, span] = jnp.dot(att, grad_panel[:, span], preferred_element_type=F32).astype(BF)
+        send(gwo_v.at[at], gwo.at[block_of(b, cols), :])
+        grad = parts[part][:, left + cols : left + 2 * cols]
+        for first in range(0, gwq.shape[0], tile):
+            span = slice(first, first + tile)
+            gwq_v[at, span, :] = jnp.dot(turned[span, :], grad, preferred_element_type=F32).astype(BF)
+        send(gwq_v.at[at], gwq.at[:, block_of(b, cols)])
+    return copies
+
+
+def block_kernel(blocks, cols, narrow, count, has_before, *refs):
+    turned, grads, parts, refs = refs[0], refs[1 : 1 + narrow], refs[1 + narrow : 1 + narrow + count], refs[1 + narrow + count :]
+    wq, wo = refs[:2]
+    before, outs = (refs[2:4], refs[6:]) if has_before else ((), refs[2:])
+    gwq, gwo, out_sum, grad_sum, gwq_v, gwo_v, sems = outs
+    copies = send_weight_grads(blocks, cols, turned, grads, parts, gwq, gwo, gwq_v, gwo_v, sems)
+    accumulate(blocks, cols, parts, wq, wo, before, out_sum, grad_sum)
+    for copy in copies:
+        copy.wait()
+
+
+def weight_grad_kernel(blocks, cols, narrow, count, *refs):
+    turned, grads, parts = refs[0], refs[1 : 1 + narrow], refs[1 + narrow : 1 + narrow + count]
+    gwq, gwo, gwkv, gwkv_v, gwq_v, gwo_v, sems = refs[3 + narrow + count :]
+    gwkv_v[...] = jnp.dot(turned[...], kv_total(parts), preferred_element_type=F32).astype(BF)
+    last = pltpu.make_async_copy(gwkv_v, gwkv, sems.at[2 * len(blocks)])
+    last.start()
+    copies = send_weight_grads(blocks, cols, turned, grads, parts, gwq, gwo, gwq_v, gwo_v, sems)
+    for copy in copies + [last]:
+        copy.wait()
+
+
+def add_pieces_kernel(near, far, own, *outs):
+    rows = own.shape[0]
+    for at, out in enumerate((own,) + outs):
+        part = slice(at * rows, (at + 1) * rows)
+        out[...] = plus(near[part, :], far[part, :]).astype(BF)
+
+
+def finish_kernel(*refs):
+    parts, output, grad = refs[:-2], refs[-2], refs[-1]
+    value = total(parts)
+    rows = output.shape[0]
+    output[...] = value[:rows].astype(BF)
+    grad[...] = value[rows:].astype(BF)
+
+
+def shards(narrow, wide, tokens, w_query, w_keyval, w_output, grad_out):
+    piece, features = tokens.shape
+    query_cols, pair_cols = w_query.shape[1], w_keyval.shape[1]
+    cols = query_cols // wide
+    if pair_cols != 2 * HD or cols % HD or cols * wide != query_cols or piece % 16 or narrow & (narrow - 1) or wide & (wide - 1) or wide < 8 or narrow < 2:
+        return row_shards(tokens, w_query, w_keyval, w_output, grad_out)
+    rows = narrow * piece
+    weight_size = features * (2 * query_cols + pair_cols)
+    full = jax.ShapeDtypeStruct((rows, 2 * cols + pair_cols), BF)
+    piece_shape = jax.ShapeDtypeStruct((piece, features), BF)
+    half = wide // 2
+    sems = pltpu.SemaphoreType.DMA((4 * wide,))
+
+    def spread(value):
+        pieces = {0: value}
+        bit = narrow // 2
+        while bit > 1:
+            pieces.update({b ^ bit: swap(p, "narrow", narrow, bit) for b, p in pieces.items()})
+            bit //= 2
+        return {b: p for b, p in pieces.items() if b}
+
+    token_pieces, grad_pieces = spread(tokens), spread(grad_out)
+    beside = [{0: v, 1: swap(v, "narrow", narrow, 1)} for v in (tokens, grad_out)]
+    far_blocks = list(range(wide - 1, 0, -2))
+    near_blocks = list(range(wide - 2, -1, -2))
+    wkv = call(
+        load_kernel,
+        [pltpu.with_memory_space_constraint(w, pltpu.HBM) for w in (w_keyval, w_query, w_output)],
+        [HBM] * 3,
+        jax.ShapeDtypeStruct(w_keyval.shape, BF),
+        VMEM,
+        [pltpu.SemaphoreType.DMA],
+        2 * MIB,
+        0,
+        2 * weight_size,
+    )
+    token_pieces, grad_pieces, wkv = lax.optimization_barrier((token_pieces, grad_pieces, wkv))
+    for pieces in (token_pieces, grad_pieces):
+        pieces.update({b ^ 1: swap(p, "narrow", narrow, 1) for b, p in pieces.items() if b})
+    token_pieces, grad_pieces = [[{**own, **p}[b] for b in range(narrow)] for own, p in zip(beside, (token_pieces, grad_pieces))]
+    most = half - 1
+    pieces = (*token_pieces, *grad_pieces)
+    count = 2 * narrow
+    far, kv = call(
+        functools.partial(project_far_kernel, far_blocks[:most], count),
+        (*pieces, w_query, w_output, wkv),
+        [VMEM] * (count + 3),
+        [
+            jax.ShapeDtypeStruct((rows, 2 * cols * most), BF),
+            jax.ShapeDtypeStruct((rows, pair_cols), BF),
+        ],
+        [VMEM] * 2,
+        [],
+        8 * MIB,
+        rows * weight_size,
+        weight_size,
+    )
+    far = swap(far, "wide", wide, 1)
+    def project(blocks):
+        return call(
+            functools.partial(project_kernel, blocks, count),
+            (*pieces, w_query, w_output),
+            [VMEM] * (count + 2),
+            jax.ShapeDtypeStruct((rows, 2 * cols * len(blocks)), BF),
+            VMEM,
+            [],
+            8 * MIB,
+            2 * rows * weight_size * len(blocks) // wide,
+            2 * weight_size * len(blocks) // wide,
+        )
+
+    near = project(near_blocks)
+    bit = 2
+    while bit < wide:
+        other = swap(kv, "wide", wide, bit)
+        if bit == 2:
+            other, near = lax.optimization_barrier((other, near))
+        kv = call(
+            add_kernel,
+            (kv, other),
+            [VMEM] * 2,
+            jax.ShapeDtypeStruct((rows, pair_cols), BF),
+            VMEM,
+            [],
+            2 * MIB,
+            2 * rows * pair_cols,
+            6 * rows * pair_cols,
+        )
+        bit *= 2
+    turned = call(
+        turn_kernel,
+        token_pieces,
+        [VMEM] * narrow,
+        jax.ShapeDtypeStruct((features, rows), BF),
+        VMEM,
+        [],
+        2 * MIB,
+        0,
+        4 * rows * features,
+    )
+    near, turned = lax.optimization_barrier((near, turned))
+    sums = call(
+        add_far_kernel,
+        (near, far),
+        [VMEM] * 2,
+        [jax.ShapeDtypeStruct((rows, 2 * cols), BF)] * most,
+        [VMEM] * most,
+        [],
+        2 * MIB,
+        rows * 2048,
+        rows * 8192,
+    )
+    received = [swap(part, "wide", wide, d) for part, d in zip(sums, near_blocks)][::-1]
+    far_own = call(
+        last_swap_kernel,
+        (project(far_blocks[most:]), kv),
+        [VMEM] * 2,
+        [jax.ShapeDtypeStruct((rows, cols + HD), BF)] * 2,
+        [VMEM] * 2,
+        [],
+        2 * MIB,
+        0,
+        4 * rows * full.shape[1],
+    )
+    far_other = [swap(part, "wide", wide, 1) for part in far_own]
+    own = call(
+        functools.partial(attend_kernel, narrow),
+        (near, kv, *far_other, *received),
+        [VMEM] * (4 + len(received)),
+        full,
+        VMEM,
+        [],
+        4 * MIB,
+        24 * rows * rows * cols,
+        2 * rows * wide * full.shape[1],
+    )
+    width = 2 * cols
+    same = {0: own, **{d: swap(own, "wide", wide, d) for d in near_blocks[:-1]}}
+    width = 2 * cols
+    sum_shapes = [jax.ShapeDtypeStruct((rows, features), F32)] * 2
+    grad_shapes = [jax.ShapeDtypeStruct(w.shape, BF) for w in (w_query, w_output)]
+
+    def grad_scratch(blocks):
+        return [pltpu.VMEM((len(blocks), features, cols), BF), pltpu.VMEM((len(blocks), cols, features), BF), sems]
+
+    def block_terms(distances, before=()):
+        blocks = [(i, 0, d) for i, d in enumerate(distances)]
+        ins = (turned, *grad_pieces, *[same[d] for d in distances], w_query, w_output, *before)
+        return call(
+            functools.partial(block_kernel, blocks, cols, narrow, len(blocks), bool(before)),
+            ins,
+            [VMEM] * (3 + narrow + len(blocks)) + ([VMEM] * 2 + [ANY] * 2 if before else []),
+            grad_shapes + sum_shapes,
+            [ANY] * 2 + [VMEM] * 2,
+            grad_scratch(blocks),
+            20 * MIB,
+            8 * rows * features * cols * len(blocks),
+            8 * features * cols * len(blocks),
+            {len(ins) - 2: 0, len(ins) - 1: 1} if before else {},
+        )
+
+    same = {0: own, **{d: swap(own, "wide", wide, d) for d in near_blocks[:-1]}}
+    first, rest = near_blocks[-2], near_blocks[:-2]
+    groups = ([0, first], rest)
+    joined = []
+    for group in groups:
+        if joined:
+            *grads, out_sum, grad_sum = block_terms([0, first])
+            same[rest[-1]], grads, out_sum, grad_sum = lax.optimization_barrier((same[rest[-1]], grads, out_sum, grad_sum))
+        together = call(
+            functools.partial(join_kernel, width),
+            [same[d] for d in group],
+            [VMEM] * len(group),
+            jax.ShapeDtypeStruct((rows, width * len(group) + pair_cols), BF),
+            VMEM,
+            [],
+            2 * MIB,
+            0,
+            4 * rows * full.shape[1] * len(group),
+        )
+        joined.append(swap(together, "wide", wide, 1))
+    *grads, out_sum, grad_sum = block_terms(rest, (out_sum, grad_sum, *grads))
+    blocks = [[(i, width * at, d + 1) for at, d in enumerate(group)] for i, group in enumerate(groups)]
+    out_sum, grad_sum = call(
+        functools.partial(back_kernel, blocks[0], cols, 1),
+        (joined[0], w_query, w_output, out_sum, grad_sum),
+        [VMEM] * 5,
+        sum_shapes,
+        [VMEM] * 2,
+        [],
+        8 * MIB,
+        4 * rows * features * cols * len(blocks[0]),
+        4 * features * cols * len(blocks[0]),
+    )
+    parts = [*joined, *same.values()]
+    piece_half = jax.ShapeDtypeStruct((narrow * piece, features), BF)
+    piece_pair = jax.ShapeDtypeStruct((2 * piece, features), BF)
+    near, far = call(
+        functools.partial(back_last_kernel, blocks[1], cols, len(parts), piece),
+        (*parts, w_query, w_output, wkv, out_sum, grad_sum),
+        [VMEM] * (len(parts) + 5),
+        [piece_half] * 2,
+        [VMEM] * 2,
+        [pltpu.VMEM((rows, features), F32), pltpu.VMEM((rows, features), F32)],
+        8 * MIB,
+        rows * weight_size,
+        weight_size,
+    )
+    far = swap(far, "narrow", narrow, 1)
+    sums = call(
+        add_pieces_kernel,
+        (near, far),
+        [VMEM] * 2,
+        [piece_pair] * (narrow // 2),
+        [VMEM] * (narrow // 2),
+        [],
+        2 * MIB,
+        2 * rows * features,
+        12 * rows * features,
+    )
+    sums = [sums[0]] + [swap(sums[i], "narrow", narrow, 2 * i) for i in range(1, narrow // 2)]
+    blocks = blocks[0] + blocks[1]
+    ins = (turned, *grad_pieces, *parts, *grads)
+    grad_wq, grad_wo, grad_wkv = call(
+        functools.partial(weight_grad_kernel, blocks, cols, narrow, len(parts)),
+        ins,
+        [VMEM] * (1 + narrow + len(parts)) + [ANY] * 2,
+        grad_shapes + [jax.ShapeDtypeStruct(w_keyval.shape, BF)],
+        [ANY] * 3,
+        [pltpu.VMEM(w_keyval.shape, BF)] + grad_scratch(blocks),
+        20 * MIB,
+        8 * rows * features * cols * len(blocks),
+        8 * features * cols * len(blocks),
+        {len(ins) - 2: 0, len(ins) - 1: 1},
+    )
+    output, grad_tokens = call(
+        finish_kernel,
+        sums,
+        [VMEM] * len(sums),
+        [piece_shape] * 2,
+        [VMEM] * 2,
+        [],
+        4 * MIB,
+        2 * narrow * piece * features,
+        4 * narrow * piece * features,
+    )
+    return (output, grad_tokens, grad_wq, grad_wkv, grad_wo)
+
+
 def solution(mesh):
     return jax.shard_map(
-        shards,
+        functools.partial(shards, mesh.shape["narrow"], mesh.shape["wide"]),
         mesh=mesh,
         in_specs=(
             P("narrow", "wide"),

time: 354 us -> 56.3 us (0.16)
  waiting for transfers between devices: 161 us -> 8.64 us
  blocking collectives: 106 us -> 0 us
  matrix products: 38 us -> 0 us
  local copies, waits for them, and re-layouts: 32.3 us -> 0.02 us
  starting transfers between devices: 0.2 us -> 24 us
  Pallas kernels: 0 us -> 22.6 us
  between operations: 13.9 us -> 0.84 us
    reduce_scatter x5 -> x0, waiting for transfers between devices: 161 us -> none  [the longest x2 106 us: wide_sum(): lax.psum_scatter(term_fn(jnp.int32(0), lax.axis_size('wide') * (all_rows...]
    all_gather x5 -> x0, blocking collectives: 106 us -> none  [the longest x1 31.2 us: shards(): grad_rows = lax.all_gather(grad_mixed, 'wide', axis=0, tiled=True)]
    dot_general x12 -> x0, matrix products: 38 us -> none  [the longest x2 14.2 us: contract_cols(): lax.dot_general(left, right, (((1,), (1,)), ((), ())), preferred_element_...]
    ppermute x0 -> x21, starting transfers between devices: none -> 24 us  [swap(): return lax.ppermute(value, axis, [(i, i ^ distance) for i in range(size)])]
    unnamed x10 -> x8, local copies, waits for them, and re-layouts: 22.7 us -> 0.02 us
    pallas_call x0 -> x19, Pallas kernels: none -> 22.6 us  [call(): pl.pallas_call(kernel, out_shape=outs, in_specs=in_specs, out_specs=out_s...]
    ppermute x0 -> x21, waiting for transfers between devices: none -> 8.64 us  [swap(): return lax.ppermute(value, axis, [(i, i ^ distance) for i in range(size)])]
    slice x5 -> x0, local copies, waits for them, and re-layouts: 8.4 us -> none  [the longest x1 8.34 us: shards(): grad_wq = grad_joined[:, :query_cols].astype(jnp.bfloat16)]
  transfers between devices with their start and end apart: 5 -> 21, of which waited for: 3 -> 10; matrix products, arithmetic and copies ran while one was open for 18% -> 0% of each run, Pallas kernels for 0% -> 31%
where the time goes in v1:
time: 56.3 us; the launch traced here: 56.1 us
  starting transfers between devices  24 us (43%)
  Pallas kernels  22.6 us (40%)
  waiting for transfers between devices  8.64 us (15%)
  between operations  0.84 us (1%)
    ppermute x21, starting transfers between devices, swap(): return lax.ppermute(value, axis, [(i, i ^ distance) for i in range(size)])  24 us
    pallas_call x19, Pallas kernels, call(): pl.pallas_call(kernel, out_shape=outs, in_specs=in_specs, out_specs=out_s...  22.6 us
    ppermute x21, waiting for transfers between devices, swap(): return lax.ppermute(value, axis, [(i, i ^ distance) for i in range(size)])  8.64 us
  transfers between devices with their start and end apart: 21, of which 10 were waited for; matrix products, arithmetic and copies ran while one was open for 0% of the time, Pallas kernels for 31%

profile of v1, /device:TPU:0, one launch (start us, length us, event | category | flops | bytes accessed | tf_op | source)
XLA Modules:
  0.0 56.1 jit_solution(60770293855511393)
XLA Ops:
  0.7 3.0 %collective-permute-start.1 = (bf16[16,2048]{1,0:T(8,128)(2,1)}, bf16[16,2048]{1,0:T(8,128)(2,1)S(1)}, u32[]{:S(2)}, u32[]{:S(2)}) collective-permute-start(bf16[16,2048]{1,0:T(8,128)(2,1)} %refs_0_.7), channel_id=1, source_target_pairs={{0,16},{8,24},{16,0},{24,8},{1,17},{9,25},{17,1},{25,9},{2,18},{10... | collective-permute-start | bytes 196616 | tf_op jit(solution)/shard_map/ppermute | solution.py:133
  3.7 0.1 collective-permute-start.2
  3.8 0.0 collective-permute-start
  3.8 0.5 collective-permute-start.4
  4.3 2.0 %shard_map.92.refs_10_.refs_8_ = bf16[2048,256]{1,0:T(8,128)(2,1)S(1)} custom-call(bf16[2048,256]{1,0:T(8,128)(2,1)} %source.1, bf16[2048,2048]{1,0:T(8,128)(2,1)} %refs_6_.1, bf16[2048,2048]{1,0:T(8,128)(2,1)} %refs_7_.5), custom_call_target="tpu_custom_call" | custom-call | bytes 17825792 | tf_op jit(solution)/shard_map/pallas_call | solution.py:137
  6.3 0.0 collective-permute-done.1.refs_2_
  6.3 1.9 %collective-permute-done.2.refs_6_.refs_3_ = bf16[16,2048]{1,0:T(8,128)(2,1)S(1)} collective-permute-done((bf16[16,2048]{1,0:T(8,128)(2,1)}, bf16[16,2048]{1,0:T(8,128)(2,1)S(1)}, u32[]{:S(2)}, u32[]{:S(2)}) %collective-permute-start.2) | collective-permute-done | bytes 65568 | tf_op jit(solution)/shard_map/ppermute | solution.py:133
  8.2 0.0 collective-permute-start.3
  8.2 0.5 collective-permute-start.5
  8.7 0.0 collective-permute-done.refs_1_
  8.7 0.0 collective-permute-done.4.refs_5_.refs_2_
  8.7 0.7 %collective-permute-done.3.refs_3_ = bf16[16,2048]{1,0:T(8,128)(2,1)S(1)} collective-permute-done((bf16[16,2048]{1,0:T(8,128)(2,1)S(1)}, bf16[16,2048]{1,0:T(8,128)(2,1)S(1)}, u32[]{:S(2)}, u32[]{:S(2)}) %collective-permute-start.3) | collective-permute-done | bytes 65568 | tf_op jit(solution)/shard_map/ppermute | solution.py:133
  9.4 0.2 collective-permute-done.5.refs_7_.refs_4_
  9.6 1.8 %shard_map.93 = (bf16[64,1536]{1,0:T(8,128)(2,1)S(1)}, bf16[64,256]{1,0:T(8,128)(2,1)S(1)}) custom-call(bf16[16,2048]{1,0:T(8,128)(2,1)S(1)} %copy-done.3, bf16[16,2048]{1,0:T(8,128)(2,1)S(1)} %collective-permute-done.refs_1_, bf16[16,2048]{1,0:T(8,128)(2,1)S(1)} %collective-permute-done.1.refs_2_, bf16[16,2048]{1,0:T(8,128)(2,1)S(1)} %collective-permute-done.3.refs_3_, ...), custom_call_target="tpu_custom_call" | custom-call | flops 570425344 | bytes 8912896 | tf_op jit(solution)/shard_map/pallas_call | solution.py:137
  11.4 1.6 %collective-permute-start.10 = (bf16[64,1536]{1,0:T(8,128)(2,1)S(1)}, bf16[64,1536]{1,0:T(8,128)(2,1)S(1)}, u32[]{:S(2)}, u32[]{:S(2)}) collective-permute-start(bf16[64,1536]{1,0:T(8,128)(2,1)S(1)} %get-tuple-element.52), channel_id=1, source_target_pairs={{0,1},{1,0},{2,3},{3,2},{4,5},{5,4},{6,7},{7,6},{8,9},{9,8},{10,11... | collective-permute-start | bytes 589832 | tf_op jit(solution)/shard_map/ppermute | solution.py:133
  13.0 1.6 %collective-permute-start.6 = (bf16[64,256]{1,0:T(8,128)(2,1)S(1)}, bf16[64,256]{1,0:T(8,128)(2,1)S(1)}, u32[]{:S(2)}, u32[]{:S(2)}) collective-permute-start(bf16[64,256]{1,0:T(8,128)(2,1)S(1)} %get-tuple-element.46.left), channel_id=1, source_target_pairs={{0,2},{1,3},{2,0},{3,1},{4,6},{5,7},{6,4},{7,5},{8,10},{9,11},{10,... | collective-permute-start | bytes 98312 | tf_op jit(solution)/shard_map/ppermute | solution.py:133
  14.5 2.1 %shard_map.94.near = bf16[64,2048]{1,0:T(8,128)(2,1)S(1)} custom-call(bf16[16,2048]{1,0:T(8,128)(2,1)S(1)} %copy-done.3, bf16[16,2048]{1,0:T(8,128)(2,1)S(1)} %collective-permute-done.refs_1_, bf16[16,2048]{1,0:T(8,128)(2,1)S(1)} %collective-permute-done.1.refs_2_, bf16[16,2048]{1,0:T(8,128)(2,1)S(1)} %collective-permute-done.3.refs_3_, ...), custom_call_target="tpu_custom_call" | custom-call | flops 570425344 | bytes 8912896 | tf_op jit(solution)/shard_map/pallas_call | solution.py:137
  16.6 0.2 collective-permute-done.6.right
  16.9 2.7 %collective-permute-start.7 = (bf16[64,256]{1,0:T(8,128)(2,1)S(1)}, bf16[64,256]{1,0:T(8,128)(2,1)S(1)}, u32[]{:S(2)}, u32[]{:S(2)}) collective-permute-start(bf16[64,256]{1,0:T(8,128)(2,1)S(1)} %shard_map.96.left), channel_id=1, source_target_pairs={{0,4},{1,5},{2,6},{3,7},{4,0},{5,1},{6,2},{7,3},{8,12},{9,13},{10,... | collective-permute-start | bytes 98312 | tf_op jit(solution)/shard_map/ppermute | solution.py:133
  19.5 0.2 shard_map.95.refs_0_
  19.8 0.1 shard_map.100
  19.8 1.6 %collective-permute-start.11 = (bf16[64,512]{1,0:T(8,128)(2,1)S(1)}, bf16[64,512]{1,0:T(8,128)(2,1)S(1)}, u32[]{:S(2)}, u32[]{:S(2)}) collective-permute-start(bf16[64,512]{1,0:T(8,128)(2,1)S(1)} %get-tuple-element.53), channel_id=1, source_target_pairs={{0,2},{1,3},{2,0},{3,1},{4,6},{5,7},{6,4},{7,5},{8,10},{9,11},{10,... | collective-permute-start | bytes 196616 | tf_op jit(solution)/shard_map/ppermute | solution.py:133
  21.5 1.4 %collective-permute-start.12 = (bf16[64,512]{1,0:T(8,128)(2,1)S(1)}, bf16[64,512]{1,0:T(8,128)(2,1)S(1)}, u32[]{:S(2)}, u32[]{:S(2)}) collective-permute-start(bf16[64,512]{1,0:T(8,128)(2,1)S(1)} %get-tuple-element.54), channel_id=1, source_target_pairs={{0,4},{1,5},{2,6},{3,7},{4,0},{5,1},{6,2},{7,3},{8,12},{9,13},{10,... | collective-permute-start | bytes 196616 | tf_op jit(solution)/shard_map/ppermute | solution.py:133
  22.9 1.4 %collective-permute-start.13 = (bf16[64,512]{1,0:T(8,128)(2,1)S(1)}, bf16[64,512]{1,0:T(8,128)(2,1)S(1)}, u32[]{:S(2)}, u32[]{:S(2)}) collective-permute-start(bf16[64,512]{1,0:T(8,128)(2,1)S(1)} %get-tuple-element.55), channel_id=1, source_target_pairs={{0,6},{1,7},{2,4},{3,5},{4,2},{5,3},{6,0},{7,1},{8,14},{9,15},{10,... | collective-permute-start | bytes 196616 | tf_op jit(solution)/shard_map/ppermute | solution.py:133
  24.3 0.6 %shard_map.98.block = bf16[64,512]{1,0:T(8,128)(2,1)S(1)} custom-call(bf16[16,2048]{1,0:T(8,128)(2,1)S(1)} %copy-done.3, bf16[16,2048]{1,0:T(8,128)(2,1)S(1)} %collective-permute-done.refs_1_, bf16[16,2048]{1,0:T(8,128)(2,1)S(1)} %collective-permute-done.1.refs_2_, bf16[16,2048]{1,0:T(8,128)(2,1)S(1)} %collective-permute-done.3.refs_3_, ...), custom_call_target="tpu_custom_call" | custom-call | flops 142606336 | bytes 2228224 | tf_op jit(solution)/shard_map/pallas_call | solution.py:137
  24.9 0.6 %collective-permute-start.8 = (bf16[64,384]{1,0:T(8,128)(2,1)S(1)}, bf16[64,384]{1,0:T(8,128)(2,1)S(1)}, u32[]{:S(2)}, u32[]{:S(2)}) collective-permute-start(bf16[64,384]{1,0:T(8,128)(2,1)S(1)} %get-tuple-element.50), channel_id=1, source_target_pairs={{0,1},{1,0},{2,3},{3,2},{4,5},{5,4},{6,7},{7,6},{8,9},{9,8},{10,11... | collective-permute-start | bytes 147464 | tf_op jit(solution)/shard_map/ppermute | solution.py:133
  25.5 1.5 %collective-permute-start.9 = (bf16[64,384]{1,0:T(8,128)(2,1)S(1)}, bf16[64,384]{1,0:T(8,128)(2,1)S(1)}, u32[]{:S(2)}, u32[]{:S(2)}) collective-permute-start(bf16[64,384]{1,0:T(8,128)(2,1)S(1)} %get-tuple-element.51), channel_id=1, source_target_pairs={{0,1},{1,0},{2,3},{3,2},{4,5},{5,4},{6,7},{7,6},{8,9},{9,8},{10,11... | collective-permute-start | bytes 147464 | tf_op jit(solution)/shard_map/ppermute | solution.py:133
  27.0 2.1 %collective-permute-done.8.far_query = bf16[64,384]{1,0:T(8,128)(2,1)S(1)} collective-permute-done((bf16[64,384]{1,0:T(8,128)(2,1)S(1)}, bf16[64,384]{1,0:T(8,128)(2,1)S(1)}, u32[]{:S(2)}, u32[]{:S(2)}) %collective-permute-start.8) | collective-permute-done | bytes 49184 | tf_op jit(solution)/shard_map/ppermute | solution.py:133
  29.1 0.5 collective-permute-done.9.far_grad
  29.6 1.1 %shard_map.101.refs_0_.refs_5_.refs_2_.refs_7_ = bf16[64,768]{1,0:T(8,128)(2,1)S(1)} custom-call(bf16[64,2048]{1,0:T(8,128)(2,1)S(1)} %shard_map.94.near, bf16[64,256]{1,0:T(8,128)(2,1)S(1)} %shard_map.97.kv, bf16[64,384]{1,0:T(8,128)(2,1)S(1)} %collective-permute-done.8.far_query, bf16[64,384]{1,0:T(8,128)(2,1)S(1)} %collective-permute-done.9.far_grad, ...), custom_call_target="tpu_custom_call" | custom-call | flops 25165824 | bytes 786432 | tf_op jit(solution)/shard_map/pallas_call | solution.py:137
  30.7 0.7 %collective-permute-start.14 = (bf16[64,768]{1,0:T(8,128)(2,1)S(1)}, bf16[64,768]{1,0:T(8,128)(2,1)S(1)}, u32[]{:S(2)}, u32[]{:S(2)}) collective-permute-start(bf16[64,768]{1,0:T(8,128)(2,1)S(1)} %shard_map.101.refs_0_.refs_5_.refs_2_.refs_7_), channel_id=1, source_target_pairs={{0,2},{1,3},{2,0},{3,1},{4,6},{5,7},{6,4},{7,5},{8,10},{9,11},{10,... | collective-permute-start | bytes 294920 | tf_op jit(solution)/shard_map/ppermute | solution.py:133
  31.5 3.3 %collective-permute-start.17 = (bf16[64,768]{1,0:T(8,128)(2,1)S(1)}, bf16[64,768]{1,0:T(8,128)(2,1)S(1)}, u32[]{:S(2)}, u32[]{:S(2)}) collective-permute-start(bf16[64,768]{1,0:T(8,128)(2,1)S(1)} %shard_map.101.refs_0_.refs_5_.refs_2_.refs_7_), channel_id=1, source_target_pairs={{0,4},{1,5},{2,6},{3,7},{4,0},{5,1},{6,2},{7,3},{8,12},{9,13},{10,... | collective-permute-start | bytes 294920 | tf_op jit(solution)/shard_map/ppermute | solution.py:133
  34.8 0.4 collective-permute-start.16
  35.2 0.4 collective-permute-done.14.refs_1_.refs_6_.refs_5_.refs_10_
  35.6 1.4 %collective-permute-start.15 = (bf16[64,1280]{1,0:T(8,128)(2,1)S(1)}, bf16[64,1280]{1,0:T(8,128)(2,1)S(1)}, u32[]{:S(2)}, u32[]{:S(2)}) collective-permute-start(bf16[64,1280]{1,0:T(8,128)(2,1)S(1)} %shard_map.102), channel_id=1, source_target_pairs={{0,1},{1,0},{2,3},{3,2},{4,5},{5,4},{6,7},{7,6},{8,9},{9,8},{10,11... | collective-permute-start | bytes 491528 | tf_op jit(solution)/shard_map/ppermute | solution.py:133
  37.0 3.6 %shard_map.103 = (bf16[2048,2048]{1,0:T(8,128)(2,1)}, bf16[2048,2048]{1,0:T(8,128)(2,1)}, f32[64,2048]{1,0:T(8,128)S(1)}, f32[64,2048]{1,0:T(8,128)S(1)}) custom-call(bf16[2048,64]{1,0:T(8,128)(2,1)S(1)} %shard_map.95.refs_0_, bf16[16,2048]{1,0:T(8,128)(2,1)S(1)} %copy-done.2, bf16[16,2048]{1,0:T(8,128)(2,1)S(1)} %collective-permute-done.4.refs_5_.refs_2_, ...), custom_call_target="tpu_custom_call" | custom-call | flops 536870912 | bytes 8388608 | tf_op jit(solution)/shard_map/pallas_call | solution.py:137
  40.6 0.7 %collective-permute-done.16.refs_0_.refs_5_.refs_3_.refs_8_ = bf16[64,768]{1,0:T(8,128)(2,1)S(1)} collective-permute-done((bf16[64,768]{1,0:T(8,128)(2,1)S(1)}, bf16[64,768]{1,0:T(8,128)(2,1)S(1)}, u32[]{:S(2)}, u32[]{:S(2)}) %collective-permute-start.16) | collective-permute-done | bytes 98336 | tf_op jit(solution)/shard_map/ppermute | solution.py:133
  41.3 0.6 %collective-permute-start.18 = (bf16[64,1280]{1,0:T(8,128)(2,1)S(1)}, bf16[64,1280]{1,0:T(8,128)(2,1)S(1)}, u32[]{:S(2)}, u32[]{:S(2)}) collective-permute-start(bf16[64,1280]{1,0:T(8,128)(2,1)S(1)} %shard_map.104), channel_id=1, source_target_pairs={{0,1},{1,0},{2,3},{3,2},{4,5},{5,4},{6,7},{7,6},{8,9},{9,8},{10,11... | collective-permute-start | bytes 491528 | tf_op jit(solution)/shard_map/ppermute | solution.py:133
  41.9 3.2 %shard_map.105 = (bf16[2048,2048]{1,0:T(8,128)(2,1)}, bf16[2048,2048]{1,0:T(8,128)(2,1)}, f32[64,2048]{1,0:T(8,128)S(1)}, f32[64,2048]{1,0:T(8,128)S(1)}) custom-call(bf16[2048,64]{1,0:T(8,128)(2,1)S(1)} %shard_map.95.refs_0_, bf16[16,2048]{1,0:T(8,128)(2,1)S(1)} %copy-done.2, ...), custom_call_target="tpu_custom_call", output_to_operand_aliasing={{0}: (11, {}), {1}: (12, {})} | custom-call | flops 536870912 | bytes 8388608 | tf_op jit(solution)/shard_map/pallas_call | solution.py:137
  45.2 1.1 %shard_map.106 = (f32[64,2048]{1,0:T(8,128)S(1)}, f32[64,2048]{1,0:T(8,128)S(1)}) custom-call(bf16[64,1280]{1,0:T(8,128)(2,1)S(1)} %collective-permute-done.15.refs_0_.refs_5_, bf16[2048,2048]{1,0:T(8,128)(2,1)S(1)} %copy-done, bf16[2048,2048]{1,0:T(8,128)(2,1)S(1)} %copy-done.1, f32[64,2048]{1,0:T(8,128)S(1)} %get-tuple-element.66.refs_3_, ...), custom_call_target="tpu_custom_call" | custom-call | flops 268435456 | bytes 4194304 | tf_op jit(solution)/shard_map/pallas_call | solution.py:137
  46.3 0.4 collective-permute-done.18.refs_1_.refs_6_
  46.7 1.4 %shard_map.107 = (bf16[64,2048]{1,0:T(8,128)(2,1)S(1)}, bf16[64,2048]{1,0:T(8,128)(2,1)S(1)}) custom-call(bf16[64,1280]{1,0:T(8,128)(2,1)S(1)} %collective-permute-done.15.refs_0_.refs_5_, bf16[64,1280]{1,0:T(8,128)(2,1)S(1)} %collective-permute-done.18.refs_1_.refs_6_, bf16[64,768]{1,0:T(8,128)(2,1)S(1)} %shard_map.101.refs_0_.refs_5_.refs_2_.refs_7_, ...), custom_call_target="tpu_custom_call" | custom-call | flops 570425344 | bytes 8912896 | tf_op jit(solution)/shard_map/pallas_call | solution.py:137
  48.2 0.1 collective-permute-start.19
  48.2 1.5 %collective-permute-done.19.far = bf16[64,2048]{1,0:T(8,128)(2,1)S(1)} collective-permute-done((bf16[64,2048]{1,0:T(8,128)(2,1)S(1)}, bf16[64,2048]{1,0:T(8,128)(2,1)S(1)}, u32[]{:S(2)}, u32[]{:S(2)}) %collective-permute-start.19) | collective-permute-done | bytes 262176 | tf_op jit(solution)/shard_map/ppermute | solution.py:133
  49.8 0.1 shard_map.108
  49.8 1.0 %collective-permute-start.20 = (bf16[32,2048]{1,0:T(8,128)(2,1)S(1)}, bf16[32,2048]{1,0:T(8,128)(2,1)S(1)}, u32[]{:S(2)}, u32[]{:S(2)}) collective-permute-start(bf16[32,2048]{1,0:T(8,128)(2,1)S(1)} %get-tuple-element.73), channel_id=1, source_target_pairs={{0,16},{8,24},{16,0},{24,8},{1,17},{9,25},{17,1},{25,9},{2,18},{10... | collective-permute-start | bytes 393224 | tf_op jit(solution)/shard_map/ppermute | solution.py:133
  50.9 4.6 %shard_map.110 = (bf16[2048,2048]{1,0:T(8,128)(2,1)}, bf16[2048,2048]{1,0:T(8,128)(2,1)}, bf16[2048,256]{1,0:T(8,128)(2,1)}) custom-call(bf16[2048,64]{1,0:T(8,128)(2,1)S(1)} %shard_map.95.refs_0_, bf16[16,2048]{1,0:T(8,128)(2,1)S(1)} %copy-done.2, ...), custom_call_target="tpu_custom_call", output_to_operand_aliasing={{0}: (11, {}), {1}: (12, {})} | custom-call | flops 1073741824 | bytes 16777216 | tf_op jit(solution)/shard_map/pallas_call | solution.py:137
  55.5 0.7 %shard_map.109 = (bf16[16,2048]{1,0:T(8,128)(2,1)}, bf16[16,2048]{1,0:T(8,128)(2,1)}) custom-call(bf16[32,2048]{1,0:T(8,128)(2,1)S(1)} %get-tuple-element.72.refs_0_, bf16[32,2048]{1,0:T(8,128)(2,1)S(1)} %collective-permute-done.20.refs_1_), custom_call_target="tpu_custom_call" | custom-call | flops 262144 | bytes 524288 | tf_op jit(solution)/shard_map/pallas_call | solution.py:137
  (21 shorter events, 0.1 us)
Async XLA Ops:
  0.6 8.9 %copy-start.3 = (bf16[16,2048]{1,0:T(8,128)(2,1)S(1)}, bf16[16,2048]{1,0:T(8,128)(2,1)}, u32[]{:S(2)}) copy-start(bf16[16,2048]{1,0:T(8,128)(2,1)} %refs_0_.7) | copy-start | bytes 196612
  0.6 8.9 %copy-start.2 = (bf16[16,2048]{1,0:T(8,128)(2,1)S(1)}, bf16[16,2048]{1,0:T(8,128)(2,1)}, u32[]{:S(2)}) copy-start(bf16[16,2048]{1,0:T(8,128)(2,1)} %refs_1_.7) | copy-start | bytes 196612
  0.7 8.9 %copy-start.1 = (bf16[2048,2048]{1,0:T(8,128)(2,1)S(1)}, bf16[2048,2048]{1,0:T(8,128)(2,1)}, u32[]{:S(2)}) copy-start(bf16[2048,2048]{1,0:T(8,128)(2,1)} %refs_7_.5) | copy-start | bytes 25165828
  0.7 8.9 %copy-start = (bf16[2048,2048]{1,0:T(8,128)(2,1)S(1)}, bf16[2048,2048]{1,0:T(8,128)(2,1)}, u32[]{:S(2)}) copy-start(bf16[2048,2048]{1,0:T(8,128)(2,1)} %refs_6_.1) | copy-start | bytes 25165828
  0.7 5.6 %collective-permute-start.1 = (bf16[16,2048]{1,0:T(8,128)(2,1)}, bf16[16,2048]{1,0:T(8,128)(2,1)S(1)}, u32[]{:S(2)}, u32[]{:S(2)}) collective-permute-start(bf16[16,2048]{1,0:T(8,128)(2,1)} %refs_0_.7), channel_id=1, source_target_pairs={{0,16},{8,24},{16,0},{24,8},{1,17},{9,25},{17,1},{25,9},{2,18},{10... | collective-permute-start | bytes 196616 | tf_op jit(solution)/shard_map/ppermute | solution.py:133
  3.7 4.5 %collective-permute-start.2 = (bf16[16,2048]{1,0:T(8,128)(2,1)}, bf16[16,2048]{1,0:T(8,128)(2,1)S(1)}, u32[]{:S(2)}, u32[]{:S(2)}) collective-permute-start(bf16[16,2048]{1,0:T(8,128)(2,1)} %refs_1_.7), channel_id=1, source_target_pairs={{0,16},{8,24},{16,0},{24,8},{1,17},{9,25},{17,1},{25,9},{2,18},{10... | collective-permute-start | bytes 196616 | tf_op jit(solution)/shard_map/ppermute | solution.py:133
  3.8 4.9 %collective-permute-start = (bf16[16,2048]{1,0:T(8,128)(2,1)}, bf16[16,2048]{1,0:T(8,128)(2,1)S(1)}, u32[]{:S(2)}, u32[]{:S(2)}) collective-permute-start(bf16[16,2048]{1,0:T(8,128)(2,1)} %refs_0_.7), channel_id=1, source_target_pairs={{0,8},{8,0},{16,24},{24,16},{1,9},{9,1},{17,25},{25,17},{2,10},{10... | collective-permute-start | bytes 196616 | tf_op jit(solution)/shard_map/ppermute | solution.py:133
  3.8 4.9 %collective-permute-start.4 = (bf16[16,2048]{1,0:T(8,128)(2,1)}, bf16[16,2048]{1,0:T(8,128)(2,1)S(1)}, u32[]{:S(2)}, u32[]{:S(2)}) collective-permute-start(bf16[16,2048]{1,0:T(8,128)(2,1)} %refs_1_.7), channel_id=1, source_target_pairs={{0,8},{8,0},{16,24},{24,16},{1,9},{9,1},{17,25},{25,17},{2,10},{10... | collective-permute-start | bytes 196616 | tf_op jit(solution)/shard_map/ppermute | solution.py:133
  8.2 1.3 %collective-permute-start.3 = (bf16[16,2048]{1,0:T(8,128)(2,1)S(1)}, bf16[16,2048]{1,0:T(8,128)(2,1)S(1)}, u32[]{:S(2)}, u32[]{:S(2)}) collective-permute-start(bf16[16,2048]{1,0:T(8,128)(2,1)S(1)} %collective-permute-done.1.refs_2_), channel_id=1, source_target_pairs={{0,8},{8,0},{16,24},{24,16},{1,9},{9,1},{17,25},{25,17},{2,10},{10... | collective-permute-start | bytes 196616 | tf_op jit(solution)/shard_map/ppermute | solution.py:133
  8.2 1.4 %collective-permute-start.5 = (bf16[16,2048]{1,0:T(8,128)(2,1)S(1)}, bf16[16,2048]{1,0:T(8,128)(2,1)S(1)}, u32[]{:S(2)}, u32[]{:S(2)}) collective-permute-start(bf16[16,2048]{1,0:T(8,128)(2,1)S(1)} %collective-permute-done.2.refs_6_.refs_3_), channel_id=1, source_target_pairs={{0,8},{8,0},{16,24},{24,16},{1,9},{9,1},{17,25},{25,17},{2,10},{10... | collective-permute-start | bytes 196616 | tf_op jit(solution)/shard_map/ppermute | solution.py:133
  11.4 8.4 %collective-permute-start.10 = (bf16[64,1536]{1,0:T(8,128)(2,1)S(1)}, bf16[64,1536]{1,0:T(8,128)(2,1)S(1)}, u32[]{:S(2)}, u32[]{:S(2)}) collective-permute-start(bf16[64,1536]{1,0:T(8,128)(2,1)S(1)} %get-tuple-element.52), channel_id=1, source_target_pairs={{0,1},{1,0},{2,3},{3,2},{4,5},{5,4},{6,7},{7,6},{8,9},{9,8},{10,11... | collective-permute-start | bytes 589832 | tf_op jit(solution)/shard_map/ppermute | solution.py:133
  13.0 3.9 %collective-permute-start.6 = (bf16[64,256]{1,0:T(8,128)(2,1)S(1)}, bf16[64,256]{1,0:T(8,128)(2,1)S(1)}, u32[]{:S(2)}, u32[]{:S(2)}) collective-permute-start(bf16[64,256]{1,0:T(8,128)(2,1)S(1)} %get-tuple-element.46.left), channel_id=1, source_target_pairs={{0,2},{1,3},{2,0},{3,1},{4,6},{5,7},{6,4},{7,5},{8,10},{9,11},{10,... | collective-permute-start | bytes 98312 | tf_op jit(solution)/shard_map/ppermute | solution.py:133
  16.9 8.0 %collective-permute-start.7 = (bf16[64,256]{1,0:T(8,128)(2,1)S(1)}, bf16[64,256]{1,0:T(8,128)(2,1)S(1)}, u32[]{:S(2)}, u32[]{:S(2)}) collective-permute-start(bf16[64,256]{1,0:T(8,128)(2,1)S(1)} %shard_map.96.left), channel_id=1, source_target_pairs={{0,4},{1,5},{2,6},{3,7},{4,0},{5,1},{6,2},{7,3},{8,12},{9,13},{10,... | collective-permute-start | bytes 98312 | tf_op jit(solution)/shard_map/ppermute | solution.py:133
  19.8 9.8 %collective-permute-start.11 = (bf16[64,512]{1,0:T(8,128)(2,1)S(1)}, bf16[64,512]{1,0:T(8,128)(2,1)S(1)}, u32[]{:S(2)}, u32[]{:S(2)}) collective-permute-start(bf16[64,512]{1,0:T(8,128)(2,1)S(1)} %get-tuple-element.53), channel_id=1, source_target_pairs={{0,2},{1,3},{2,0},{3,1},{4,6},{5,7},{6,4},{7,5},{8,10},{9,11},{10,... | collective-permute-start | bytes 196616 | tf_op jit(solution)/shard_map/ppermute | solution.py:133
  21.5 8.2 %collective-permute-start.12 = (bf16[64,512]{1,0:T(8,128)(2,1)S(1)}, bf16[64,512]{1,0:T(8,128)(2,1)S(1)}, u32[]{:S(2)}, u32[]{:S(2)}) collective-permute-start(bf16[64,512]{1,0:T(8,128)(2,1)S(1)} %get-tuple-element.54), channel_id=1, source_target_pairs={{0,4},{1,5},{2,6},{3,7},{4,0},{5,1},{6,2},{7,3},{8,12},{9,13},{10,... | collective-permute-start | bytes 196616 | tf_op jit(solution)/shard_map/ppermute | solution.py:133
  22.9 6.7 %collective-permute-start.13 = (bf16[64,512]{1,0:T(8,128)(2,1)S(1)}, bf16[64,512]{1,0:T(8,128)(2,1)S(1)}, u32[]{:S(2)}, u32[]{:S(2)}) collective-permute-start(bf16[64,512]{1,0:T(8,128)(2,1)S(1)} %get-tuple-element.55), channel_id=1, source_target_pairs={{0,6},{1,7},{2,4},{3,5},{4,2},{5,3},{6,0},{7,1},{8,14},{9,15},{10,... | collective-permute-start | bytes 196616 | tf_op jit(solution)/shard_map/ppermute | solution.py:133
  24.9 4.2 %collective-permute-start.8 = (bf16[64,384]{1,0:T(8,128)(2,1)S(1)}, bf16[64,384]{1,0:T(8,128)(2,1)S(1)}, u32[]{:S(2)}, u32[]{:S(2)}) collective-permute-start(bf16[64,384]{1,0:T(8,128)(2,1)S(1)} %get-tuple-element.50), channel_id=1, source_target_pairs={{0,1},{1,0},{2,3},{3,2},{4,5},{5,4},{6,7},{7,6},{8,9},{9,8},{10,11... | collective-permute-start | bytes 147464 | tf_op jit(solution)/shard_map/ppermute | solution.py:133
  25.5 4.1 %collective-permute-start.9 = (bf16[64,384]{1,0:T(8,128)(2,1)S(1)}, bf16[64,384]{1,0:T(8,128)(2,1)S(1)}, u32[]{:S(2)}, u32[]{:S(2)}) collective-permute-start(bf16[64,384]{1,0:T(8,128)(2,1)S(1)} %get-tuple-element.51), channel_id=1, source_target_pairs={{0,1},{1,0},{2,3},{3,2},{4,5},{5,4},{6,7},{7,6},{8,9},{9,8},{10,11... | collective-permute-start | bytes 147464 | tf_op jit(solution)/shard_map/ppermute | solution.py:133
  30.7 4.9 %collective-permute-start.14 = (bf16[64,768]{1,0:T(8,128)(2,1)S(1)}, bf16[64,768]{1,0:T(8,128)(2,1)S(1)}, u32[]{:S(2)}, u32[]{:S(2)}) collective-permute-start(bf16[64,768]{1,0:T(8,128)(2,1)S(1)} %shard_map.101.refs_0_.refs_5_.refs_2_.refs_7_), channel_id=1, source_target_pairs={{0,2},{1,3},{2,0},{3,1},{4,6},{5,7},{6,4},{7,5},{8,10},{9,11},{10,... | collective-permute-start | bytes 294920 | tf_op jit(solution)/shard_map/ppermute | solution.py:133
  31.5 9.2 %collective-permute-start.17 = (bf16[64,768]{1,0:T(8,128)(2,1)S(1)}, bf16[64,768]{1,0:T(8,128)(2,1)S(1)}, u32[]{:S(2)}, u32[]{:S(2)}) collective-permute-start(bf16[64,768]{1,0:T(8,128)(2,1)S(1)} %shard_map.101.refs_0_.refs_5_.refs_2_.refs_7_), channel_id=1, source_target_pairs={{0,4},{1,5},{2,6},{3,7},{4,0},{5,1},{6,2},{7,3},{8,12},{9,13},{10,... | collective-permute-start | bytes 294920 | tf_op jit(solution)/shard_map/ppermute | solution.py:133
  34.8 6.5 %collective-permute-start.16 = (bf16[64,768]{1,0:T(8,128)(2,1)S(1)}, bf16[64,768]{1,0:T(8,128)(2,1)S(1)}, u32[]{:S(2)}, u32[]{:S(2)}) collective-permute-start(bf16[64,768]{1,0:T(8,128)(2,1)S(1)} %shard_map.101.refs_0_.refs_5_.refs_2_.refs_7_), channel_id=1, source_target_pairs={{0,6},{1,7},{2,4},{3,5},{4,2},{5,3},{6,0},{7,1},{8,14},{9,15},{10,... | collective-permute-start | bytes 294920 | tf_op jit(solution)/shard_map/ppermute | solution.py:133
  35.6 9.6 %collective-permute-start.15 = (bf16[64,1280]{1,0:T(8,128)(2,1)S(1)}, bf16[64,1280]{1,0:T(8,128)(2,1)S(1)}, u32[]{:S(2)}, u32[]{:S(2)}) collective-permute-start(bf16[64,1280]{1,0:T(8,128)(2,1)S(1)} %shard_map.102), channel_id=1, source_target_pairs={{0,1},{1,0},{2,3},{3,2},{4,5},{5,4},{6,7},{7,6},{8,9},{9,8},{10,11... | collective-permute-start | bytes 491528 | tf_op jit(solution)/shard_map/ppermute | solution.py:133
  41.3 5.4 %collective-permute-start.18 = (bf16[64,1280]{1,0:T(8,128)(2,1)S(1)}, bf16[64,1280]{1,0:T(8,128)(2,1)S(1)}, u32[]{:S(2)}, u32[]{:S(2)}) collective-permute-start(bf16[64,1280]{1,0:T(8,128)(2,1)S(1)} %shard_map.104), channel_id=1, source_target_pairs={{0,1},{1,0},{2,3},{3,2},{4,5},{5,4},{6,7},{7,6},{8,9},{9,8},{10,11... | collective-permute-start | bytes 491528 | tf_op jit(solution)/shard_map/ppermute | solution.py:133
  48.2 1.6 %collective-permute-start.19 = (bf16[64,2048]{1,0:T(8,128)(2,1)S(1)}, bf16[64,2048]{1,0:T(8,128)(2,1)S(1)}, u32[]{:S(2)}, u32[]{:S(2)}) collective-permute-start(bf16[64,2048]{1,0:T(8,128)(2,1)S(1)} %get-tuple-element.71), channel_id=1, source_target_pairs={{0,8},{8,0},{16,24},{24,16},{1,9},{9,1},{17,25},{25,17},{2,10},{10... | collective-permute-start | bytes 786440 | tf_op jit(solution)/shard_map/ppermute | solution.py:133
  49.8 5.6 %collective-permute-start.20 = (bf16[32,2048]{1,0:T(8,128)(2,1)S(1)}, bf16[32,2048]{1,0:T(8,128)(2,1)S(1)}, u32[]{:S(2)}, u32[]{:S(2)}) collective-permute-start(bf16[32,2048]{1,0:T(8,128)(2,1)S(1)} %get-tuple-element.73), channel_id=1, source_target_pairs={{0,16},{8,24},{16,0},{24,8},{1,17},{9,25},{17,1},{25,9},{2,18},{10... | collective-permute-start | bytes 393224 | tf_op jit(solution)/shard_map/ppermute | solution.py:133

commit v2 on v1

--- a/solution.py
+++ b/solution.py
@@ -227,7 +227,7 @@
     parts, out = refs[:-1], refs[-1]
     width = parts[0].shape[1]
     cols, far = width // 2, (far_query, far_grad)
-    block = near[:, near.shape[1] - width :].astype(F32) + jnp.concatenate([r[:, :cols].astype(F32) for r in far], axis=1)
+    block = near[...].astype(F32) + jnp.concatenate([r[:, :cols].astype(F32) for r in far], axis=1)
     block = block + total(parts)
     pair = kv[...].astype(F32) + jnp.concatenate([r[:, cols:].astype(F32) for r in far], axis=1)
     value = jnp.concatenate([block, pair], axis=1).astype(BF)
@@ -426,7 +426,7 @@
         weight_size,
     )
     far = swap(far, "wide", wide, 1)
-    def project(blocks):
+    def project(blocks, pieces=pieces):
         return call(
             functools.partial(project_kernel, blocks, count),
             (*pieces, w_query, w_output),
@@ -439,12 +439,12 @@
             2 * weight_size * len(blocks) // wide,
         )
 
-    near = project(near_blocks)
+    near = project(near_blocks[:-1])
     bit = 2
     while bit < wide:
         other = swap(kv, "wide", wide, bit)
         if bit == 2:
-            other, near = lax.optimization_barrier((other, near))
+            other, _ = lax.optimization_barrier((other, near))
         kv = call(
             add_kernel,
             (kv, other),
@@ -457,9 +457,23 @@
             6 * rows * pair_cols,
         )
         bit *= 2
+    sums = call(
+        add_far_kernel,
+        (near, far),
+        [VMEM] * 2,
+        [jax.ShapeDtypeStruct((rows, 2 * cols), BF)] * most,
+        [VMEM] * most,
+        [],
+        2 * MIB,
+        rows * 2048,
+        rows * 8192,
+    )
+    received = [swap(part, "wide", wide, d) for part, d in zip(sums, near_blocks)]
+    later, _ = lax.optimization_barrier((pieces, sums[-1]))
+    near_last = project(near_blocks[-1:], later)
     turned = call(
         turn_kernel,
-        token_pieces,
+        later[:narrow],
         [VMEM] * narrow,
         jax.ShapeDtypeStruct((features, rows), BF),
         VMEM,
@@ -468,19 +482,7 @@
         0,
         4 * rows * features,
     )
-    near, turned = lax.optimization_barrier((near, turned))
-    sums = call(
-        add_far_kernel,
-        (near, far),
-        [VMEM] * 2,
-        [jax.ShapeDtypeStruct((rows, 2 * cols), BF)] * most,
-        [VMEM] * most,
-        [],
-        2 * MIB,
-        rows * 2048,
-        rows * 8192,
-    )
-    received = [swap(part, "wide", wide, d) for part, d in zip(sums, near_blocks)][::-1]
+    near_last, turned = lax.optimization_barrier((near_last, turned))
     far_own = call(
         last_swap_kernel,
         (project(far_blocks[most:]), kv),
@@ -495,7 +497,7 @@
     far_other = [swap(part, "wide", wide, 1) for part in far_own]
     own = call(
         functools.partial(attend_kernel, narrow),
-        (near, kv, *far_other, *received),
+        (near_last, kv, *far_other, *received),
         [VMEM] * (4 + len(received)),
         full,
         VMEM,

time: 56.3 us -> 56.3 us (level)
    pallas_call x19 -> x20, Pallas kernels: 22.6 us -> 22.8 us  [call(): pl.pallas_call(kernel, out_shape=outs, in_specs=in_specs, out_specs=out_s...]
  transfers between devices with their start and end apart: 21 -> 21, of which waited for: 10 -> 10; matrix products, arithmetic and copies ran while one was open for 0% -> 0% of each run, Pallas kernels for 31% -> 32%
where the time goes in v2:
time: 56.3 us; the launch traced here: 56.1 us
  starting transfers between devices  24.2 us (43%)
  Pallas kernels  22.8 us (40%)
  waiting for transfers between devices  8.27 us (15%)
  between operations  0.83 us (1%)
    ppermute x21, starting transfers between devices, swap(): return lax.ppermute(value, axis, [(i, i ^ distance) for i in range(size)])  24.2 us
    pallas_call x20, Pallas kernels, call(): pl.pallas_call(kernel, out_shape=outs, in_specs=in_specs, out_specs=out_s...  22.8 us
    ppermute x21, waiting for transfers between devices, swap(): return lax.ppermute(value, axis, [(i, i ^ distance) for i in range(size)])  8.27 us
  transfers between devices with their start and end apart: 21, of which 10 were waited for; matrix products, arithmetic and copies ran while one was open for 0% of the time, Pallas kernels for 32%

profile of v2, /device:TPU:0, one launch (start us, length us, event | category | flops | bytes accessed | tf_op | source)
XLA Modules:
  0.0 56.1 jit_solution(2950138627356842845)
XLA Ops:
  0.7 3.0 %collective-permute-start.1 = (bf16[16,2048]{1,0:T(8,128)(2,1)}, bf16[16,2048]{1,0:T(8,128)(2,1)S(1)}, u32[]{:S(2)}, u32[]{:S(2)}) collective-permute-start(bf16[16,2048]{1,0:T(8,128)(2,1)} %refs_0_.7), channel_id=1, source_target_pairs={{0,16},{8,24},{16,0},{24,8},{1,17},{9,25},{17,1},{25,9},{2,18},{10... | collective-permute-start | bytes 196616 | tf_op jit(solution)/shard_map/ppermute | solution.py:133
  3.7 0.1 collective-permute-start.2
  3.8 0.5 collective-permute-start.4
  4.3 2.0 %shard_map.92.refs_10_.refs_8_ = bf16[2048,256]{1,0:T(8,128)(2,1)S(1)} custom-call(bf16[2048,256]{1,0:T(8,128)(2,1)} %source.1, bf16[2048,2048]{1,0:T(8,128)(2,1)} %refs_6_.1, bf16[2048,2048]{1,0:T(8,128)(2,1)} %refs_7_.5), custom_call_target="tpu_custom_call" | custom-call | bytes 17825792 | tf_op jit(solution)/shard_map/pallas_call | solution.py:137
  6.3 0.0 collective-permute-done.1.refs_2_
  6.3 1.9 %collective-permute-done.2.refs_6_.refs_3_ = bf16[16,2048]{1,0:T(8,128)(2,1)S(1)} collective-permute-done((bf16[16,2048]{1,0:T(8,128)(2,1)}, bf16[16,2048]{1,0:T(8,128)(2,1)S(1)}, u32[]{:S(2)}, u32[]{:S(2)}) %collective-permute-start.2) | collective-permute-done | bytes 65568 | tf_op jit(solution)/shard_map/ppermute | solution.py:133
  8.2 0.5 collective-permute-start.5
  8.7 0.0 collective-permute-done.refs_1_
  8.7 0.0 collective-permute-done.4.refs_5_.refs_2_
  8.7 0.7 %collective-permute-done.3.refs_3_ = bf16[16,2048]{1,0:T(8,128)(2,1)S(1)} collective-permute-done((bf16[16,2048]{1,0:T(8,128)(2,1)S(1)}, bf16[16,2048]{1,0:T(8,128)(2,1)S(1)}, u32[]{:S(2)}, u32[]{:S(2)}) %collective-permute-start.3) | collective-permute-done | bytes 65568 | tf_op jit(solution)/shard_map/ppermute | solution.py:133
  9.4 0.2 collective-permute-done.5.refs_7_.refs_4_
  9.6 1.8 %shard_map.94 = (bf16[64,1536]{1,0:T(8,128)(2,1)S(1)}, bf16[64,256]{1,0:T(8,128)(2,1)S(1)}) custom-call(bf16[16,2048]{1,0:T(8,128)(2,1)S(1)} %copy-done.3, bf16[16,2048]{1,0:T(8,128)(2,1)S(1)} %collective-permute-done.refs_1_, bf16[16,2048]{1,0:T(8,128)(2,1)S(1)} %collective-permute-done.1.refs_2_, bf16[16,2048]{1,0:T(8,128)(2,1)S(1)} %collective-permute-done.3.refs_3_, ...), custom_call_target="tpu_custom_call" | custom-call | flops 570425344 | bytes 8912896 | tf_op jit(solution)/shard_map/pallas_call | solution.py:137
  11.4 1.6 %collective-permute-start.6 = (bf16[64,1536]{1,0:T(8,128)(2,1)S(1)}, bf16[64,1536]{1,0:T(8,128)(2,1)S(1)}, u32[]{:S(2)}, u32[]{:S(2)}) collective-permute-start(bf16[64,1536]{1,0:T(8,128)(2,1)S(1)} %get-tuple-element.53), channel_id=1, source_target_pairs={{0,1},{1,0},{2,3},{3,2},{4,5},{5,4},{6,7},{7,6},{8,9},{9,8},{10,11... | collective-permute-start | bytes 589832 | tf_op jit(solution)/shard_map/ppermute | solution.py:133
  13.0 1.6 %collective-permute-start.7 = (bf16[64,256]{1,0:T(8,128)(2,1)S(1)}, bf16[64,256]{1,0:T(8,128)(2,1)S(1)}, u32[]{:S(2)}, u32[]{:S(2)}) collective-permute-start(bf16[64,256]{1,0:T(8,128)(2,1)S(1)} %get-tuple-element.64.left), channel_id=1, source_target_pairs={{0,2},{1,3},{2,0},{3,1},{4,6},{5,7},{6,4},{7,5},{8,10},{9,11},{10,... | collective-permute-start | bytes 98312 | tf_op jit(solution)/shard_map/ppermute | solution.py:133
  14.5 1.6 %shard_map.93.near = bf16[64,1536]{1,0:T(8,128)(2,1)S(1)} custom-call(bf16[16,2048]{1,0:T(8,128)(2,1)S(1)} %copy-done.3, bf16[16,2048]{1,0:T(8,128)(2,1)S(1)} %collective-permute-done.refs_1_, bf16[16,2048]{1,0:T(8,128)(2,1)S(1)} %collective-permute-done.1.refs_2_, bf16[16,2048]{1,0:T(8,128)(2,1)S(1)} %collective-permute-done.3.refs_3_, ...), custom_call_target="tpu_custom_call" | custom-call | flops 427819008 | bytes 6684672 | tf_op jit(solution)/shard_map/pallas_call | solution.py:137
  16.2 0.7 %collective-permute-done.7.right = bf16[64,256]{1,0:T(8,128)(2,1)S(1)} collective-permute-done((bf16[64,256]{1,0:T(8,128)(2,1)S(1)}, bf16[64,256]{1,0:T(8,128)(2,1)S(1)}, u32[]{:S(2)}, u32[]{:S(2)}) %collective-permute-start.7) | collective-permute-done | bytes 32800 | tf_op jit(solution)/shard_map/ppermute | solution.py:133
  16.9 2.7 %collective-permute-start.8 = (bf16[64,256]{1,0:T(8,128)(2,1)S(1)}, bf16[64,256]{1,0:T(8,128)(2,1)S(1)}, u32[]{:S(2)}, u32[]{:S(2)}) collective-permute-start(bf16[64,256]{1,0:T(8,128)(2,1)S(1)} %shard_map.98.left), channel_id=1, source_target_pairs={{0,4},{1,5},{2,6},{3,7},{4,0},{5,1},{6,2},{7,3},{8,12},{9,13},{10,... | collective-permute-start | bytes 98312 | tf_op jit(solution)/shard_map/ppermute | solution.py:133
  19.5 0.0 collective-permute-done.6.far
  19.6 2.7 %collective-permute-start.11 = (bf16[64,512]{1,0:T(8,128)(2,1)S(1)}, bf16[64,512]{1,0:T(8,128)(2,1)S(1)}, u32[]{:S(2)}, u32[]{:S(2)}) collective-permute-start(bf16[64,512]{1,0:T(8,128)(2,1)S(1)} %get-tuple-element.68), channel_id=1, source_target_pairs={{0,6},{1,7},{2,4},{3,5},{4,2},{5,3},{6,0},{7,1},{8,14},{9,15},{10,... | collective-permute-start | bytes 196616 | tf_op jit(solution)/shard_map/ppermute | solution.py:133
  22.3 0.4 collective-permute-start.12
  22.7 1.4 %collective-permute-start.13 = (bf16[64,512]{1,0:T(8,128)(2,1)S(1)}, bf16[64,512]{1,0:T(8,128)(2,1)S(1)}, u32[]{:S(2)}, u32[]{:S(2)}) collective-permute-start(bf16[64,512]{1,0:T(8,128)(2,1)S(1)} %get-tuple-element.54), channel_id=1, source_target_pairs={{0,2},{1,3},{2,0},{3,1},{4,6},{5,7},{6,4},{7,5},{8,10},{9,11},{10,... | collective-permute-start | bytes 196616 | tf_op jit(solution)/shard_map/ppermute | solution.py:133
  24.1 0.6 %shard_map.100.block = bf16[64,512]{1,0:T(8,128)(2,1)S(1)} custom-call(bf16[16,2048]{1,0:T(8,128)(2,1)S(1)} %copy-done.3, bf16[16,2048]{1,0:T(8,128)(2,1)S(1)} %collective-permute-done.refs_1_, bf16[16,2048]{1,0:T(8,128)(2,1)S(1)} %collective-permute-done.1.refs_2_, bf16[16,2048]{1,0:T(8,128)(2,1)S(1)} %collective-permute-done.3.refs_3_, ...), custom_call_target="tpu_custom_call" | custom-call | flops 142606336 | bytes 2228224 | tf_op jit(solution)/shard_map/pallas_call | solution.py:137
  24.7 0.6 %collective-permute-start.9 = (bf16[64,384]{1,0:T(8,128)(2,1)S(1)}, bf16[64,384]{1,0:T(8,128)(2,1)S(1)}, u32[]{:S(2)}, u32[]{:S(2)}) collective-permute-start(bf16[64,384]{1,0:T(8,128)(2,1)S(1)} %get-tuple-element.66), channel_id=1, source_target_pairs={{0,1},{1,0},{2,3},{3,2},{4,5},{5,4},{6,7},{7,6},{8,9},{9,8},{10,11... | collective-permute-start | bytes 147464 | tf_op jit(solution)/shard_map/ppermute | solution.py:133
  25.3 1.5 %collective-permute-start.10 = (bf16[64,384]{1,0:T(8,128)(2,1)S(1)}, bf16[64,384]{1,0:T(8,128)(2,1)S(1)}, u32[]{:S(2)}, u32[]{:S(2)}) collective-permute-start(bf16[64,384]{1,0:T(8,128)(2,1)S(1)} %get-tuple-element.67), channel_id=1, source_target_pairs={{0,1},{1,0},{2,3},{3,2},{4,5},{5,4},{6,7},{7,6},{8,9},{9,8},{10,11... | collective-permute-start | bytes 147464 | tf_op jit(solution)/shard_map/ppermute | solution.py:133
  26.8 0.2 shard_map.97.refs_0_
  27.0 0.6 %shard_map.96.near = bf16[64,512]{1,0:T(8,128)(2,1)S(1)} custom-call(bf16[16,2048]{1,0:T(8,128)(2,1)S(1)} %copy-done.3, bf16[16,2048]{1,0:T(8,128)(2,1)S(1)} %collective-permute-done.refs_1_, bf16[16,2048]{1,0:T(8,128)(2,1)S(1)} %collective-permute-done.1.refs_2_, bf16[16,2048]{1,0:T(8,128)(2,1)S(1)} %collective-permute-done.3.refs_3_, ...), custom_call_target="tpu_custom_call" | custom-call | flops 142606336 | bytes 2228224 | tf_op jit(solution)/shard_map/pallas_call | solution.py:137
  27.6 1.2 %collective-permute-done.9.far_query = bf16[64,384]{1,0:T(8,128)(2,1)S(1)} collective-permute-done((bf16[64,384]{1,0:T(8,128)(2,1)S(1)}, bf16[64,384]{1,0:T(8,128)(2,1)S(1)}, u32[]{:S(2)}, u32[]{:S(2)}) %collective-permute-start.9) | collective-permute-done | bytes 49184 | tf_op jit(solution)/shard_map/ppermute | solution.py:133
  28.9 0.6 collective-permute-done.10.far_grad
  29.4 0.0 collective-permute-done.12.refs_1_
  29.5 1.1 %shard_map.102.refs_0_.refs_5_.refs_2_.refs_7_ = bf16[64,768]{1,0:T(8,128)(2,1)S(1)} custom-call(bf16[64,512]{1,0:T(8,128)(2,1)S(1)} %shard_map.96.near, bf16[64,256]{1,0:T(8,128)(2,1)S(1)} %shard_map.99.kv, bf16[64,384]{1,0:T(8,128)(2,1)S(1)} %collective-permute-done.9.far_query, bf16[64,384]{1,0:T(8,128)(2,1)S(1)} %collective-permute-done.10.far_grad, ...), custom_call_target="tpu_custom_call" | custom-call | flops 25165824 | bytes 786432 | tf_op jit(solution)/shard_map/pallas_call | solution.py:137
  30.5 1.3 %collective-permute-start.14 = (bf16[64,768]{1,0:T(8,128)(2,1)S(1)}, bf16[64,768]{1,0:T(8,128)(2,1)S(1)}, u32[]{:S(2)}, u32[]{:S(2)}) collective-permute-start(bf16[64,768]{1,0:T(8,128)(2,1)S(1)} %shard_map.102.refs_0_.refs_5_.refs_2_.refs_7_), channel_id=1, source_target_pairs={{0,2},{1,3},{2,0},{3,1},{4,6},{5,7},{6,4},{7,5},{8,10},{9,11},{10,... | collective-permute-start | bytes 294920 | tf_op jit(solution)/shard_map/ppermute | solution.py:133
  31.9 2.9 %collective-permute-start.17 = (bf16[64,768]{1,0:T(8,128)(2,1)S(1)}, bf16[64,768]{1,0:T(8,128)(2,1)S(1)}, u32[]{:S(2)}, u32[]{:S(2)}) collective-permute-start(bf16[64,768]{1,0:T(8,128)(2,1)S(1)} %shard_map.102.refs_0_.refs_5_.refs_2_.refs_7_), channel_id=1, source_target_pairs={{0,4},{1,5},{2,6},{3,7},{4,0},{5,1},{6,2},{7,3},{8,12},{9,13},{10,... | collective-permute-start | bytes 294920 | tf_op jit(solution)/shard_map/ppermute | solution.py:133
  34.8 0.2 collective-permute-start.16
  35.0 0.3 collective-permute-done.14.refs_1_.refs_6_.refs_5_.refs_10_
  35.3 1.6 %collective-permute-start.15 = (bf16[64,1280]{1,0:T(8,128)(2,1)S(1)}, bf16[64,1280]{1,0:T(8,128)(2,1)S(1)}, u32[]{:S(2)}, u32[]{:S(2)}) collective-permute-start(bf16[64,1280]{1,0:T(8,128)(2,1)S(1)} %shard_map.103), channel_id=1, source_target_pairs={{0,1},{1,0},{2,3},{3,2},{4,5},{5,4},{6,7},{7,6},{8,9},{9,8},{10,11... | collective-permute-start | bytes 491528 | tf_op jit(solution)/shard_map/ppermute | solution.py:133
  37.0 3.6 %shard_map.104 = (bf16[2048,2048]{1,0:T(8,128)(2,1)}, bf16[2048,2048]{1,0:T(8,128)(2,1)}, f32[64,2048]{1,0:T(8,128)S(1)}, f32[64,2048]{1,0:T(8,128)S(1)}) custom-call(bf16[2048,64]{1,0:T(8,128)(2,1)S(1)} %shard_map.97.refs_0_, bf16[16,2048]{1,0:T(8,128)(2,1)S(1)} %copy-done.2, bf16[16,2048]{1,0:T(8,128)(2,1)S(1)} %collective-permute-done.4.refs_5_.refs_2_, ...), custom_call_target="tpu_custom_call" | custom-call | flops 536870912 | bytes 8388608 | tf_op jit(solution)/shard_map/pallas_call | solution.py:137
  40.6 0.7 %collective-permute-done.16.refs_0_.refs_5_.refs_3_.refs_8_ = bf16[64,768]{1,0:T(8,128)(2,1)S(1)} collective-permute-done((bf16[64,768]{1,0:T(8,128)(2,1)S(1)}, bf16[64,768]{1,0:T(8,128)(2,1)S(1)}, u32[]{:S(2)}, u32[]{:S(2)}) %collective-permute-start.16) | collective-permute-done | bytes 98336 | tf_op jit(solution)/shard_map/ppermute | solution.py:133
  41.3 0.6 %collective-permute-start.18 = (bf16[64,1280]{1,0:T(8,128)(2,1)S(1)}, bf16[64,1280]{1,0:T(8,128)(2,1)S(1)}, u32[]{:S(2)}, u32[]{:S(2)}) collective-permute-start(bf16[64,1280]{1,0:T(8,128)(2,1)S(1)} %shard_map.105), channel_id=1, source_target_pairs={{0,1},{1,0},{2,3},{3,2},{4,5},{5,4},{6,7},{7,6},{8,9},{9,8},{10,11... | collective-permute-start | bytes 491528 | tf_op jit(solution)/shard_map/ppermute | solution.py:133
  41.9 3.2 %shard_map.106 = (bf16[2048,2048]{1,0:T(8,128)(2,1)}, bf16[2048,2048]{1,0:T(8,128)(2,1)}, f32[64,2048]{1,0:T(8,128)S(1)}, f32[64,2048]{1,0:T(8,128)S(1)}) custom-call(bf16[2048,64]{1,0:T(8,128)(2,1)S(1)} %shard_map.97.refs_0_, bf16[16,2048]{1,0:T(8,128)(2,1)S(1)} %copy-done.2, ...), custom_call_target="tpu_custom_call", output_to_operand_aliasing={{0}: (11, {}), {1}: (12, {})} | custom-call | flops 536870912 | bytes 8388608 | tf_op jit(solution)/shard_map/pallas_call | solution.py:137
  45.2 1.1 %shard_map.107 = (f32[64,2048]{1,0:T(8,128)S(1)}, f32[64,2048]{1,0:T(8,128)S(1)}) custom-call(bf16[64,1280]{1,0:T(8,128)(2,1)S(1)} %collective-permute-done.15.refs_0_.refs_5_, bf16[2048,2048]{1,0:T(8,128)(2,1)S(1)} %copy-done, bf16[2048,2048]{1,0:T(8,128)(2,1)S(1)} %copy-done.1, f32[64,2048]{1,0:T(8,128)S(1)} %get-tuple-element.80.refs_3_, ...), custom_call_target="tpu_custom_call" | custom-call | flops 268435456 | bytes 4194304 | tf_op jit(solution)/shard_map/pallas_call | solution.py:137
  46.3 0.4 collective-permute-done.18.refs_1_.refs_6_
  46.7 1.4 %shard_map.108 = (bf16[64,2048]{1,0:T(8,128)(2,1)S(1)}, bf16[64,2048]{1,0:T(8,128)(2,1)S(1)}) custom-call(bf16[64,1280]{1,0:T(8,128)(2,1)S(1)} %collective-permute-done.15.refs_0_.refs_5_, bf16[64,1280]{1,0:T(8,128)(2,1)S(1)} %collective-permute-done.18.refs_1_.refs_6_, bf16[64,768]{1,0:T(8,128)(2,1)S(1)} %shard_map.102.refs_0_.refs_5_.refs_2_.refs_7_, ...), custom_call_target="tpu_custom_call" | custom-call | flops 570425344 | bytes 8912896 | tf_op jit(solution)/shard_map/pallas_call | solution.py:137
  48.2 0.1 collective-permute-start.19
  48.2 1.5 %collective-permute-done.19.far = bf16[64,2048]{1,0:T(8,128)(2,1)S(1)} collective-permute-done((bf16[64,2048]{1,0:T(8,128)(2,1)S(1)}, bf16[64,2048]{1,0:T(8,128)(2,1)S(1)}, u32[]{:S(2)}, u32[]{:S(2)}) %collective-permute-start.19) | collective-permute-done | bytes 262176 | tf_op jit(solution)/shard_map/ppermute | solution.py:133
  49.8 0.1 shard_map.109
  49.8 1.0 %collective-permute-start.20 = (bf16[32,2048]{1,0:T(8,128)(2,1)S(1)}, bf16[32,2048]{1,0:T(8,128)(2,1)S(1)}, u32[]{:S(2)}, u32[]{:S(2)}) collective-permute-start(bf16[32,2048]{1,0:T(8,128)(2,1)S(1)} %get-tuple-element.87), channel_id=1, source_target_pairs={{0,16},{8,24},{16,0},{24,8},{1,17},{9,25},{17,1},{25,9},{2,18},{10... | collective-permute-start | bytes 393224 | tf_op jit(solution)/shard_map/ppermute | solution.py:133
  50.9 4.6 %shard_map.111 = (bf16[2048,2048]{1,0:T(8,128)(2,1)}, bf16[2048,2048]{1,0:T(8,128)(2,1)}, bf16[2048,256]{1,0:T(8,128)(2,1)}) custom-call(bf16[2048,64]{1,0:T(8,128)(2,1)S(1)} %shard_map.97.refs_0_, bf16[16,2048]{1,0:T(8,128)(2,1)S(1)} %copy-done.2, ...), custom_call_target="tpu_custom_call", output_to_operand_aliasing={{0}: (11, {}), {1}: (12, {})} | custom-call | flops 1073741824 | bytes 16777216 | tf_op jit(solution)/shard_map/pallas_call | solution.py:137
  55.5 0.7 %shard_map.110 = (bf16[16,2048]{1,0:T(8,128)(2,1)}, bf16[16,2048]{1,0:T(8,128)(2,1)}) custom-call(bf16[32,2048]{1,0:T(8,128)(2,1)S(1)} %get-tuple-element.86.refs_0_, bf16[32,2048]{1,0:T(8,128)(2,1)S(1)} %collective-permute-done.20.refs_1_), custom_call_target="tpu_custom_call" | custom-call | flops 262144 | bytes 524288 | tf_op jit(solution)/shard_map/pallas_call | solution.py:137
  (22 shorter events, 0.2 us)
Async XLA Ops:
  0.6 8.9 %copy-start.3 = (bf16[16,2048]{1,0:T(8,128)(2,1)S(1)}, bf16[16,2048]{1,0:T(8,128)(2,1)}, u32[]{:S(2)}) copy-start(bf16[16,2048]{1,0:T(8,128)(2,1)} %refs_0_.7) | copy-start | bytes 196612
  0.6 8.9 %copy-start.2 = (bf16[16,2048]{1,0:T(8,128)(2,1)S(1)}, bf16[16,2048]{1,0:T(8,128)(2,1)}, u32[]{:S(2)}) copy-start(bf16[16,2048]{1,0:T(8,128)(2,1)} %refs_1_.7) | copy-start | bytes 196612
  0.7 8.9 %copy-start.1 = (bf16[2048,2048]{1,0:T(8,128)(2,1)S(1)}, bf16[2048,2048]{1,0:T(8,128)(2,1)}, u32[]{:S(2)}) copy-start(bf16[2048,2048]{1,0:T(8,128)(2,1)} %refs_7_.5) | copy-start | bytes 25165828
  0.7 8.9 %copy-start = (bf16[2048,2048]{1,0:T(8,128)(2,1)S(1)}, bf16[2048,2048]{1,0:T(8,128)(2,1)}, u32[]{:S(2)}) copy-start(bf16[2048,2048]{1,0:T(8,128)(2,1)} %refs_6_.1) | copy-start | bytes 25165828
  0.7 5.6 %collective-permute-start.1 = (bf16[16,2048]{1,0:T(8,128)(2,1)}, bf16[16,2048]{1,0:T(8,128)(2,1)S(1)}, u32[]{:S(2)}, u32[]{:S(2)}) collective-permute-start(bf16[16,2048]{1,0:T(8,128)(2,1)} %refs_0_.7), channel_id=1, source_target_pairs={{0,16},{8,24},{16,0},{24,8},{1,17},{9,25},{17,1},{25,9},{2,18},{10... | collective-permute-start | bytes 196616 | tf_op jit(solution)/shard_map/ppermute | solution.py:133
  3.7 4.5 %collective-permute-start.2 = (bf16[16,2048]{1,0:T(8,128)(2,1)}, bf16[16,2048]{1,0:T(8,128)(2,1)S(1)}, u32[]{:S(2)}, u32[]{:S(2)}) collective-permute-start(bf16[16,2048]{1,0:T(8,128)(2,1)} %refs_1_.7), channel_id=1, source_target_pairs={{0,16},{8,24},{16,0},{24,8},{1,17},{9,25},{17,1},{25,9},{2,18},{10... | collective-permute-start | bytes 196616 | tf_op jit(solution)/shard_map/ppermute | solution.py:133
  3.8 4.9 %collective-permute-start = (bf16[16,2048]{1,0:T(8,128)(2,1)}, bf16[16,2048]{1,0:T(8,128)(2,1)S(1)}, u32[]{:S(2)}, u32[]{:S(2)}) collective-permute-start(bf16[16,2048]{1,0:T(8,128)(2,1)} %refs_0_.7), channel_id=1, source_target_pairs={{0,8},{8,0},{16,24},{24,16},{1,9},{9,1},{17,25},{25,17},{2,10},{10... | collective-permute-start | bytes 196616 | tf_op jit(solution)/shard_map/ppermute | solution.py:133
  3.8 4.9 %collective-permute-start.4 = (bf16[16,2048]{1,0:T(8,128)(2,1)}, bf16[16,2048]{1,0:T(8,128)(2,1)S(1)}, u32[]{:S(2)}, u32[]{:S(2)}) collective-permute-start(bf16[16,2048]{1,0:T(8,128)(2,1)} %refs_1_.7), channel_id=1, source_target_pairs={{0,8},{8,0},{16,24},{24,16},{1,9},{9,1},{17,25},{25,17},{2,10},{10... | collective-permute-start | bytes 196616 | tf_op jit(solution)/shard_map/ppermute | solution.py:133
  8.2 1.3 %collective-permute-start.3 = (bf16[16,2048]{1,0:T(8,128)(2,1)S(1)}, bf16[16,2048]{1,0:T(8,128)(2,1)S(1)}, u32[]{:S(2)}, u32[]{:S(2)}) collective-permute-start(bf16[16,2048]{1,0:T(8,128)(2,1)S(1)} %collective-permute-done.1.refs_2_), channel_id=1, source_target_pairs={{0,8},{8,0},{16,24},{24,16},{1,9},{9,1},{17,25},{25,17},{2,10},{10... | collective-permute-start | bytes 196616 | tf_op jit(solution)/shard_map/ppermute | solution.py:133
  8.2 1.4 %collective-permute-start.5 = (bf16[16,2048]{1,0:T(8,128)(2,1)S(1)}, bf16[16,2048]{1,0:T(8,128)(2,1)S(1)}, u32[]{:S(2)}, u32[]{:S(2)}) collective-permute-start(bf16[16,2048]{1,0:T(8,128)(2,1)S(1)} %collective-permute-done.2.refs_6_.refs_3_), channel_id=1, source_target_pairs={{0,8},{8,0},{16,24},{24,16},{1,9},{9,1},{17,25},{25,17},{2,10},{10... | collective-permute-start | bytes 196616 | tf_op jit(solution)/shard_map/ppermute | solution.py:133
  11.4 8.2 %collective-permute-start.6 = (bf16[64,1536]{1,0:T(8,128)(2,1)S(1)}, bf16[64,1536]{1,0:T(8,128)(2,1)S(1)}, u32[]{:S(2)}, u32[]{:S(2)}) collective-permute-start(bf16[64,1536]{1,0:T(8,128)(2,1)S(1)} %get-tuple-element.53), channel_id=1, source_target_pairs={{0,1},{1,0},{2,3},{3,2},{4,5},{5,4},{6,7},{7,6},{8,9},{9,8},{10,11... | collective-permute-start | bytes 589832 | tf_op jit(solution)/shard_map/ppermute | solution.py:133
  13.0 3.9 %collective-permute-start.7 = (bf16[64,256]{1,0:T(8,128)(2,1)S(1)}, bf16[64,256]{1,0:T(8,128)(2,1)S(1)}, u32[]{:S(2)}, u32[]{:S(2)}) collective-permute-start(bf16[64,256]{1,0:T(8,128)(2,1)S(1)} %get-tuple-element.64.left), channel_id=1, source_target_pairs={{0,2},{1,3},{2,0},{3,1},{4,6},{5,7},{6,4},{7,5},{8,10},{9,11},{10,... | collective-permute-start | bytes 98312 | tf_op jit(solution)/shard_map/ppermute | solution.py:133
  16.9 7.8 %collective-permute-start.8 = (bf16[64,256]{1,0:T(8,128)(2,1)S(1)}, bf16[64,256]{1,0:T(8,128)(2,1)S(1)}, u32[]{:S(2)}, u32[]{:S(2)}) collective-permute-start(bf16[64,256]{1,0:T(8,128)(2,1)S(1)} %shard_map.98.left), channel_id=1, source_target_pairs={{0,4},{1,5},{2,6},{3,7},{4,0},{5,1},{6,2},{7,3},{8,12},{9,13},{10,... | collective-permute-start | bytes 98312 | tf_op jit(solution)/shard_map/ppermute | solution.py:133
  19.6 9.8 %collective-permute-start.11 = (bf16[64,512]{1,0:T(8,128)(2,1)S(1)}, bf16[64,512]{1,0:T(8,128)(2,1)S(1)}, u32[]{:S(2)}, u32[]{:S(2)}) collective-permute-start(bf16[64,512]{1,0:T(8,128)(2,1)S(1)} %get-tuple-element.68), channel_id=1, source_target_pairs={{0,6},{1,7},{2,4},{3,5},{4,2},{5,3},{6,0},{7,1},{8,14},{9,15},{10,... | collective-permute-start | bytes 196616 | tf_op jit(solution)/shard_map/ppermute | solution.py:133
  22.3 7.1 %collective-permute-start.12 = (bf16[64,512]{1,0:T(8,128)(2,1)S(1)}, bf16[64,512]{1,0:T(8,128)(2,1)S(1)}, u32[]{:S(2)}, u32[]{:S(2)}) collective-permute-start(bf16[64,512]{1,0:T(8,128)(2,1)S(1)} %get-tuple-element.69), channel_id=1, source_target_pairs={{0,4},{1,5},{2,6},{3,7},{4,0},{5,1},{6,2},{7,3},{8,12},{9,13},{10,... | collective-permute-start | bytes 196616 | tf_op jit(solution)/shard_map/ppermute | solution.py:133
  22.7 6.7 %collective-permute-start.13 = (bf16[64,512]{1,0:T(8,128)(2,1)S(1)}, bf16[64,512]{1,0:T(8,128)(2,1)S(1)}, u32[]{:S(2)}, u32[]{:S(2)}) collective-permute-start(bf16[64,512]{1,0:T(8,128)(2,1)S(1)} %get-tuple-element.54), channel_id=1, source_target_pairs={{0,2},{1,3},{2,0},{3,1},{4,6},{5,7},{6,4},{7,5},{8,10},{9,11},{10,... | collective-permute-start | bytes 196616 | tf_op jit(solution)/shard_map/ppermute | solution.py:133
  24.7 4.2 %collective-permute-start.9 = (bf16[64,384]{1,0:T(8,128)(2,1)S(1)}, bf16[64,384]{1,0:T(8,128)(2,1)S(1)}, u32[]{:S(2)}, u32[]{:S(2)}) collective-permute-start(bf16[64,384]{1,0:T(8,128)(2,1)S(1)} %get-tuple-element.66), channel_id=1, source_target_pairs={{0,1},{1,0},{2,3},{3,2},{4,5},{5,4},{6,7},{7,6},{8,9},{9,8},{10,11... | collective-permute-start | bytes 147464 | tf_op jit(solution)/shard_map/ppermute | solution.py:133
  25.3 4.1 %collective-permute-start.10 = (bf16[64,384]{1,0:T(8,128)(2,1)S(1)}, bf16[64,384]{1,0:T(8,128)(2,1)S(1)}, u32[]{:S(2)}, u32[]{:S(2)}) collective-permute-start(bf16[64,384]{1,0:T(8,128)(2,1)S(1)} %get-tuple-element.67), channel_id=1, source_target_pairs={{0,1},{1,0},{2,3},{3,2},{4,5},{5,4},{6,7},{7,6},{8,9},{9,8},{10,11... | collective-permute-start | bytes 147464 | tf_op jit(solution)/shard_map/ppermute | solution.py:133
  30.5 4.8 %collective-permute-start.14 = (bf16[64,768]{1,0:T(8,128)(2,1)S(1)}, bf16[64,768]{1,0:T(8,128)(2,1)S(1)}, u32[]{:S(2)}, u32[]{:S(2)}) collective-permute-start(bf16[64,768]{1,0:T(8,128)(2,1)S(1)} %shard_map.102.refs_0_.refs_5_.refs_2_.refs_7_), channel_id=1, source_target_pairs={{0,2},{1,3},{2,0},{3,1},{4,6},{5,7},{6,4},{7,5},{8,10},{9,11},{10,... | collective-permute-start | bytes 294920 | tf_op jit(solution)/shard_map/ppermute | solution.py:133
  31.9 8.7 %collective-permute-start.17 = (bf16[64,768]{1,0:T(8,128)(2,1)S(1)}, bf16[64,768]{1,0:T(8,128)(2,1)S(1)}, u32[]{:S(2)}, u32[]{:S(2)}) collective-permute-start(bf16[64,768]{1,0:T(8,128)(2,1)S(1)} %shard_map.102.refs_0_.refs_5_.refs_2_.refs_7_), channel_id=1, source_target_pairs={{0,4},{1,5},{2,6},{3,7},{4,0},{5,1},{6,2},{7,3},{8,12},{9,13},{10,... | collective-permute-start | bytes 294920 | tf_op jit(solution)/shard_map/ppermute | solution.py:133
  34.8 6.5 %collective-permute-start.16 = (bf16[64,768]{1,0:T(8,128)(2,1)S(1)}, bf16[64,768]{1,0:T(8,128)(2,1)S(1)}, u32[]{:S(2)}, u32[]{:S(2)}) collective-permute-start(bf16[64,768]{1,0:T(8,128)(2,1)S(1)} %shard_map.102.refs_0_.refs_5_.refs_2_.refs_7_), channel_id=1, source_target_pairs={{0,6},{1,7},{2,4},{3,5},{4,2},{5,3},{6,0},{7,1},{8,14},{9,15},{10,... | collective-permute-start | bytes 294920 | tf_op jit(solution)/shard_map/ppermute | solution.py:133
  35.3 9.8 %collective-permute-start.15 = (bf16[64,1280]{1,0:T(8,128)(2,1)S(1)}, bf16[64,1280]{1,0:T(8,128)(2,1)S(1)}, u32[]{:S(2)}, u32[]{:S(2)}) collective-permute-start(bf16[64,1280]{1,0:T(8,128)(2,1)S(1)} %shard_map.103), channel_id=1, source_target_pairs={{0,1},{1,0},{2,3},{3,2},{4,5},{5,4},{6,7},{7,6},{8,9},{9,8},{10,11... | collective-permute-start | bytes 491528 | tf_op jit(solution)/shard_map/ppermute | solution.py:133
  41.3 5.4 %collective-permute-start.18 = (bf16[64,1280]{1,0:T(8,128)(2,1)S(1)}, bf16[64,1280]{1,0:T(8,128)(2,1)S(1)}, u32[]{:S(2)}, u32[]{:S(2)}) collective-permute-start(bf16[64,1280]{1,0:T(8,128)(2,1)S(1)} %shard_map.105), channel_id=1, source_target_pairs={{0,1},{1,0},{2,3},{3,2},{4,5},{5,4},{6,7},{7,6},{8,9},{9,8},{10,11... | collective-permute-start | bytes 491528 | tf_op jit(solution)/shard_map/ppermute | solution.py:133
  48.2 1.6 %collective-permute-start.19 = (bf16[64,2048]{1,0:T(8,128)(2,1)S(1)}, bf16[64,2048]{1,0:T(8,128)(2,1)S(1)}, u32[]{:S(2)}, u32[]{:S(2)}) collective-permute-start(bf16[64,2048]{1,0:T(8,128)(2,1)S(1)} %get-tuple-element.85), channel_id=1, source_target_pairs={{0,8},{8,0},{16,24},{24,16},{1,9},{9,1},{17,25},{25,17},{2,10},{10... | collective-permute-start | bytes 786440 | tf_op jit(solution)/shard_map/ppermute | solution.py:133
  49.8 5.6 %collective-permute-start.20 = (bf16[32,2048]{1,0:T(8,128)(2,1)S(1)}, bf16[32,2048]{1,0:T(8,128)(2,1)S(1)}, u32[]{:S(2)}, u32[]{:S(2)}) collective-permute-start(bf16[32,2048]{1,0:T(8,128)(2,1)S(1)} %get-tuple-element.87), channel_id=1, source_target_pairs={{0,16},{8,24},{16,0},{24,8},{1,17},{9,25},{17,1},{25,9},{2,18},{10... | collective-permute-start | bytes 393224 | tf_op jit(solution)/shard_map/ppermute | solution.py:133

commit v3 on v2

--- a/solution.py
+++ b/solution.py
@@ -177,28 +177,19 @@
         out[:, left + cols : left + 2 * cols] = contract_cols(grad_panel, output_block(wo, b, cols)).astype(BF)
 
 
-def project_far_kernel(blocks, count, *refs):
+def project_first_kernel(b, count, *refs):
     pieces, (wq, wo, wkv, out, kv) = refs[:count], refs[count:]
     token_panel, grad_panel = panels(pieces)
-    project_blocks(token_panel, grad_panel, blocks, wq, wo, out.shape[1], out)
     kv[...] = jnp.dot(token_panel, wkv[...], preferred_element_type=F32).astype(BF)
+    width = out.shape[1] - kv.shape[1]
+    out[:, width:] = kv[...]
+    project_blocks(token_panel, grad_panel, [b], wq, wo, width, out)
 
 
 def project_kernel(blocks, count, *refs):
     pieces, (wq, wo, out) = refs[:count], refs[count:]
     token_panel, grad_panel = panels(pieces)
     project_blocks(token_panel, grad_panel, blocks, wq, wo, out.shape[1], out)
-
-
-def last_swap_kernel(block, kv, *outs):
-    cols, kv_cols = block.shape[1] // len(outs), kv.shape[1] // len(outs)
-    for at, out in enumerate(outs):
-        out[:, :cols] = block[:, at * cols : (at + 1) * cols]
-        out[:, cols:] = kv[:, at * kv_cols : (at + 1) * kv_cols]
-
-
-def add_kernel(left, right, out):
-    out[...] = plus(left[...], right[...]).astype(BF)
 
 
 def turn_kernel(*refs):
@@ -216,21 +207,23 @@
     return value
 
 
-def add_far_kernel(near, far, *outs):
-    width = outs[0].shape[1]
-    for at, out in enumerate(outs):
-        part = slice(at * width, (at + 1) * width)
-        out[...] = plus(near[:, part], far[:, part]).astype(BF)
-
-
-def attend_kernel(narrow, near, kv, far_query, far_grad, *refs):
+def add_first_kernel(near, kv, far, out, pair):
+    width = near.shape[1]
+    out[:, :width] = plus(near[...], far[:, :width]).astype(BF)
+    pair[...] = plus(kv[...], far[:, width:]).astype(BF)
+    out[:, width:] = pair[...]
+
+
+def add_next_kernel(near, far, pair, out):
+    width = near.shape[1]
+    out[:, :width] = plus(near[...], far[...]).astype(BF)
+    out[:, width:] = pair[...]
+
+
+def attend_kernel(narrow, near, far, pair, *refs):
     parts, out = refs[:-1], refs[-1]
-    width = parts[0].shape[1]
-    cols, far = width // 2, (far_query, far_grad)
-    block = near[...].astype(F32) + jnp.concatenate([r[:, :cols].astype(F32) for r in far], axis=1)
-    block = block + total(parts)
-    pair = kv[...].astype(F32) + jnp.concatenate([r[:, cols:].astype(F32) for r in far], axis=1)
-    value = jnp.concatenate([block, pair], axis=1).astype(BF)
+    value = jnp.concatenate([plus(near[...], far[...]), pair[...].astype(F32)], axis=1)
+    value = (value + total(parts)).astype(BF)
     rows = value.shape[0]
     cols = (value.shape[1] - 2 * HD) // 2
     piece = rows // narrow
@@ -411,66 +404,52 @@
     most = half - 1
     pieces = (*token_pieces, *grad_pieces)
     count = 2 * narrow
+
+    def project(block, pieces=pieces):
+        return call(
+            functools.partial(project_kernel, [block], count),
+            (*pieces, w_query, w_output),
+            [VMEM] * (count + 2),
+            jax.ShapeDtypeStruct((rows, 2 * cols), BF),
+            VMEM,
+            [],
+            8 * MIB,
+            4 * rows * features * cols,
+            4 * features * cols,
+        )
+
     far, kv = call(
-        functools.partial(project_far_kernel, far_blocks[:most], count),
+        functools.partial(project_first_kernel, far_blocks[0], count),
         (*pieces, w_query, w_output, wkv),
         [VMEM] * (count + 3),
-        [
-            jax.ShapeDtypeStruct((rows, 2 * cols * most), BF),
-            jax.ShapeDtypeStruct((rows, pair_cols), BF),
-        ],
+        [full, jax.ShapeDtypeStruct((rows, pair_cols), BF)],
         [VMEM] * 2,
         [],
         8 * MIB,
-        rows * weight_size,
-        weight_size,
-    )
-    far = swap(far, "wide", wide, 1)
-    def project(blocks, pieces=pieces):
-        return call(
-            functools.partial(project_kernel, blocks, count),
-            (*pieces, w_query, w_output),
-            [VMEM] * (count + 2),
-            jax.ShapeDtypeStruct((rows, 2 * cols * len(blocks)), BF),
-            VMEM,
-            [],
-            8 * MIB,
-            2 * rows * weight_size * len(blocks) // wide,
-            2 * weight_size * len(blocks) // wide,
-        )
-
-    near = project(near_blocks[:-1])
-    bit = 2
-    while bit < wide:
-        other = swap(kv, "wide", wide, bit)
-        if bit == 2:
-            other, _ = lax.optimization_barrier((other, near))
-        kv = call(
-            add_kernel,
-            (kv, other),
-            [VMEM] * 2,
-            jax.ShapeDtypeStruct((rows, pair_cols), BF),
-            VMEM,
+        2 * rows * features * (2 * cols + pair_cols),
+        2 * features * (2 * cols + pair_cols),
+    )
+    far = [swap(far, "wide", wide, 1)] + [swap(project(b), "wide", wide, 1) for b in far_blocks[1:most]]
+    sums, pair = [], None
+    for at in range(most):
+        near = project(near_blocks[at])
+        added, *rest = call(
+            add_next_kernel if sums else add_first_kernel,
+            (near, far[at], pair) if sums else (near, kv, far[at]),
+            [VMEM] * 3,
+            [full] if sums else [full, jax.ShapeDtypeStruct((rows, pair_cols), BF)],
+            [VMEM] * (1 if sums else 2),
             [],
             2 * MIB,
-            2 * rows * pair_cols,
-            6 * rows * pair_cols,
+            rows * 1024,
+            rows * 4096,
         )
-        bit *= 2
-    sums = call(
-        add_far_kernel,
-        (near, far),
-        [VMEM] * 2,
-        [jax.ShapeDtypeStruct((rows, 2 * cols), BF)] * most,
-        [VMEM] * most,
-        [],
-        2 * MIB,
-        rows * 2048,
-        rows * 8192,
-    )
+        pair = rest[0] if rest else pair
+        sums.append(added)
     received = [swap(part, "wide", wide, d) for part, d in zip(sums, near_blocks)]
+    far_last = swap(project(far_blocks[most]), "wide", wide, 1)
     later, _ = lax.optimization_barrier((pieces, sums[-1]))
-    near_last = project(near_blocks[-1:], later)
+    near_last = project(near_blocks[most], later)
     turned = call(
         turn_kernel,
         later[:narrow],
@@ -483,22 +462,10 @@
         4 * rows * features,
     )
     near_last, turned = lax.optimization_barrier((near_last, turned))
-    far_own = call(
-        last_swap_kernel,
-        (project(far_blocks[most:]), kv),
-        [VMEM] * 2,
-        [jax.ShapeDtypeStruct((rows, cols + HD), BF)] * 2,
-        [VMEM] * 2,
-        [],
-        2 * MIB,
-        0,
-        4 * rows * full.shape[1],
-    )
-    far_other = [swap(part, "wide", wide, 1) for part in far_own]
     own = call(
         functools.partial(attend_kernel, narrow),
-        (near_last, kv, *far_other, *received),
-        [VMEM] * (4 + len(received)),
+        (near_last, far_last, pair, *received),
+        [VMEM] * (3 + len(received)),
         full,
         VMEM,
         [],

time: 56.3 us -> 55.3 us (0.982)
  starting transfers between devices: 24.2 us -> 21.4 us
  waiting for transfers between devices: 8.27 us -> 9.65 us
    ppermute x21 -> x20, starting transfers between devices: 24.2 us -> 21.4 us  [swap(): return lax.ppermute(value, axis, [(i, i ^ distance) for i in range(size)])]
    ppermute x21 -> x20, waiting for transfers between devices: 8.27 us -> 9.65 us  [swap(): return lax.ppermute(value, axis, [(i, i ^ distance) for i in range(size)])]
    pallas_call x20 -> x23, Pallas kernels: 22.8 us -> 23.3 us  [call(): pl.pallas_call(kernel, out_shape=outs, in_specs=in_specs, out_specs=out_s...]
  transfers between devices with their start and end apart: 21 -> 20, of which waited for: 10 -> 8; matrix products, arithmetic and copies ran while one was open for 0% -> 0% of each run, Pallas kernels for 32% -> 35%
where the time goes in v3:
time: 55.3 us; the launch traced here: 55.2 us
  Pallas kernels  23.3 us (42%)
  starting transfers between devices  21.4 us (39%)
  waiting for transfers between devices  9.65 us (17%)
  between operations  0.85 us (2%)
    pallas_call x23, Pallas kernels, call(): pl.pallas_call(kernel, out_shape=outs, in_specs=in_specs, out_specs=out_s...  23.3 us
    ppermute x20, starting transfers between devices, swap(): return lax.ppermute(value, axis, [(i, i ^ distance) for i in range(size)])  21.4 us
    ppermute x20, waiting for transfers between devices, swap(): return lax.ppermute(value, axis, [(i, i ^ distance) for i in range(size)])  9.65 us
  transfers between devices with their start and end apart: 20, of which 8 were waited for; matrix products, arithmetic and copies ran while one was open for 0% of the time, Pallas kernels for 35%

profile of v3, /device:TPU:0, one launch (start us, length us, event | category | flops | bytes accessed | tf_op | source)
XLA Modules:
  0.0 55.2 jit_solution(12341117764347565916)
XLA Ops:
  0.7 3.0 %collective-permute-start.1 = (bf16[16,2048]{1,0:T(8,128)(2,1)}, bf16[16,2048]{1,0:T(8,128)(2,1)S(1)}, u32[]{:S(2)}, u32[]{:S(2)}) collective-permute-start(bf16[16,2048]{1,0:T(8,128)(2,1)} %refs_0_.15), channel_id=1, source_target_pairs={{0,16},{8,24},{16,0},{24,8},{1,17},{9,25},{17,1},{25,9},{2,18},{10... | collective-permute-start | bytes 196616 | tf_op jit(solution)/shard_map/ppermute | solution.py:133
  3.7 0.1 collective-permute-start.2
  3.8 0.5 collective-permute-start.4
  4.3 2.0 %shard_map.92.refs_10_.refs_8_ = bf16[2048,256]{1,0:T(8,128)(2,1)S(1)} custom-call(bf16[2048,256]{1,0:T(8,128)(2,1)} %source.1, bf16[2048,2048]{1,0:T(8,128)(2,1)} %refs_6_.1, bf16[2048,2048]{1,0:T(8,128)(2,1)} %refs_7_.5), custom_call_target="tpu_custom_call" | custom-call | bytes 17825792 | tf_op jit(solution)/shard_map/pallas_call | solution.py:137
  6.3 0.0 collective-permute-done.1.refs_2_
  6.3 1.9 %collective-permute-done.2.refs_6_.refs_3_ = bf16[16,2048]{1,0:T(8,128)(2,1)S(1)} collective-permute-done((bf16[16,2048]{1,0:T(8,128)(2,1)}, bf16[16,2048]{1,0:T(8,128)(2,1)S(1)}, u32[]{:S(2)}, u32[]{:S(2)}) %collective-permute-start.2) | collective-permute-done | bytes 65568 | tf_op jit(solution)/shard_map/ppermute | solution.py:133
  8.2 0.5 collective-permute-start.5
  8.7 0.0 collective-permute-done.refs_1_
  8.7 0.0 collective-permute-done.4.refs_5_.refs_2_
  8.7 0.7 %collective-permute-done.3.refs_3_ = bf16[16,2048]{1,0:T(8,128)(2,1)S(1)} collective-permute-done((bf16[16,2048]{1,0:T(8,128)(2,1)S(1)}, bf16[16,2048]{1,0:T(8,128)(2,1)S(1)}, u32[]{:S(2)}, u32[]{:S(2)}) %collective-permute-start.3) | collective-permute-done | bytes 65568 | tf_op jit(solution)/shard_map/ppermute | solution.py:133
  9.4 0.2 collective-permute-done.5.refs_7_.refs_4_
  9.6 0.8 %shard_map.96 = (bf16[64,768]{1,0:T(8,128)(2,1)S(1)}, bf16[64,256]{1,0:T(8,128)(2,1)S(1)}) custom-call(bf16[16,2048]{1,0:T(8,128)(2,1)S(1)} %copy-done.3, bf16[16,2048]{1,0:T(8,128)(2,1)S(1)} %collective-permute-done.refs_1_, bf16[16,2048]{1,0:T(8,128)(2,1)S(1)} %collective-permute-done.1.refs_2_, bf16[16,2048]{1,0:T(8,128)(2,1)S(1)} %collective-permute-done.3.refs_3_, ...), custom_call_target="tpu_custom_call" | custom-call | flops 201326592 | bytes 3145728 | tf_op jit(solution)/shard_map/pallas_call | solution.py:137
  10.4 1.6 %collective-permute-start.7 = (bf16[64,768]{1,0:T(8,128)(2,1)S(1)}, bf16[64,768]{1,0:T(8,128)(2,1)S(1)}, u32[]{:S(2)}, u32[]{:S(2)}) collective-permute-start(bf16[64,768]{1,0:T(8,128)(2,1)S(1)} %get-tuple-element.50), channel_id=1, source_target_pairs={{0,1},{1,0},{2,3},{3,2},{4,5},{5,4},{6,7},{7,6},{8,9},{9,8},{10,11... | collective-permute-start | bytes 294920 | tf_op jit(solution)/shard_map/ppermute | solution.py:133
  12.0 0.6 %shard_map.103 = bf16[64,512]{1,0:T(8,128)(2,1)S(1)} custom-call(bf16[16,2048]{1,0:T(8,128)(2,1)S(1)} %copy-done.3, bf16[16,2048]{1,0:T(8,128)(2,1)S(1)} %collective-permute-done.refs_1_, bf16[16,2048]{1,0:T(8,128)(2,1)S(1)} %collective-permute-done.1.refs_2_, bf16[16,2048]{1,0:T(8,128)(2,1)S(1)} %collective-permute-done.3.refs_3_, ...), custom_call_target="tpu_custom_call" | custom-call | flops 134217728 | bytes 2097152 | tf_op jit(solution)/shard_map/pallas_call | solution.py:137
  12.6 0.6 %collective-permute-start.10 = (bf16[64,512]{1,0:T(8,128)(2,1)S(1)}, bf16[64,512]{1,0:T(8,128)(2,1)S(1)}, u32[]{:S(2)}, u32[]{:S(2)}) collective-permute-start(bf16[64,512]{1,0:T(8,128)(2,1)S(1)} %shard_map.103), channel_id=1, source_target_pairs={{0,1},{1,0},{2,3},{3,2},{4,5},{5,4},{6,7},{7,6},{8,9},{9,8},{10,11... | collective-permute-start | bytes 196616 | tf_op jit(solution)/shard_map/ppermute | solution.py:133
  13.1 0.6 %shard_map.94 = bf16[64,512]{1,0:T(8,128)(2,1)S(1)} custom-call(bf16[16,2048]{1,0:T(8,128)(2,1)S(1)} %copy-done.3, bf16[16,2048]{1,0:T(8,128)(2,1)S(1)} %collective-permute-done.refs_1_, bf16[16,2048]{1,0:T(8,128)(2,1)S(1)} %collective-permute-done.1.refs_2_, bf16[16,2048]{1,0:T(8,128)(2,1)S(1)} %collective-permute-done.3.refs_3_, ...), custom_call_target="tpu_custom_call" | custom-call | flops 134217728 | bytes 2097152 | tf_op jit(solution)/shard_map/pallas_call | solution.py:137
  13.8 1.6 %collective-permute-start.6 = (bf16[64,512]{1,0:T(8,128)(2,1)S(1)}, bf16[64,512]{1,0:T(8,128)(2,1)S(1)}, u32[]{:S(2)}, u32[]{:S(2)}) collective-permute-start(bf16[64,512]{1,0:T(8,128)(2,1)S(1)} %shard_map.94), channel_id=1, source_target_pairs={{0,1},{1,0},{2,3},{3,2},{4,5},{5,4},{6,7},{7,6},{8,9},{9,8},{10,11... | collective-permute-start | bytes 196616 | tf_op jit(solution)/shard_map/ppermute | solution.py:133
  15.4 0.6 %shard_map.102.near = bf16[64,512]{1,0:T(8,128)(2,1)S(1)} custom-call(bf16[16,2048]{1,0:T(8,128)(2,1)S(1)} %copy-done.3, bf16[16,2048]{1,0:T(8,128)(2,1)S(1)} %collective-permute-done.refs_1_, bf16[16,2048]{1,0:T(8,128)(2,1)S(1)} %collective-permute-done.1.refs_2_, bf16[16,2048]{1,0:T(8,128)(2,1)S(1)} %collective-permute-done.3.refs_3_, ...), custom_call_target="tpu_custom_call" | custom-call | flops 134217728 | bytes 2097152 | tf_op jit(solution)/shard_map/pallas_call | solution.py:137
  16.0 0.6 %shard_map.95.near = bf16[64,512]{1,0:T(8,128)(2,1)S(1)} custom-call(bf16[16,2048]{1,0:T(8,128)(2,1)S(1)} %copy-done.3, bf16[16,2048]{1,0:T(8,128)(2,1)S(1)} %collective-permute-done.refs_1_, bf16[16,2048]{1,0:T(8,128)(2,1)S(1)} %collective-permute-done.1.refs_2_, bf16[16,2048]{1,0:T(8,128)(2,1)S(1)} %collective-permute-done.3.refs_3_, ...), custom_call_target="tpu_custom_call" | custom-call | flops 134217728 | bytes 2097152 | tf_op jit(solution)/shard_map/pallas_call | solution.py:137
  16.6 0.6 %shard_map.93.near = bf16[64,512]{1,0:T(8,128)(2,1)S(1)} custom-call(bf16[16,2048]{1,0:T(8,128)(2,1)S(1)} %copy-done.3, bf16[16,2048]{1,0:T(8,128)(2,1)S(1)} %collective-permute-done.refs_1_, bf16[16,2048]{1,0:T(8,128)(2,1)S(1)} %collective-permute-done.1.refs_2_, bf16[16,2048]{1,0:T(8,128)(2,1)S(1)} %collective-permute-done.3.refs_3_, ...), custom_call_target="tpu_custom_call" | custom-call | flops 134217728 | bytes 2097152 | tf_op jit(solution)/shard_map/pallas_call | solution.py:137
  17.3 3.6 %collective-permute-start.9 = (bf16[64,768]{1,0:T(8,128)(2,1)S(1)}, bf16[64,768]{1,0:T(8,128)(2,1)S(1)}, u32[]{:S(2)}, u32[]{:S(2)}) collective-permute-start(bf16[64,768]{1,0:T(8,128)(2,1)S(1)} %get-tuple-element.61), channel_id=1, source_target_pairs={{0,6},{1,7},{2,4},{3,5},{4,2},{5,3},{6,0},{7,1},{8,14},{9,15},{10,... | collective-permute-start | bytes 294920 | tf_op jit(solution)/shard_map/ppermute | solution.py:133
  21.0 0.1 collective-permute-start.11
  21.1 0.9 %collective-permute-start.12 = (bf16[64,768]{1,0:T(8,128)(2,1)S(1)}, bf16[64,768]{1,0:T(8,128)(2,1)S(1)}, u32[]{:S(2)}, u32[]{:S(2)}) collective-permute-start(bf16[64,768]{1,0:T(8,128)(2,1)S(1)} %shard_map.98), channel_id=1, source_target_pairs={{0,2},{1,3},{2,0},{3,1},{4,6},{5,7},{6,4},{7,5},{8,10},{9,11},{10,... | collective-permute-start | bytes 294920 | tf_op jit(solution)/shard_map/ppermute | solution.py:133
  22.0 0.6 %shard_map.101 = bf16[64,512]{1,0:T(8,128)(2,1)S(1)} custom-call(bf16[16,2048]{1,0:T(8,128)(2,1)S(1)} %copy-done.3, bf16[16,2048]{1,0:T(8,128)(2,1)S(1)} %collective-permute-done.refs_1_, bf16[16,2048]{1,0:T(8,128)(2,1)S(1)} %collective-permute-done.1.refs_2_, bf16[16,2048]{1,0:T(8,128)(2,1)S(1)} %collective-permute-done.3.refs_3_, ...), custom_call_target="tpu_custom_call" | custom-call | flops 134217728 | bytes 2097152 | tf_op jit(solution)/shard_map/pallas_call | solution.py:137
  22.6 1.4 %collective-permute-start.8 = (bf16[64,512]{1,0:T(8,128)(2,1)S(1)}, bf16[64,512]{1,0:T(8,128)(2,1)S(1)}, u32[]{:S(2)}, u32[]{:S(2)}) collective-permute-start(bf16[64,512]{1,0:T(8,128)(2,1)S(1)} %shard_map.101), channel_id=1, source_target_pairs={{0,1},{1,0},{2,3},{3,2},{4,5},{5,4},{6,7},{7,6},{8,9},{9,8},{10,11... | collective-permute-start | bytes 196616 | tf_op jit(solution)/shard_map/ppermute | solution.py:133
  24.0 0.2 shard_map.100.refs_0_
  24.2 0.6 %shard_map.99.near = bf16[64,512]{1,0:T(8,128)(2,1)S(1)} custom-call(bf16[16,2048]{1,0:T(8,128)(2,1)S(1)} %copy-done.3, bf16[16,2048]{1,0:T(8,128)(2,1)S(1)} %collective-permute-done.refs_1_, bf16[16,2048]{1,0:T(8,128)(2,1)S(1)} %collective-permute-done.1.refs_2_, bf16[16,2048]{1,0:T(8,128)(2,1)S(1)} %collective-permute-done.3.refs_3_, ...), custom_call_target="tpu_custom_call" | custom-call | flops 134217728 | bytes 2097152 | tf_op jit(solution)/shard_map/pallas_call | solution.py:137
  24.8 2.1 %collective-permute-done.8.far = bf16[64,512]{1,0:T(8,128)(2,1)S(1)} collective-permute-done((bf16[64,512]{1,0:T(8,128)(2,1)S(1)}, bf16[64,512]{1,0:T(8,128)(2,1)S(1)}, u32[]{:S(2)}, u32[]{:S(2)}) %collective-permute-start.8) | collective-permute-done | bytes 65568 | tf_op jit(solution)/shard_map/ppermute | solution.py:133
  26.9 1.9 %collective-permute-done.11.refs_1_ = bf16[64,768]{1,0:T(8,128)(2,1)S(1)} collective-permute-done((bf16[64,768]{1,0:T(8,128)(2,1)S(1)}, bf16[64,768]{1,0:T(8,128)(2,1)S(1)}, u32[]{:S(2)}, u32[]{:S(2)}) %collective-permute-start.11) | collective-permute-done | bytes 98336 | tf_op jit(solution)/shard_map/ppermute | solution.py:133
  28.9 1.1 %shard_map.105.refs_0_.refs_5_.refs_2_.refs_7_ = bf16[64,768]{1,0:T(8,128)(2,1)S(1)} custom-call(bf16[64,512]{1,0:T(8,128)(2,1)S(1)} %shard_map.99.near, bf16[64,512]{1,0:T(8,128)(2,1)S(1)} %collective-permute-done.8.far, bf16[64,256]{1,0:T(8,128)(2,1)S(1)} %get-tuple-element.51.pair, bf16[64,768]{1,0:T(8,128)(2,1)S(1)} %collective-permute-done.9.refs_0_, ...), custom_call_target="tpu_custom_call" | custom-call | flops 25165824 | bytes 786432 | tf_op jit(solution)/shard_map/pallas_call | solution.py:137
  30.0 0.6 %collective-permute-start.13 = (bf16[64,768]{1,0:T(8,128)(2,1)S(1)}, bf16[64,768]{1,0:T(8,128)(2,1)S(1)}, u32[]{:S(2)}, u32[]{:S(2)}) collective-permute-start(bf16[64,768]{1,0:T(8,128)(2,1)S(1)} %shard_map.105.refs_0_.refs_5_.refs_2_.refs_7_), channel_id=1, source_target_pairs={{0,2},{1,3},{2,0},{3,1},{4,6},{5,7},{6,4},{7,5},{8,10},{9,11},{10,... | collective-permute-start | bytes 294920 | tf_op jit(solution)/shard_map/ppermute | solution.py:133
  30.6 2.6 %collective-permute-start.16 = (bf16[64,768]{1,0:T(8,128)(2,1)S(1)}, bf16[64,768]{1,0:T(8,128)(2,1)S(1)}, u32[]{:S(2)}, u32[]{:S(2)}) collective-permute-start(bf16[64,768]{1,0:T(8,128)(2,1)S(1)} %shard_map.105.refs_0_.refs_5_.refs_2_.refs_7_), channel_id=1, source_target_pairs={{0,4},{1,5},{2,6},{3,7},{4,0},{5,1},{6,2},{7,3},{8,12},{9,13},{10,... | collective-permute-start | bytes 294920 | tf_op jit(solution)/shard_map/ppermute | solution.py:133
  33.1 1.3 %collective-permute-start.15 = (bf16[64,768]{1,0:T(8,128)(2,1)S(1)}, bf16[64,768]{1,0:T(8,128)(2,1)S(1)}, u32[]{:S(2)}, u32[]{:S(2)}) collective-permute-start(bf16[64,768]{1,0:T(8,128)(2,1)S(1)} %shard_map.105.refs_0_.refs_5_.refs_2_.refs_7_), channel_id=1, source_target_pairs={{0,6},{1,7},{2,4},{3,5},{4,2},{5,3},{6,0},{7,1},{8,14},{9,15},{10,... | collective-permute-start | bytes 294920 | tf_op jit(solution)/shard_map/ppermute | solution.py:133
  34.4 0.7 %collective-permute-done.13.refs_1_.refs_6_.refs_5_.refs_10_ = bf16[64,768]{1,0:T(8,128)(2,1)S(1)} collective-permute-done((bf16[64,768]{1,0:T(8,128)(2,1)S(1)}, bf16[64,768]{1,0:T(8,128)(2,1)S(1)}, u32[]{:S(2)}, u32[]{:S(2)}) %collective-permute-start.13) | collective-permute-done | bytes 98336 | tf_op jit(solution)/shard_map/ppermute | solution.py:133
  35.1 1.0 %collective-permute-start.14 = (bf16[64,1280]{1,0:T(8,128)(2,1)S(1)}, bf16[64,1280]{1,0:T(8,128)(2,1)S(1)}, u32[]{:S(2)}, u32[]{:S(2)}) collective-permute-start(bf16[64,1280]{1,0:T(8,128)(2,1)S(1)} %shard_map.106), channel_id=1, source_target_pairs={{0,1},{1,0},{2,3},{3,2},{4,5},{5,4},{6,7},{7,6},{8,9},{9,8},{10,11... | collective-permute-start | bytes 491528 | tf_op jit(solution)/shard_map/ppermute | solution.py:133
  36.1 3.6 %shard_map.107 = (bf16[2048,2048]{1,0:T(8,128)(2,1)}, bf16[2048,2048]{1,0:T(8,128)(2,1)}, f32[64,2048]{1,0:T(8,128)S(1)}, f32[64,2048]{1,0:T(8,128)S(1)}) custom-call(bf16[2048,64]{1,0:T(8,128)(2,1)S(1)} %shard_map.100.refs_0_, bf16[16,2048]{1,0:T(8,128)(2,1)S(1)} %copy-done.2, bf16[16,2048]{1,0:T(8,128)(2,1)S(1)} %collective-permute-done.4.refs_5_.refs_2_, ...), custom_call_target="tpu_custom_call" | custom-call | flops 536870912 | bytes 8388608 | tf_op jit(solution)/shard_map/pallas_call | solution.py:137
  39.7 0.6 %collective-permute-done.16.refs_1_.refs_6_.refs_4_.refs_9_ = bf16[64,768]{1,0:T(8,128)(2,1)S(1)} collective-permute-done((bf16[64,768]{1,0:T(8,128)(2,1)S(1)}, bf16[64,768]{1,0:T(8,128)(2,1)S(1)}, u32[]{:S(2)}, u32[]{:S(2)}) %collective-permute-start.16) | collective-permute-done | bytes 98336 | tf_op jit(solution)/shard_map/ppermute | solution.py:133
  40.3 1.0 %collective-permute-start.17 = (bf16[64,1280]{1,0:T(8,128)(2,1)S(1)}, bf16[64,1280]{1,0:T(8,128)(2,1)S(1)}, u32[]{:S(2)}, u32[]{:S(2)}) collective-permute-start(bf16[64,1280]{1,0:T(8,128)(2,1)S(1)} %shard_map.108), channel_id=1, source_target_pairs={{0,1},{1,0},{2,3},{3,2},{4,5},{5,4},{6,7},{7,6},{8,9},{9,8},{10,11... | collective-permute-start | bytes 491528 | tf_op jit(solution)/shard_map/ppermute | solution.py:133
  41.3 3.2 %shard_map.109 = (bf16[2048,2048]{1,0:T(8,128)(2,1)}, bf16[2048,2048]{1,0:T(8,128)(2,1)}, f32[64,2048]{1,0:T(8,128)S(1)}, f32[64,2048]{1,0:T(8,128)S(1)}) custom-call(bf16[2048,64]{1,0:T(8,128)(2,1)S(1)} %shard_map.100.refs_0_, bf16[16,2048]{1,0:T(8,128)(2,1)S(1)} %copy-done.2, ...), custom_call_target="tpu_custom_call", output_to_operand_aliasing={{0}: (11, {}), {1}: (12, {})} | custom-call | flops 536870912 | bytes 8388608 | tf_op jit(solution)/shard_map/pallas_call | solution.py:137
  44.6 1.1 %shard_map.110 = (f32[64,2048]{1,0:T(8,128)S(1)}, f32[64,2048]{1,0:T(8,128)S(1)}) custom-call(bf16[64,1280]{1,0:T(8,128)(2,1)S(1)} %collective-permute-done.14.refs_0_.refs_5_, bf16[2048,2048]{1,0:T(8,128)(2,1)S(1)} %copy-done, bf16[2048,2048]{1,0:T(8,128)(2,1)S(1)} %copy-done.1, f32[64,2048]{1,0:T(8,128)S(1)} %get-tuple-element.72.refs_3_, ...), custom_call_target="tpu_custom_call" | custom-call | flops 268435456 | bytes 4194304 | tf_op jit(solution)/shard_map/pallas_call | solution.py:137
  45.7 0.0 collective-permute-done.17.refs_1_.refs_6_
  45.7 1.4 %shard_map.111 = (bf16[64,2048]{1,0:T(8,128)(2,1)S(1)}, bf16[64,2048]{1,0:T(8,128)(2,1)S(1)}) custom-call(bf16[64,1280]{1,0:T(8,128)(2,1)S(1)} %collective-permute-done.14.refs_0_.refs_5_, bf16[64,1280]{1,0:T(8,128)(2,1)S(1)} %collective-permute-done.17.refs_1_.refs_6_, bf16[64,768]{1,0:T(8,128)(2,1)S(1)} %shard_map.105.refs_0_.refs_5_.refs_2_.refs_7_, ...), custom_call_target="tpu_custom_call" | custom-call | flops 570425344 | bytes 8912896 | tf_op jit(solution)/shard_map/pallas_call | solution.py:137
  47.2 0.1 collective-permute-start.18
  47.2 1.5 %collective-permute-done.18.far = bf16[64,2048]{1,0:T(8,128)(2,1)S(1)} collective-permute-done((bf16[64,2048]{1,0:T(8,128)(2,1)S(1)}, bf16[64,2048]{1,0:T(8,128)(2,1)S(1)}, u32[]{:S(2)}, u32[]{:S(2)}) %collective-permute-start.18) | collective-permute-done | bytes 262176 | tf_op jit(solution)/shard_map/ppermute | solution.py:133
  48.8 0.1 shard_map.112
  48.8 1.0 %collective-permute-start.19 = (bf16[32,2048]{1,0:T(8,128)(2,1)S(1)}, bf16[32,2048]{1,0:T(8,128)(2,1)S(1)}, u32[]{:S(2)}, u32[]{:S(2)}) collective-permute-start(bf16[32,2048]{1,0:T(8,128)(2,1)S(1)} %get-tuple-element.79), channel_id=1, source_target_pairs={{0,16},{8,24},{16,0},{24,8},{1,17},{9,25},{17,1},{25,9},{2,18},{10... | collective-permute-start | bytes 393224 | tf_op jit(solution)/shard_map/ppermute | solution.py:133
  49.9 4.6 %shard_map.114 = (bf16[2048,2048]{1,0:T(8,128)(2,1)}, bf16[2048,2048]{1,0:T(8,128)(2,1)}, bf16[2048,256]{1,0:T(8,128)(2,1)}) custom-call(bf16[2048,64]{1,0:T(8,128)(2,1)S(1)} %shard_map.100.refs_0_, bf16[16,2048]{1,0:T(8,128)(2,1)S(1)} %copy-done.2, ...), custom_call_target="tpu_custom_call", output_to_operand_aliasing={{0}: (11, {}), {1}: (12, {})} | custom-call | flops 1073741824 | bytes 16777216 | tf_op jit(solution)/shard_map/pallas_call | solution.py:137
  54.5 0.7 %shard_map.113 = (bf16[16,2048]{1,0:T(8,128)(2,1)}, bf16[16,2048]{1,0:T(8,128)(2,1)}) custom-call(bf16[32,2048]{1,0:T(8,128)(2,1)S(1)} %get-tuple-element.78.refs_0_, bf16[32,2048]{1,0:T(8,128)(2,1)S(1)} %collective-permute-done.19.refs_1_), custom_call_target="tpu_custom_call" | custom-call | flops 262144 | bytes 524288 | tf_op jit(solution)/shard_map/pallas_call | solution.py:137
  (23 shorter events, 0.1 us)
Async XLA Ops:
  0.6 8.9 %copy-start.3 = (bf16[16,2048]{1,0:T(8,128)(2,1)S(1)}, bf16[16,2048]{1,0:T(8,128)(2,1)}, u32[]{:S(2)}) copy-start(bf16[16,2048]{1,0:T(8,128)(2,1)} %refs_0_.15) | copy-start | bytes 196612
  0.6 8.9 %copy-start.2 = (bf16[16,2048]{1,0:T(8,128)(2,1)S(1)}, bf16[16,2048]{1,0:T(8,128)(2,1)}, u32[]{:S(2)}) copy-start(bf16[16,2048]{1,0:T(8,128)(2,1)} %refs_1_.7) | copy-start | bytes 196612
  0.7 8.9 %copy-start.1 = (bf16[2048,2048]{1,0:T(8,128)(2,1)S(1)}, bf16[2048,2048]{1,0:T(8,128)(2,1)}, u32[]{:S(2)}) copy-start(bf16[2048,2048]{1,0:T(8,128)(2,1)} %refs_7_.5) | copy-start | bytes 25165828
  0.7 8.9 %copy-start = (bf16[2048,2048]{1,0:T(8,128)(2,1)S(1)}, bf16[2048,2048]{1,0:T(8,128)(2,1)}, u32[]{:S(2)}) copy-start(bf16[2048,2048]{1,0:T(8,128)(2,1)} %refs_6_.1) | copy-start | bytes 25165828
  0.7 5.6 %collective-permute-start.1 = (bf16[16,2048]{1,0:T(8,128)(2,1)}, bf16[16,2048]{1,0:T(8,128)(2,1)S(1)}, u32[]{:S(2)}, u32[]{:S(2)}) collective-permute-start(bf16[16,2048]{1,0:T(8,128)(2,1)} %refs_0_.15), channel_id=1, source_target_pairs={{0,16},{8,24},{16,0},{24,8},{1,17},{9,25},{17,1},{25,9},{2,18},{10... | collective-permute-start | bytes 196616 | tf_op jit(solution)/shard_map/ppermute | solution.py:133
  3.7 4.5 %collective-permute-start.2 = (bf16[16,2048]{1,0:T(8,128)(2,1)}, bf16[16,2048]{1,0:T(8,128)(2,1)S(1)}, u32[]{:S(2)}, u32[]{:S(2)}) collective-permute-start(bf16[16,2048]{1,0:T(8,128)(2,1)} %refs_1_.7), channel_id=1, source_target_pairs={{0,16},{8,24},{16,0},{24,8},{1,17},{9,25},{17,1},{25,9},{2,18},{10... | collective-permute-start | bytes 196616 | tf_op jit(solution)/shard_map/ppermute | solution.py:133
  3.8 4.9 %collective-permute-start = (bf16[16,2048]{1,0:T(8,128)(2,1)}, bf16[16,2048]{1,0:T(8,128)(2,1)S(1)}, u32[]{:S(2)}, u32[]{:S(2)}) collective-permute-start(bf16[16,2048]{1,0:T(8,128)(2,1)} %refs_0_.15), channel_id=1, source_target_pairs={{0,8},{8,0},{16,24},{24,16},{1,9},{9,1},{17,25},{25,17},{2,10},{10... | collective-permute-start | bytes 196616 | tf_op jit(solution)/shard_map/ppermute | solution.py:133
  3.8 4.9 %collective-permute-start.4 = (bf16[16,2048]{1,0:T(8,128)(2,1)}, bf16[16,2048]{1,0:T(8,128)(2,1)S(1)}, u32[]{:S(2)}, u32[]{:S(2)}) collective-permute-start(bf16[16,2048]{1,0:T(8,128)(2,1)} %refs_1_.7), channel_id=1, source_target_pairs={{0,8},{8,0},{16,24},{24,16},{1,9},{9,1},{17,25},{25,17},{2,10},{10... | collective-permute-start | bytes 196616 | tf_op jit(solution)/shard_map/ppermute | solution.py:133
  8.2 1.3 %collective-permute-start.3 = (bf16[16,2048]{1,0:T(8,128)(2,1)S(1)}, bf16[16,2048]{1,0:T(8,128)(2,1)S(1)}, u32[]{:S(2)}, u32[]{:S(2)}) collective-permute-start(bf16[16,2048]{1,0:T(8,128)(2,1)S(1)} %collective-permute-done.1.refs_2_), channel_id=1, source_target_pairs={{0,8},{8,0},{16,24},{24,16},{1,9},{9,1},{17,25},{25,17},{2,10},{10... | collective-permute-start | bytes 196616 | tf_op jit(solution)/shard_map/ppermute | solution.py:133
  8.2 1.4 %collective-permute-start.5 = (bf16[16,2048]{1,0:T(8,128)(2,1)S(1)}, bf16[16,2048]{1,0:T(8,128)(2,1)S(1)}, u32[]{:S(2)}, u32[]{:S(2)}) collective-permute-start(bf16[16,2048]{1,0:T(8,128)(2,1)S(1)} %collective-permute-done.2.refs_6_.refs_3_), channel_id=1, source_target_pairs={{0,8},{8,0},{16,24},{24,16},{1,9},{9,1},{17,25},{25,17},{2,10},{10... | collective-permute-start | bytes 196616 | tf_op jit(solution)/shard_map/ppermute | solution.py:133
  10.4 6.9 %collective-permute-start.7 = (bf16[64,768]{1,0:T(8,128)(2,1)S(1)}, bf16[64,768]{1,0:T(8,128)(2,1)S(1)}, u32[]{:S(2)}, u32[]{:S(2)}) collective-permute-start(bf16[64,768]{1,0:T(8,128)(2,1)S(1)} %get-tuple-element.50), channel_id=1, source_target_pairs={{0,1},{1,0},{2,3},{3,2},{4,5},{5,4},{6,7},{7,6},{8,9},{9,8},{10,11... | collective-permute-start | bytes 294920 | tf_op jit(solution)/shard_map/ppermute | solution.py:133
  12.6 8.4 %collective-permute-start.10 = (bf16[64,512]{1,0:T(8,128)(2,1)S(1)}, bf16[64,512]{1,0:T(8,128)(2,1)S(1)}, u32[]{:S(2)}, u32[]{:S(2)}) collective-permute-start(bf16[64,512]{1,0:T(8,128)(2,1)S(1)} %shard_map.103), channel_id=1, source_target_pairs={{0,1},{1,0},{2,3},{3,2},{4,5},{5,4},{6,7},{7,6},{8,9},{9,8},{10,11... | collective-permute-start | bytes 196616 | tf_op jit(solution)/shard_map/ppermute | solution.py:133
  13.8 7.3 %collective-permute-start.6 = (bf16[64,512]{1,0:T(8,128)(2,1)S(1)}, bf16[64,512]{1,0:T(8,128)(2,1)S(1)}, u32[]{:S(2)}, u32[]{:S(2)}) collective-permute-start(bf16[64,512]{1,0:T(8,128)(2,1)S(1)} %shard_map.94), channel_id=1, source_target_pairs={{0,1},{1,0},{2,3},{3,2},{4,5},{5,4},{6,7},{7,6},{8,9},{9,8},{10,11... | collective-permute-start | bytes 196616 | tf_op jit(solution)/shard_map/ppermute | solution.py:133
  17.3 9.6 %collective-permute-start.9 = (bf16[64,768]{1,0:T(8,128)(2,1)S(1)}, bf16[64,768]{1,0:T(8,128)(2,1)S(1)}, u32[]{:S(2)}, u32[]{:S(2)}) collective-permute-start(bf16[64,768]{1,0:T(8,128)(2,1)S(1)} %get-tuple-element.61), channel_id=1, source_target_pairs={{0,6},{1,7},{2,4},{3,5},{4,2},{5,3},{6,0},{7,1},{8,14},{9,15},{10,... | collective-permute-start | bytes 294920 | tf_op jit(solution)/shard_map/ppermute | solution.py:133
  21.0 7.9 %collective-permute-start.11 = (bf16[64,768]{1,0:T(8,128)(2,1)S(1)}, bf16[64,768]{1,0:T(8,128)(2,1)S(1)}, u32[]{:S(2)}, u32[]{:S(2)}) collective-permute-start(bf16[64,768]{1,0:T(8,128)(2,1)S(1)} %shard_map.104), channel_id=1, source_target_pairs={{0,4},{1,5},{2,6},{3,7},{4,0},{5,1},{6,2},{7,3},{8,12},{9,13},{10,... | collective-permute-start | bytes 294920 | tf_op jit(solution)/shard_map/ppermute | solution.py:133
  21.1 7.8 %collective-permute-start.12 = (bf16[64,768]{1,0:T(8,128)(2,1)S(1)}, bf16[64,768]{1,0:T(8,128)(2,1)S(1)}, u32[]{:S(2)}, u32[]{:S(2)}) collective-permute-start(bf16[64,768]{1,0:T(8,128)(2,1)S(1)} %shard_map.98), channel_id=1, source_target_pairs={{0,2},{1,3},{2,0},{3,1},{4,6},{5,7},{6,4},{7,5},{8,10},{9,11},{10,... | collective-permute-start | bytes 294920 | tf_op jit(solution)/shard_map/ppermute | solution.py:133
  22.6 4.3 %collective-permute-start.8 = (bf16[64,512]{1,0:T(8,128)(2,1)S(1)}, bf16[64,512]{1,0:T(8,128)(2,1)S(1)}, u32[]{:S(2)}, u32[]{:S(2)}) collective-permute-start(bf16[64,512]{1,0:T(8,128)(2,1)S(1)} %shard_map.101), channel_id=1, source_target_pairs={{0,1},{1,0},{2,3},{3,2},{4,5},{5,4},{6,7},{7,6},{8,9},{9,8},{10,11... | collective-permute-start | bytes 196616 | tf_op jit(solution)/shard_map/ppermute | solution.py:133
  30.0 5.1 %collective-permute-start.13 = (bf16[64,768]{1,0:T(8,128)(2,1)S(1)}, bf16[64,768]{1,0:T(8,128)(2,1)S(1)}, u32[]{:S(2)}, u32[]{:S(2)}) collective-permute-start(bf16[64,768]{1,0:T(8,128)(2,1)S(1)} %shard_map.105.refs_0_.refs_5_.refs_2_.refs_7_), channel_id=1, source_target_pairs={{0,2},{1,3},{2,0},{3,1},{4,6},{5,7},{6,4},{7,5},{8,10},{9,11},{10,... | collective-permute-start | bytes 294920 | tf_op jit(solution)/shard_map/ppermute | solution.py:133
  30.6 9.8 %collective-permute-start.16 = (bf16[64,768]{1,0:T(8,128)(2,1)S(1)}, bf16[64,768]{1,0:T(8,128)(2,1)S(1)}, u32[]{:S(2)}, u32[]{:S(2)}) collective-permute-start(bf16[64,768]{1,0:T(8,128)(2,1)S(1)} %shard_map.105.refs_0_.refs_5_.refs_2_.refs_7_), channel_id=1, source_target_pairs={{0,4},{1,5},{2,6},{3,7},{4,0},{5,1},{6,2},{7,3},{8,12},{9,13},{10,... | collective-permute-start | bytes 294920 | tf_op jit(solution)/shard_map/ppermute | solution.py:133
  33.1 7.2 %collective-permute-start.15 = (bf16[64,768]{1,0:T(8,128)(2,1)S(1)}, bf16[64,768]{1,0:T(8,128)(2,1)S(1)}, u32[]{:S(2)}, u32[]{:S(2)}) collective-permute-start(bf16[64,768]{1,0:T(8,128)(2,1)S(1)} %shard_map.105.refs_0_.refs_5_.refs_2_.refs_7_), channel_id=1, source_target_pairs={{0,6},{1,7},{2,4},{3,5},{4,2},{5,3},{6,0},{7,1},{8,14},{9,15},{10,... | collective-permute-start | bytes 294920 | tf_op jit(solution)/shard_map/ppermute | solution.py:133
  35.1 9.4 %collective-permute-start.14 = (bf16[64,1280]{1,0:T(8,128)(2,1)S(1)}, bf16[64,1280]{1,0:T(8,128)(2,1)S(1)}, u32[]{:S(2)}, u32[]{:S(2)}) collective-permute-start(bf16[64,1280]{1,0:T(8,128)(2,1)S(1)} %shard_map.106), channel_id=1, source_target_pairs={{0,1},{1,0},{2,3},{3,2},{4,5},{5,4},{6,7},{7,6},{8,9},{9,8},{10,11... | collective-permute-start | bytes 491528 | tf_op jit(solution)/shard_map/ppermute | solution.py:133
  40.3 5.4 %collective-permute-start.17 = (bf16[64,1280]{1,0:T(8,128)(2,1)S(1)}, bf16[64,1280]{1,0:T(8,128)(2,1)S(1)}, u32[]{:S(2)}, u32[]{:S(2)}) collective-permute-start(bf16[64,1280]{1,0:T(8,128)(2,1)S(1)} %shard_map.108), channel_id=1, source_target_pairs={{0,1},{1,0},{2,3},{3,2},{4,5},{5,4},{6,7},{7,6},{8,9},{9,8},{10,11... | collective-permute-start | bytes 491528 | tf_op jit(solution)/shard_map/ppermute | solution.py:133
  47.2 1.6 %collective-permute-start.18 = (bf16[64,2048]{1,0:T(8,128)(2,1)S(1)}, bf16[64,2048]{1,0:T(8,128)(2,1)S(1)}, u32[]{:S(2)}, u32[]{:S(2)}) collective-permute-start(bf16[64,2048]{1,0:T(8,128)(2,1)S(1)} %get-tuple-element.77), channel_id=1, source_target_pairs={{0,8},{8,0},{16,24},{24,16},{1,9},{9,1},{17,25},{25,17},{2,10},{10... | collective-permute-start | bytes 786440 | tf_op jit(solution)/shard_map/ppermute | solution.py:133
  48.8 5.6 %collective-permute-start.19 = (bf16[32,2048]{1,0:T(8,128)(2,1)S(1)}, bf16[32,2048]{1,0:T(8,128)(2,1)S(1)}, u32[]{:S(2)}, u32[]{:S(2)}) collective-permute-start(bf16[32,2048]{1,0:T(8,128)(2,1)S(1)} %get-tuple-element.79), channel_id=1, source_target_pairs={{0,16},{8,24},{16,0},{24,8},{1,17},{9,25},{17,1},{25,9},{2,18},{10... | collective-permute-start | bytes 393224 | tf_op jit(solution)/shard_map/ppermute | solution.py:133

commit v4 on v3

--- a/solution.py
+++ b/solution.py
@@ -177,13 +177,32 @@
         out[:, left + cols : left + 2 * cols] = contract_cols(grad_panel, output_block(wo, b, cols)).astype(BF)
 
 
-def project_first_kernel(b, count, *refs):
-    pieces, (wq, wo, wkv, out, kv) = refs[:count], refs[count:]
-    token_panel, grad_panel = panels(pieces)
-    kv[...] = jnp.dot(token_panel, wkv[...], preferred_element_type=F32).astype(BF)
-    width = out.shape[1] - kv.shape[1]
-    out[:, width:] = kv[...]
-    project_blocks(token_panel, grad_panel, [b], wq, wo, width, out)
+def query_columns(panel, blocks, wq, out):
+    cols = out.shape[1] // len(blocks)
+    for at, b in enumerate(blocks):
+        out[:, at * cols : (at + 1) * cols] = jnp.dot(panel, query_block(wq, b, cols), preferred_element_type=F32).astype(BF)
+
+
+def project_first_kernel(blocks, count, *refs):
+    pieces, (wq, wkv, out, kv) = refs[:count], refs[count:]
+    panel = jnp.concatenate([r[...] for r in pieces], axis=0)
+    kv[...] = jnp.dot(panel, wkv[...], preferred_element_type=F32).astype(BF)
+    query_columns(panel, blocks, wq, out)
+
+
+def project_query_kernel(blocks, count, *refs):
+    pieces, (wq, out) = refs[:count], refs[count:]
+    query_columns(jnp.concatenate([r[...] for r in pieces], axis=0), blocks, wq, out)
+
+
+def join_block_kernel(b, at, count, *refs):
+    pieces, (wo, queries, *kv, out) = refs[:count], refs[count:]
+    cols = wo.shape[0] // lax.axis_size("wide")
+    out[:, :cols] = queries[:, at * cols : (at + 1) * cols]
+    panel = jnp.concatenate([r[...] for r in pieces], axis=0)
+    out[:, cols : 2 * cols] = contract_cols(panel, output_block(wo, b, cols)).astype(BF)
+    if kv:
+        out[:, 2 * cols :] = kv[0][...]
 
 
 def project_kernel(blocks, count, *refs):
@@ -397,10 +416,37 @@
         0,
         2 * weight_size,
     )
-    token_pieces, grad_pieces, wkv = lax.optimization_barrier((token_pieces, grad_pieces, wkv))
-    for pieces in (token_pieces, grad_pieces):
-        pieces.update({b ^ 1: swap(p, "narrow", narrow, 1) for b, p in pieces.items() if b})
-    token_pieces, grad_pieces = [[{**own, **p}[b] for b in range(narrow)] for own, p in zip(beside, (token_pieces, grad_pieces))]
+    def complete(pieces, own, behind):
+        pieces, _ = lax.optimization_barrier((pieces, behind))
+        pieces = {**own, **pieces}
+        pieces.update({b ^ 1: swap(p, "narrow", narrow, 1) for b, p in pieces.items() if b > 1})
+        return [pieces[b] for b in range(narrow)]
+
+    token_pieces = complete(token_pieces, beside[0], wkv)
+    kv_shape = jax.ShapeDtypeStruct((rows, pair_cols), BF)
+    query_first, kv = call(
+        functools.partial(project_first_kernel, far_blocks[:1], narrow),
+        (*token_pieces, w_query, wkv),
+        [VMEM] * (narrow + 2),
+        [jax.ShapeDtypeStruct((rows, cols), BF), kv_shape],
+        [VMEM] * 2,
+        [],
+        8 * MIB,
+        2 * rows * features * (cols + pair_cols),
+        2 * features * (cols + pair_cols),
+    )
+    grad_pieces = complete(grad_pieces, beside[1], wkv)
+    query_rest = call(
+        functools.partial(project_query_kernel, far_blocks[1:], narrow),
+        (*token_pieces, w_query),
+        [VMEM] * (narrow + 1),
+        jax.ShapeDtypeStruct((rows, cols * (half - 1)), BF),
+        VMEM,
+        [],
+        8 * MIB,
+        2 * rows * features * cols * (half - 1),
+        2 * features * cols * (half - 1),
+    )
     most = half - 1
     pieces = (*token_pieces, *grad_pieces)
     count = 2 * narrow
@@ -418,18 +464,22 @@
             4 * features * cols,
         )
 
-    far, kv = call(
-        functools.partial(project_first_kernel, far_blocks[0], count),
-        (*pieces, w_query, w_output, wkv),
-        [VMEM] * (count + 3),
-        [full, jax.ShapeDtypeStruct((rows, pair_cols), BF)],
-        [VMEM] * 2,
-        [],
-        8 * MIB,
-        2 * rows * features * (2 * cols + pair_cols),
-        2 * features * (2 * cols + pair_cols),
-    )
-    far = [swap(far, "wide", wide, 1)] + [swap(project(b), "wide", wide, 1) for b in far_blocks[1:most]]
+    def far_swap(at):
+        queries = (query_rest,) if at else (query_first, kv)
+        block = call(
+            functools.partial(join_block_kernel, far_blocks[at], max(at - 1, 0), narrow),
+            (*grad_pieces, w_output, *queries),
+            [VMEM] * (narrow + 1 + len(queries)),
+            jax.ShapeDtypeStruct((rows, 2 * cols + (0 if at else pair_cols)), BF),
+            VMEM,
+            [],
+            8 * MIB,
+            2 * rows * features * cols,
+            2 * features * cols,
+        )
+        return swap(block, "wide", wide, 1)
+
+    far = [far_swap(at) for at in range(most)]
     sums, pair = [], None
     for at in range(most):
         near = project(near_blocks[at])
@@ -447,7 +497,7 @@
         pair = rest[0] if rest else pair
         sums.append(added)
     received = [swap(part, "wide", wide, d) for part, d in zip(sums, near_blocks)]
-    far_last = swap(project(far_blocks[most]), "wide", wide, 1)
+    far_last = far_swap(most)
     later, _ = lax.optimization_barrier((pieces, sums[-1]))
     near_last = project(near_blocks[most], later)
     turned = call(

time: 55.3 us -> 55.2 us (level)
  waiting for transfers between devices: 9.65 us -> 11.9 us
  starting transfers between devices: 21.4 us -> 19.5 us
    ppermute x20, waiting for transfers between devices: 9.65 us -> 11.9 us  [swap(): return lax.ppermute(value, axis, [(i, i ^ distance) for i in range(size)])]
    ppermute x20, starting transfers between devices: 21.4 us -> 19.5 us  [swap(): return lax.ppermute(value, axis, [(i, i ^ distance) for i in range(size)])]
    pallas_call x23 -> x25, Pallas kernels: 23.3 us -> 22.8 us  [call(): pl.pallas_call(kernel, out_shape=outs, in_specs=in_specs, out_specs=out_s...]
  transfers between devices with their start and end apart: 20 -> 20, of which waited for: 8 -> 9; matrix products, arithmetic and copies ran while one was open for 0% -> 0% of each run, Pallas kernels for 35% -> 35%
where the time goes in v4:
time: 55.2 us; the launch traced here: 55.1 us
  Pallas kernels  22.8 us (41%)
  starting transfers between devices  19.5 us (35%)
  waiting for transfers between devices  11.9 us (22%)
  between operations  0.85 us (2%)
    pallas_call x25, Pallas kernels, call(): pl.pallas_call(kernel, out_shape=outs, in_specs=in_specs, out_specs=out_s...  22.8 us
    ppermute x20, starting transfers between devices, swap(): return lax.ppermute(value, axis, [(i, i ^ distance) for i in range(size)])  19.5 us
    ppermute x20, waiting for transfers between devices, swap(): return lax.ppermute(value, axis, [(i, i ^ distance) for i in range(size)])  11.9 us
  transfers between devices with their start and end apart: 20, of which 9 were waited for; matrix products, arithmetic and copies ran while one was open for 0% of the time, Pallas kernels for 35%

profile of v4, /device:TPU:0, one launch (start us, length us, event | category | flops | bytes accessed | tf_op | source)
XLA Modules:
  0.0 55.1 jit_solution(18169121694969854317)
XLA Ops:
  0.7 3.0 %collective-permute-start.1 = (bf16[16,2048]{1,0:T(8,128)(2,1)}, bf16[16,2048]{1,0:T(8,128)(2,1)S(1)}, u32[]{:S(2)}, u32[]{:S(2)}) collective-permute-start(bf16[16,2048]{1,0:T(8,128)(2,1)} %refs_0_.18), channel_id=1, source_target_pairs={{0,16},{8,24},{16,0},{24,8},{1,17},{9,25},{17,1},{25,9},{2,18},{10... | collective-permute-start | bytes 196616 | tf_op jit(solution)/shard_map/ppermute | solution.py:133
  3.7 0.1 collective-permute-start.4
  3.7 0.0 collective-permute-start
  3.7 1.2 %shard_map.92.refs_5_.refs_8_ = bf16[2048,256]{1,0:T(8,128)(2,1)S(1)} custom-call(bf16[2048,256]{1,0:T(8,128)(2,1)} %source.1, bf16[2048,2048]{1,0:T(8,128)(2,1)} %refs_6_.1, bf16[2048,2048]{1,0:T(8,128)(2,1)} %refs_7_.5), custom_call_target="tpu_custom_call" | custom-call | bytes 17825792 | tf_op jit(solution)/shard_map/pallas_call | solution.py:137
  5.0 0.0 copy-start
  5.0 1.3 %collective-permute-done.1.refs_2_ = bf16[16,2048]{1,0:T(8,128)(2,1)S(1)} collective-permute-done((bf16[16,2048]{1,0:T(8,128)(2,1)}, bf16[16,2048]{1,0:T(8,128)(2,1)S(1)}, u32[]{:S(2)}, u32[]{:S(2)}) %collective-permute-start.1) | collective-permute-done | bytes 65568 | tf_op jit(solution)/shard_map/ppermute | solution.py:133
  6.3 0.5 collective-permute-start.3
  6.8 1.4 %collective-permute-done.4.refs_6_.refs_2_.refs_3_ = bf16[16,2048]{1,0:T(8,128)(2,1)S(1)} collective-permute-done((bf16[16,2048]{1,0:T(8,128)(2,1)}, bf16[16,2048]{1,0:T(8,128)(2,1)S(1)}, u32[]{:S(2)}, u32[]{:S(2)}) %collective-permute-start.4) | collective-permute-done | bytes 65568 | tf_op jit(solution)/shard_map/ppermute | solution.py:133
  8.2 0.5 shard_map.97
  8.7 0.7 %collective-permute-done.5.refs_7_.refs_3_.refs_4_ = bf16[16,2048]{1,0:T(8,128)(2,1)S(1)} collective-permute-done((bf16[16,2048]{1,0:T(8,128)(2,1)S(1)}, bf16[16,2048]{1,0:T(8,128)(2,1)S(1)}, u32[]{:S(2)}, u32[]{:S(2)}) %collective-permute-start.5) | collective-permute-done | bytes 65568 | tf_op jit(solution)/shard_map/ppermute | solution.py:133
  9.4 0.4 shard_map.98
  9.8 1.6 %collective-permute-start.7 = (bf16[64,768]{1,0:T(8,128)(2,1)S(1)}, bf16[64,768]{1,0:T(8,128)(2,1)S(1)}, u32[]{:S(2)}, u32[]{:S(2)}) collective-permute-start(bf16[64,768]{1,0:T(8,128)(2,1)S(1)} %shard_map.98), channel_id=1, source_target_pairs={{0,1},{1,0},{2,3},{3,2},{4,5},{5,4},{6,7},{7,6},{8,9},{9,8},{10,11... | collective-permute-start | bytes 294920 | tf_op jit(solution)/shard_map/ppermute | solution.py:133
  11.4 0.7 %shard_map.94.refs_5_ = bf16[64,768]{1,0:T(8,128)(2,1)S(1)} custom-call(bf16[16,2048]{1,0:T(8,128)(2,1)S(1)} %copy-done.3, bf16[16,2048]{1,0:T(8,128)(2,1)S(1)} %collective-permute-done.refs_1_, bf16[16,2048]{1,0:T(8,128)(2,1)S(1)} %collective-permute-done.1.refs_2_, bf16[16,2048]{1,0:T(8,128)(2,1)S(1)} %collective-permute-done.2.refs_3_, ...), custom_call_target="tpu_custom_call" | custom-call | flops 201326592 | bytes 3145728 | tf_op jit(solution)/shard_map/pallas_call | solution.py:137
  12.1 0.5 shard_map.105
  12.6 0.6 %collective-permute-start.10 = (bf16[64,512]{1,0:T(8,128)(2,1)S(1)}, bf16[64,512]{1,0:T(8,128)(2,1)S(1)}, u32[]{:S(2)}, u32[]{:S(2)}) collective-permute-start(bf16[64,512]{1,0:T(8,128)(2,1)S(1)} %shard_map.105), channel_id=1, source_target_pairs={{0,1},{1,0},{2,3},{3,2},{4,5},{5,4},{6,7},{7,6},{8,9},{9,8},{10,11... | collective-permute-start | bytes 196616 | tf_op jit(solution)/shard_map/ppermute | solution.py:133
  13.1 0.4 shard_map.95
  13.6 1.6 %collective-permute-start.6 = (bf16[64,512]{1,0:T(8,128)(2,1)S(1)}, bf16[64,512]{1,0:T(8,128)(2,1)S(1)}, u32[]{:S(2)}, u32[]{:S(2)}) collective-permute-start(bf16[64,512]{1,0:T(8,128)(2,1)S(1)} %shard_map.95), channel_id=1, source_target_pairs={{0,1},{1,0},{2,3},{3,2},{4,5},{5,4},{6,7},{7,6},{8,9},{9,8},{10,11... | collective-permute-start | bytes 196616 | tf_op jit(solution)/shard_map/ppermute | solution.py:133
  15.2 0.6 %shard_map.104.near = bf16[64,512]{1,0:T(8,128)(2,1)S(1)} custom-call(bf16[16,2048]{1,0:T(8,128)(2,1)S(1)} %copy-done.3, bf16[16,2048]{1,0:T(8,128)(2,1)S(1)} %collective-permute-done.refs_1_, bf16[16,2048]{1,0:T(8,128)(2,1)S(1)} %collective-permute-done.1.refs_2_, bf16[16,2048]{1,0:T(8,128)(2,1)S(1)} %collective-permute-done.2.refs_3_, ...), custom_call_target="tpu_custom_call" | custom-call | flops 134217728 | bytes 2097152 | tf_op jit(solution)/shard_map/pallas_call | solution.py:137
  15.8 0.6 %shard_map.96.near = bf16[64,512]{1,0:T(8,128)(2,1)S(1)} custom-call(bf16[16,2048]{1,0:T(8,128)(2,1)S(1)} %copy-done.3, bf16[16,2048]{1,0:T(8,128)(2,1)S(1)} %collective-permute-done.refs_1_, bf16[16,2048]{1,0:T(8,128)(2,1)S(1)} %collective-permute-done.1.refs_2_, bf16[16,2048]{1,0:T(8,128)(2,1)S(1)} %collective-permute-done.2.refs_3_, ...), custom_call_target="tpu_custom_call" | custom-call | flops 134217728 | bytes 2097152 | tf_op jit(solution)/shard_map/pallas_call | solution.py:137
  16.4 0.6 %shard_map.93.near = bf16[64,512]{1,0:T(8,128)(2,1)S(1)} custom-call(bf16[16,2048]{1,0:T(8,128)(2,1)S(1)} %copy-done.3, bf16[16,2048]{1,0:T(8,128)(2,1)S(1)} %collective-permute-done.refs_1_, bf16[16,2048]{1,0:T(8,128)(2,1)S(1)} %collective-permute-done.1.refs_2_, bf16[16,2048]{1,0:T(8,128)(2,1)S(1)} %collective-permute-done.2.refs_3_, ...), custom_call_target="tpu_custom_call" | custom-call | flops 134217728 | bytes 2097152 | tf_op jit(solution)/shard_map/pallas_call | solution.py:137
  17.1 3.7 %collective-permute-start.9 = (bf16[64,768]{1,0:T(8,128)(2,1)S(1)}, bf16[64,768]{1,0:T(8,128)(2,1)S(1)}, u32[]{:S(2)}, u32[]{:S(2)}) collective-permute-start(bf16[64,768]{1,0:T(8,128)(2,1)S(1)} %get-tuple-element.59), channel_id=1, source_target_pairs={{0,6},{1,7},{2,4},{3,5},{4,2},{5,3},{6,0},{7,1},{8,14},{9,15},{10,... | collective-permute-start | bytes 294920 | tf_op jit(solution)/shard_map/ppermute | solution.py:133
  20.8 0.1 collective-permute-start.11
  20.9 0.8 %collective-permute-start.12 = (bf16[64,768]{1,0:T(8,128)(2,1)S(1)}, bf16[64,768]{1,0:T(8,128)(2,1)S(1)}, u32[]{:S(2)}, u32[]{:S(2)}) collective-permute-start(bf16[64,768]{1,0:T(8,128)(2,1)S(1)} %shard_map.100), channel_id=1, source_target_pairs={{0,2},{1,3},{2,0},{3,1},{4,6},{5,7},{6,4},{7,5},{8,10},{9,11},{10,... | collective-permute-start | bytes 294920 | tf_op jit(solution)/shard_map/ppermute | solution.py:133
  21.8 0.4 shard_map.103
  22.2 0.6 %collective-permute-start.8 = (bf16[64,512]{1,0:T(8,128)(2,1)S(1)}, bf16[64,512]{1,0:T(8,128)(2,1)S(1)}, u32[]{:S(2)}, u32[]{:S(2)}) collective-permute-start(bf16[64,512]{1,0:T(8,128)(2,1)S(1)} %shard_map.103), channel_id=1, source_target_pairs={{0,1},{1,0},{2,3},{3,2},{4,5},{5,4},{6,7},{7,6},{8,9},{9,8},{10,11... | collective-permute-start | bytes 196616 | tf_op jit(solution)/shard_map/ppermute | solution.py:133
  22.8 0.2 shard_map.102.refs_0_
  23.0 0.6 %shard_map.101.near = bf16[64,512]{1,0:T(8,128)(2,1)S(1)} custom-call(bf16[16,2048]{1,0:T(8,128)(2,1)S(1)} %copy-done.3, bf16[16,2048]{1,0:T(8,128)(2,1)S(1)} %collective-permute-done.refs_1_, bf16[16,2048]{1,0:T(8,128)(2,1)S(1)} %collective-permute-done.1.refs_2_, bf16[16,2048]{1,0:T(8,128)(2,1)S(1)} %collective-permute-done.2.refs_3_, ...), custom_call_target="tpu_custom_call" | custom-call | flops 134217728 | bytes 2097152 | tf_op jit(solution)/shard_map/pallas_call | solution.py:137
  23.6 2.9 %collective-permute-done.8.far = bf16[64,512]{1,0:T(8,128)(2,1)S(1)} collective-permute-done((bf16[64,512]{1,0:T(8,128)(2,1)S(1)}, bf16[64,512]{1,0:T(8,128)(2,1)S(1)}, u32[]{:S(2)}, u32[]{:S(2)}) %collective-permute-start.8) | collective-permute-done | bytes 65568 | tf_op jit(solution)/shard_map/ppermute | solution.py:133
  26.5 2.0 %collective-permute-done.11.refs_1_ = bf16[64,768]{1,0:T(8,128)(2,1)S(1)} collective-permute-done((bf16[64,768]{1,0:T(8,128)(2,1)S(1)}, bf16[64,768]{1,0:T(8,128)(2,1)S(1)}, u32[]{:S(2)}, u32[]{:S(2)}) %collective-permute-start.11) | collective-permute-done | bytes 98336 | tf_op jit(solution)/shard_map/ppermute | solution.py:133
  28.5 1.1 %shard_map.107.refs_0_.refs_5_.refs_2_.refs_7_ = bf16[64,768]{1,0:T(8,128)(2,1)S(1)} custom-call(bf16[64,512]{1,0:T(8,128)(2,1)S(1)} %shard_map.101.near, bf16[64,512]{1,0:T(8,128)(2,1)S(1)} %collective-permute-done.8.far, bf16[64,256]{1,0:T(8,128)(2,1)S(1)} %get-tuple-element.49.pair, bf16[64,768]{1,0:T(8,128)(2,1)S(1)} %collective-permute-done.9.refs_0_, ...), custom_call_target="tpu_custom_call" | custom-call | flops 25165824 | bytes 786432 | tf_op jit(solution)/shard_map/pallas_call | solution.py:137
  29.6 0.6 %collective-permute-start.13 = (bf16[64,768]{1,0:T(8,128)(2,1)S(1)}, bf16[64,768]{1,0:T(8,128)(2,1)S(1)}, u32[]{:S(2)}, u32[]{:S(2)}) collective-permute-start(bf16[64,768]{1,0:T(8,128)(2,1)S(1)} %shard_map.107.refs_0_.refs_5_.refs_2_.refs_7_), channel_id=1, source_target_pairs={{0,2},{1,3},{2,0},{3,1},{4,6},{5,7},{6,4},{7,5},{8,10},{9,11},{10,... | collective-permute-start | bytes 294920 | tf_op jit(solution)/shard_map/ppermute | solution.py:133
  30.2 2.6 %collective-permute-start.16 = (bf16[64,768]{1,0:T(8,128)(2,1)S(1)}, bf16[64,768]{1,0:T(8,128)(2,1)S(1)}, u32[]{:S(2)}, u32[]{:S(2)}) collective-permute-start(bf16[64,768]{1,0:T(8,128)(2,1)S(1)} %shard_map.107.refs_0_.refs_5_.refs_2_.refs_7_), channel_id=1, source_target_pairs={{0,4},{1,5},{2,6},{3,7},{4,0},{5,1},{6,2},{7,3},{8,12},{9,13},{10,... | collective-permute-start | bytes 294920 | tf_op jit(solution)/shard_map/ppermute | solution.py:133
  32.8 1.3 %collective-permute-start.15 = (bf16[64,768]{1,0:T(8,128)(2,1)S(1)}, bf16[64,768]{1,0:T(8,128)(2,1)S(1)}, u32[]{:S(2)}, u32[]{:S(2)}) collective-permute-start(bf16[64,768]{1,0:T(8,128)(2,1)S(1)} %shard_map.107.refs_0_.refs_5_.refs_2_.refs_7_), channel_id=1, source_target_pairs={{0,6},{1,7},{2,4},{3,5},{4,2},{5,3},{6,0},{7,1},{8,14},{9,15},{10,... | collective-permute-start | bytes 294920 | tf_op jit(solution)/shard_map/ppermute | solution.py:133
  34.1 0.7 %collective-permute-done.13.refs_1_.refs_6_.refs_5_.refs_10_ = bf16[64,768]{1,0:T(8,128)(2,1)S(1)} collective-permute-done((bf16[64,768]{1,0:T(8,128)(2,1)S(1)}, bf16[64,768]{1,0:T(8,128)(2,1)S(1)}, u32[]{:S(2)}, u32[]{:S(2)}) %collective-permute-start.13) | collective-permute-done | bytes 98336 | tf_op jit(solution)/shard_map/ppermute | solution.py:133
  34.8 0.5 collective-permute-start.14
  35.3 3.6 %shard_map.109 = (bf16[2048,2048]{1,0:T(8,128)(2,1)}, bf16[2048,2048]{1,0:T(8,128)(2,1)}, f32[64,2048]{1,0:T(8,128)S(1)}, f32[64,2048]{1,0:T(8,128)S(1)}) custom-call(bf16[2048,64]{1,0:T(8,128)(2,1)S(1)} %shard_map.102.refs_0_, bf16[16,2048]{1,0:T(8,128)(2,1)S(1)} %copy-done.2, bf16[16,2048]{1,0:T(8,128)(2,1)S(1)} %collective-permute-done.3.refs_5_.refs_1_.refs_2_, ...), custom_call_target="tpu_custom_call" | custom-call | flops 536870912 | bytes 8388608 | tf_op jit(solution)/shard_map/pallas_call | solution.py:137
  38.9 1.0 %collective-permute-done.16.refs_1_.refs_6_.refs_4_.refs_9_ = bf16[64,768]{1,0:T(8,128)(2,1)S(1)} collective-permute-done((bf16[64,768]{1,0:T(8,128)(2,1)S(1)}, bf16[64,768]{1,0:T(8,128)(2,1)S(1)}, u32[]{:S(2)}, u32[]{:S(2)}) %collective-permute-start.16) | collective-permute-done | bytes 98336 | tf_op jit(solution)/shard_map/ppermute | solution.py:133
  40.0 0.6 %collective-permute-start.17 = (bf16[64,1280]{1,0:T(8,128)(2,1)S(1)}, bf16[64,1280]{1,0:T(8,128)(2,1)S(1)}, u32[]{:S(2)}, u32[]{:S(2)}) collective-permute-start(bf16[64,1280]{1,0:T(8,128)(2,1)S(1)} %shard_map.110), channel_id=1, source_target_pairs={{0,1},{1,0},{2,3},{3,2},{4,5},{5,4},{6,7},{7,6},{8,9},{9,8},{10,11... | collective-permute-start | bytes 491528 | tf_op jit(solution)/shard_map/ppermute | solution.py:133
  40.6 3.2 %shard_map.111 = (bf16[2048,2048]{1,0:T(8,128)(2,1)}, bf16[2048,2048]{1,0:T(8,128)(2,1)}, f32[64,2048]{1,0:T(8,128)S(1)}, f32[64,2048]{1,0:T(8,128)S(1)}) custom-call(bf16[2048,64]{1,0:T(8,128)(2,1)S(1)} %shard_map.102.refs_0_, bf16[16,2048]{1,0:T(8,128)(2,1)S(1)} %copy-done.2, ...), custom_call_target="tpu_custom_call", output_to_operand_aliasing={{0}: (11, {}), {1}: (12, {})} | custom-call | flops 536870912 | bytes 8388608 | tf_op jit(solution)/shard_map/pallas_call | solution.py:137
  43.9 1.1 %shard_map.112 = (f32[64,2048]{1,0:T(8,128)S(1)}, f32[64,2048]{1,0:T(8,128)S(1)}) custom-call(bf16[64,1280]{1,0:T(8,128)(2,1)S(1)} %collective-permute-done.14.refs_0_.refs_5_, bf16[2048,2048]{1,0:T(8,128)(2,1)S(1)} %copy-done.1, bf16[2048,2048]{1,0:T(8,128)(2,1)S(1)} %copy-done, f32[64,2048]{1,0:T(8,128)S(1)} %get-tuple-element.70.refs_3_, ...), custom_call_target="tpu_custom_call" | custom-call | flops 268435456 | bytes 4194304 | tf_op jit(solution)/shard_map/pallas_call | solution.py:137
  45.0 0.4 collective-permute-done.17.refs_1_.refs_6_
  45.4 1.4 %shard_map.113 = (bf16[64,2048]{1,0:T(8,128)(2,1)S(1)}, bf16[64,2048]{1,0:T(8,128)(2,1)S(1)}) custom-call(bf16[64,1280]{1,0:T(8,128)(2,1)S(1)} %collective-permute-done.14.refs_0_.refs_5_, bf16[64,1280]{1,0:T(8,128)(2,1)S(1)} %collective-permute-done.17.refs_1_.refs_6_, bf16[64,768]{1,0:T(8,128)(2,1)S(1)} %shard_map.107.refs_0_.refs_5_.refs_2_.refs_7_, ...), custom_call_target="tpu_custom_call" | custom-call | flops 570425344 | bytes 8912896 | tf_op jit(solution)/shard_map/pallas_call | solution.py:137
  46.8 0.1 collective-permute-start.18
  46.9 1.5 %collective-permute-done.18.far = bf16[64,2048]{1,0:T(8,128)(2,1)S(1)} collective-permute-done((bf16[64,2048]{1,0:T(8,128)(2,1)S(1)}, bf16[64,2048]{1,0:T(8,128)(2,1)S(1)}, u32[]{:S(2)}, u32[]{:S(2)}) %collective-permute-start.18) | collective-permute-done | bytes 262176 | tf_op jit(solution)/shard_map/ppermute | solution.py:133
  48.4 0.1 shard_map.114
  48.5 1.3 %collective-permute-start.19 = (bf16[32,2048]{1,0:T(8,128)(2,1)S(1)}, bf16[32,2048]{1,0:T(8,128)(2,1)S(1)}, u32[]{:S(2)}, u32[]{:S(2)}) collective-permute-start(bf16[32,2048]{1,0:T(8,128)(2,1)S(1)} %get-tuple-element.77), channel_id=1, source_target_pairs={{0,16},{8,24},{16,0},{24,8},{1,17},{9,25},{17,1},{25,9},{2,18},{10... | collective-permute-start | bytes 393224 | tf_op jit(solution)/shard_map/ppermute | solution.py:133
  49.8 4.6 %shard_map.116 = (bf16[2048,2048]{1,0:T(8,128)(2,1)}, bf16[2048,2048]{1,0:T(8,128)(2,1)}, bf16[2048,256]{1,0:T(8,128)(2,1)}) custom-call(bf16[2048,64]{1,0:T(8,128)(2,1)S(1)} %shard_map.102.refs_0_, bf16[16,2048]{1,0:T(8,128)(2,1)S(1)} %copy-done.2, ...), custom_call_target="tpu_custom_call", output_to_operand_aliasing={{0}: (11, {}), {1}: (12, {})} | custom-call | flops 1073741824 | bytes 16777216 | tf_op jit(solution)/shard_map/pallas_call | solution.py:137
  54.4 0.7 %shard_map.115 = (bf16[16,2048]{1,0:T(8,128)(2,1)}, bf16[16,2048]{1,0:T(8,128)(2,1)}) custom-call(bf16[32,2048]{1,0:T(8,128)(2,1)S(1)} %get-tuple-element.76.refs_0_, bf16[32,2048]{1,0:T(8,128)(2,1)S(1)} %collective-permute-done.19.refs_1_), custom_call_target="tpu_custom_call" | custom-call | flops 262144 | bytes 524288 | tf_op jit(solution)/shard_map/pallas_call | solution.py:137
  (25 shorter events, 0.2 us)
Async XLA Ops:
  0.6 7.5 %copy-start.3 = (bf16[16,2048]{1,0:T(8,128)(2,1)S(1)}, bf16[16,2048]{1,0:T(8,128)(2,1)}, u32[]{:S(2)}) copy-start(bf16[16,2048]{1,0:T(8,128)(2,1)} %refs_0_.18) | copy-start | bytes 196612
  0.6 5.6 %copy-start.2 = (bf16[16,2048]{1,0:T(8,128)(2,1)S(1)}, bf16[16,2048]{1,0:T(8,128)(2,1)}, u32[]{:S(2)}) copy-start(bf16[16,2048]{1,0:T(8,128)(2,1)} %refs_1_.7) | copy-start | bytes 196612
  0.7 7.5 %copy-start.1 = (bf16[2048,2048]{1,0:T(8,128)(2,1)S(1)}, bf16[2048,2048]{1,0:T(8,128)(2,1)}, u32[]{:S(2)}) copy-start(bf16[2048,2048]{1,0:T(8,128)(2,1)} %refs_6_.1) | copy-start | bytes 25165828
  0.7 5.6 %collective-permute-start.1 = (bf16[16,2048]{1,0:T(8,128)(2,1)}, bf16[16,2048]{1,0:T(8,128)(2,1)S(1)}, u32[]{:S(2)}, u32[]{:S(2)}) collective-permute-start(bf16[16,2048]{1,0:T(8,128)(2,1)} %refs_0_.18), channel_id=1, source_target_pairs={{0,16},{8,24},{16,0},{24,8},{1,17},{9,25},{17,1},{25,9},{2,18},{10... | collective-permute-start | bytes 196616 | tf_op jit(solution)/shard_map/ppermute | solution.py:133
  3.7 4.5 %collective-permute-start.4 = (bf16[16,2048]{1,0:T(8,128)(2,1)}, bf16[16,2048]{1,0:T(8,128)(2,1)S(1)}, u32[]{:S(2)}, u32[]{:S(2)}) collective-permute-start(bf16[16,2048]{1,0:T(8,128)(2,1)} %refs_1_.7), channel_id=1, source_target_pairs={{0,16},{8,24},{16,0},{24,8},{1,17},{9,25},{17,1},{25,9},{2,18},{10... | collective-permute-start | bytes 196616 | tf_op jit(solution)/shard_map/ppermute | solution.py:133
  3.7 4.4 %collective-permute-start = (bf16[16,2048]{1,0:T(8,128)(2,1)}, bf16[16,2048]{1,0:T(8,128)(2,1)S(1)}, u32[]{:S(2)}, u32[]{:S(2)}) collective-permute-start(bf16[16,2048]{1,0:T(8,128)(2,1)} %refs_0_.18), channel_id=1, source_target_pairs={{0,8},{8,0},{16,24},{24,16},{1,9},{9,1},{17,25},{25,17},{2,10},{10... | collective-permute-start | bytes 196616 | tf_op jit(solution)/shard_map/ppermute | solution.py:133
  5.0 4.4 %copy-start = (bf16[2048,2048]{1,0:T(8,128)(2,1)S(1)}, bf16[2048,2048]{1,0:T(8,128)(2,1)}, u32[]{:S(2)}) copy-start(bf16[2048,2048]{1,0:T(8,128)(2,1)} %refs_7_.5) | copy-start | bytes 25165828
  6.3 1.9 %collective-permute-start.2 = (bf16[16,2048]{1,0:T(8,128)(2,1)S(1)}, bf16[16,2048]{1,0:T(8,128)(2,1)S(1)}, u32[]{:S(2)}, u32[]{:S(2)}) collective-permute-start(bf16[16,2048]{1,0:T(8,128)(2,1)S(1)} %collective-permute-done.1.refs_2_), channel_id=1, source_target_pairs={{0,8},{8,0},{16,24},{24,16},{1,9},{9,1},{17,25},{25,17},{2,10},{10... | collective-permute-start | bytes 196616 | tf_op jit(solution)/shard_map/ppermute | solution.py:133
  6.3 2.4 %collective-permute-start.3 = (bf16[16,2048]{1,0:T(8,128)(2,1)S(1)}, bf16[16,2048]{1,0:T(8,128)(2,1)S(1)}, u32[]{:S(2)}, u32[]{:S(2)}) collective-permute-start(bf16[16,2048]{1,0:T(8,128)(2,1)S(1)} %copy-done.2), channel_id=1, source_target_pairs={{0,8},{8,0},{16,24},{24,16},{1,9},{9,1},{17,25},{25,17},{2,10},{10... | collective-permute-start | bytes 196616 | tf_op jit(solution)/shard_map/ppermute | solution.py:133
  8.1 1.3 %collective-permute-start.5 = (bf16[16,2048]{1,0:T(8,128)(2,1)S(1)}, bf16[16,2048]{1,0:T(8,128)(2,1)S(1)}, u32[]{:S(2)}, u32[]{:S(2)}) collective-permute-start(bf16[16,2048]{1,0:T(8,128)(2,1)S(1)} %collective-permute-done.4.refs_6_.refs_2_.refs_3_), channel_id=1, source_target_pairs={{0,8},{8,0},{16,24},{24,16},{1,9},{9,1},{17,25},{25,17},{2,10},{10... | collective-permute-start | bytes 196616 | tf_op jit(solution)/shard_map/ppermute | solution.py:133
  9.8 7.2 %collective-permute-start.7 = (bf16[64,768]{1,0:T(8,128)(2,1)S(1)}, bf16[64,768]{1,0:T(8,128)(2,1)S(1)}, u32[]{:S(2)}, u32[]{:S(2)}) collective-permute-start(bf16[64,768]{1,0:T(8,128)(2,1)S(1)} %shard_map.98), channel_id=1, source_target_pairs={{0,1},{1,0},{2,3},{3,2},{4,5},{5,4},{6,7},{7,6},{8,9},{9,8},{10,11... | collective-permute-start | bytes 294920 | tf_op jit(solution)/shard_map/ppermute | solution.py:133
  12.6 8.2 %collective-permute-start.10 = (bf16[64,512]{1,0:T(8,128)(2,1)S(1)}, bf16[64,512]{1,0:T(8,128)(2,1)S(1)}, u32[]{:S(2)}, u32[]{:S(2)}) collective-permute-start(bf16[64,512]{1,0:T(8,128)(2,1)S(1)} %shard_map.105), channel_id=1, source_target_pairs={{0,1},{1,0},{2,3},{3,2},{4,5},{5,4},{6,7},{7,6},{8,9},{9,8},{10,11... | collective-permute-start | bytes 196616 | tf_op jit(solution)/shard_map/ppermute | solution.py:133
  13.6 7.3 %collective-permute-start.6 = (bf16[64,512]{1,0:T(8,128)(2,1)S(1)}, bf16[64,512]{1,0:T(8,128)(2,1)S(1)}, u32[]{:S(2)}, u32[]{:S(2)}) collective-permute-start(bf16[64,512]{1,0:T(8,128)(2,1)S(1)} %shard_map.95), channel_id=1, source_target_pairs={{0,1},{1,0},{2,3},{3,2},{4,5},{5,4},{6,7},{7,6},{8,9},{9,8},{10,11... | collective-permute-start | bytes 196616 | tf_op jit(solution)/shard_map/ppermute | solution.py:133
  17.1 9.4 %collective-permute-start.9 = (bf16[64,768]{1,0:T(8,128)(2,1)S(1)}, bf16[64,768]{1,0:T(8,128)(2,1)S(1)}, u32[]{:S(2)}, u32[]{:S(2)}) collective-permute-start(bf16[64,768]{1,0:T(8,128)(2,1)S(1)} %get-tuple-element.59), channel_id=1, source_target_pairs={{0,6},{1,7},{2,4},{3,5},{4,2},{5,3},{6,0},{7,1},{8,14},{9,15},{10,... | collective-permute-start | bytes 294920 | tf_op jit(solution)/shard_map/ppermute | solution.py:133
  20.8 7.7 %collective-permute-start.11 = (bf16[64,768]{1,0:T(8,128)(2,1)S(1)}, bf16[64,768]{1,0:T(8,128)(2,1)S(1)}, u32[]{:S(2)}, u32[]{:S(2)}) collective-permute-start(bf16[64,768]{1,0:T(8,128)(2,1)S(1)} %shard_map.106), channel_id=1, source_target_pairs={{0,4},{1,5},{2,6},{3,7},{4,0},{5,1},{6,2},{7,3},{8,12},{9,13},{10,... | collective-permute-start | bytes 294920 | tf_op jit(solution)/shard_map/ppermute | solution.py:133
  20.9 7.6 %collective-permute-start.12 = (bf16[64,768]{1,0:T(8,128)(2,1)S(1)}, bf16[64,768]{1,0:T(8,128)(2,1)S(1)}, u32[]{:S(2)}, u32[]{:S(2)}) collective-permute-start(bf16[64,768]{1,0:T(8,128)(2,1)S(1)} %shard_map.100), channel_id=1, source_target_pairs={{0,2},{1,3},{2,0},{3,1},{4,6},{5,7},{6,4},{7,5},{8,10},{9,11},{10,... | collective-permute-start | bytes 294920 | tf_op jit(solution)/shard_map/ppermute | solution.py:133
  22.2 4.3 %collective-permute-start.8 = (bf16[64,512]{1,0:T(8,128)(2,1)S(1)}, bf16[64,512]{1,0:T(8,128)(2,1)S(1)}, u32[]{:S(2)}, u32[]{:S(2)}) collective-permute-start(bf16[64,512]{1,0:T(8,128)(2,1)S(1)} %shard_map.103), channel_id=1, source_target_pairs={{0,1},{1,0},{2,3},{3,2},{4,5},{5,4},{6,7},{7,6},{8,9},{9,8},{10,11... | collective-permute-start | bytes 196616 | tf_op jit(solution)/shard_map/ppermute | solution.py:133
  29.6 5.1 %collective-permute-start.13 = (bf16[64,768]{1,0:T(8,128)(2,1)S(1)}, bf16[64,768]{1,0:T(8,128)(2,1)S(1)}, u32[]{:S(2)}, u32[]{:S(2)}) collective-permute-start(bf16[64,768]{1,0:T(8,128)(2,1)S(1)} %shard_map.107.refs_0_.refs_5_.refs_2_.refs_7_), channel_id=1, source_target_pairs={{0,2},{1,3},{2,0},{3,1},{4,6},{5,7},{6,4},{7,5},{8,10},{9,11},{10,... | collective-permute-start | bytes 294920 | tf_op jit(solution)/shard_map/ppermute | solution.py:133
  30.2 9.7 %collective-permute-start.16 = (bf16[64,768]{1,0:T(8,128)(2,1)S(1)}, bf16[64,768]{1,0:T(8,128)(2,1)S(1)}, u32[]{:S(2)}, u32[]{:S(2)}) collective-permute-start(bf16[64,768]{1,0:T(8,128)(2,1)S(1)} %shard_map.107.refs_0_.refs_5_.refs_2_.refs_7_), channel_id=1, source_target_pairs={{0,4},{1,5},{2,6},{3,7},{4,0},{5,1},{6,2},{7,3},{8,12},{9,13},{10,... | collective-permute-start | bytes 294920 | tf_op jit(solution)/shard_map/ppermute | solution.py:133
  32.8 7.2 %collective-permute-start.15 = (bf16[64,768]{1,0:T(8,128)(2,1)S(1)}, bf16[64,768]{1,0:T(8,128)(2,1)S(1)}, u32[]{:S(2)}, u32[]{:S(2)}) collective-permute-start(bf16[64,768]{1,0:T(8,128)(2,1)S(1)} %shard_map.107.refs_0_.refs_5_.refs_2_.refs_7_), channel_id=1, source_target_pairs={{0,6},{1,7},{2,4},{3,5},{4,2},{5,3},{6,0},{7,1},{8,14},{9,15},{10,... | collective-permute-start | bytes 294920 | tf_op jit(solution)/shard_map/ppermute | solution.py:133
  34.8 9.1 %collective-permute-start.14 = (bf16[64,1280]{1,0:T(8,128)(2,1)S(1)}, bf16[64,1280]{1,0:T(8,128)(2,1)S(1)}, u32[]{:S(2)}, u32[]{:S(2)}) collective-permute-start(bf16[64,1280]{1,0:T(8,128)(2,1)S(1)} %shard_map.108), channel_id=1, source_target_pairs={{0,1},{1,0},{2,3},{3,2},{4,5},{5,4},{6,7},{7,6},{8,9},{9,8},{10,11... | collective-permute-start | bytes 491528 | tf_op jit(solution)/shard_map/ppermute | solution.py:133
  40.0 5.4 %collective-permute-start.17 = (bf16[64,1280]{1,0:T(8,128)(2,1)S(1)}, bf16[64,1280]{1,0:T(8,128)(2,1)S(1)}, u32[]{:S(2)}, u32[]{:S(2)}) collective-permute-start(bf16[64,1280]{1,0:T(8,128)(2,1)S(1)} %shard_map.110), channel_id=1, source_target_pairs={{0,1},{1,0},{2,3},{3,2},{4,5},{5,4},{6,7},{7,6},{8,9},{9,8},{10,11... | collective-permute-start | bytes 491528 | tf_op jit(solution)/shard_map/ppermute | solution.py:133
  46.8 1.6 %collective-permute-start.18 = (bf16[64,2048]{1,0:T(8,128)(2,1)S(1)}, bf16[64,2048]{1,0:T(8,128)(2,1)S(1)}, u32[]{:S(2)}, u32[]{:S(2)}) collective-permute-start(bf16[64,2048]{1,0:T(8,128)(2,1)S(1)} %get-tuple-element.75), channel_id=1, source_target_pairs={{0,8},{8,0},{16,24},{24,16},{1,9},{9,1},{17,25},{25,17},{2,10},{10... | collective-permute-start | bytes 786440 | tf_op jit(solution)/shard_map/ppermute | solution.py:133
  48.5 5.9 %collective-permute-start.19 = (bf16[32,2048]{1,0:T(8,128)(2,1)S(1)}, bf16[32,2048]{1,0:T(8,128)(2,1)S(1)}, u32[]{:S(2)}, u32[]{:S(2)}) collective-permute-start(bf16[32,2048]{1,0:T(8,128)(2,1)S(1)} %get-tuple-element.77), channel_id=1, source_target_pairs={{0,16},{8,24},{16,0},{24,8},{1,17},{9,25},{17,1},{25,9},{2,18},{10... | collective-permute-start | bytes 393224 | tf_op jit(solution)/shard_map/ppermute | solution.py:133

commit v5 on v4

--- a/solution.py
+++ b/solution.py
@@ -403,8 +403,9 @@
 
     token_pieces, grad_pieces = spread(tokens), spread(grad_out)
     beside = [{0: v, 1: swap(v, "narrow", narrow, 1)} for v in (tokens, grad_out)]
-    far_blocks = list(range(wide - 1, 0, -2))
     near_blocks = list(range(wide - 2, -1, -2))
+    near_blocks[:2] = near_blocks[1::-1]
+    far_blocks = [b + 1 for b in near_blocks]
     wkv = call(
         load_kernel,
         [pltpu.with_memory_space_constraint(w, pltpu.HBM) for w in (w_keyval, w_query, w_output)],
@@ -524,7 +525,6 @@
         2 * rows * wide * full.shape[1],
     )
     width = 2 * cols
-    same = {0: own, **{d: swap(own, "wide", wide, d) for d in near_blocks[:-1]}}
     width = 2 * cols
     sum_shapes = [jax.ShapeDtypeStruct((rows, features), F32)] * 2
     grad_shapes = [jax.ShapeDtypeStruct(w.shape, BF) for w in (w_query, w_output)]
@@ -548,8 +548,8 @@
             {len(ins) - 2: 0, len(ins) - 1: 1} if before else {},
         )
 
-    same = {0: own, **{d: swap(own, "wide", wide, d) for d in near_blocks[:-1]}}
-    first, rest = near_blocks[-2], near_blocks[:-2]
+    same = {0: own, **{d: swap(own, "wide", wide, d) for d in range(wide - 2, 0, -2)}}
+    first, rest = 2, list(range(wide - 2, 2, -2))
     groups = ([0, first], rest)
     joined = []
     for group in groups:

time: 55.2 us -> 56.4 us (1.022)
  transfers between devices with their start and end apart: 20 -> 20, of which waited for: 9 -> 9; matrix products, arithmetic and copies ran while one was open for 0% -> 0% of each run, Pallas kernels for 35% -> 34%
where the time goes in v5:
time: 56.4 us; the launch traced here: 55.8 us
  Pallas kernels  22.8 us (40%)
  starting transfers between devices  19.8 us (35%)
  waiting for transfers between devices  12.3 us (22%)
  between operations  0.85 us (2%)
    pallas_call x25, Pallas kernels, call(): pl.pallas_call(kernel, out_shape=outs, in_specs=in_specs, out_specs=out_s...  22.8 us
    ppermute x20, starting transfers between devices, swap(): return lax.ppermute(value, axis, [(i, i ^ distance) for i in range(size)])  19.8 us
    ppermute x20, waiting for transfers between devices, swap(): return lax.ppermute(value, axis, [(i, i ^ distance) for i in range(size)])  12.3 us
  transfers between devices with their start and end apart: 20, of which 9 were waited for; matrix products, arithmetic and copies ran while one was open for 0% of the time, Pallas kernels for 34%

profile of v5, /device:TPU:0, one launch (start us, length us, event | category | flops | bytes accessed | tf_op | source)
XLA Modules:
  0.0 55.8 jit_solution(6091152458749232737)
XLA Ops:
  0.7 3.0 %collective-permute-start.1 = (bf16[16,2048]{1,0:T(8,128)(2,1)}, bf16[16,2048]{1,0:T(8,128)(2,1)S(1)}, u32[]{:S(2)}, u32[]{:S(2)}) collective-permute-start(bf16[16,2048]{1,0:T(8,128)(2,1)} %refs_0_.18), channel_id=1, source_target_pairs={{0,16},{8,24},{16,0},{24,8},{1,17},{9,25},{17,1},{25,9},{2,18},{10... | collective-permute-start | bytes 196616 | tf_op jit(solution)/shard_map/ppermute | solution.py:133
  3.7 0.1 collective-permute-start.4
  3.7 0.0 collective-permute-start
  3.7 1.2 %shard_map.92.refs_5_.refs_8_ = bf16[2048,256]{1,0:T(8,128)(2,1)S(1)} custom-call(bf16[2048,256]{1,0:T(8,128)(2,1)} %source.1, bf16[2048,2048]{1,0:T(8,128)(2,1)} %refs_6_.1, bf16[2048,2048]{1,0:T(8,128)(2,1)} %refs_7_.5), custom_call_target="tpu_custom_call" | custom-call | bytes 17825792 | tf_op jit(solution)/shard_map/pallas_call | solution.py:137
  5.0 0.0 copy-start
  5.0 1.3 %collective-permute-done.1.refs_2_ = bf16[16,2048]{1,0:T(8,128)(2,1)S(1)} collective-permute-done((bf16[16,2048]{1,0:T(8,128)(2,1)}, bf16[16,2048]{1,0:T(8,128)(2,1)S(1)}, u32[]{:S(2)}, u32[]{:S(2)}) %collective-permute-start.1) | collective-permute-done | bytes 65568 | tf_op jit(solution)/shard_map/ppermute | solution.py:133
  6.3 0.5 collective-permute-start.3
  6.8 1.4 %collective-permute-done.4.refs_6_.refs_2_.refs_3_ = bf16[16,2048]{1,0:T(8,128)(2,1)S(1)} collective-permute-done((bf16[16,2048]{1,0:T(8,128)(2,1)}, bf16[16,2048]{1,0:T(8,128)(2,1)S(1)}, u32[]{:S(2)}, u32[]{:S(2)}) %collective-permute-start.4) | collective-permute-done | bytes 65568 | tf_op jit(solution)/shard_map/ppermute | solution.py:133
  8.2 0.4 shard_map.97
  8.6 0.8 %collective-permute-done.5.refs_7_.refs_3_.refs_4_ = bf16[16,2048]{1,0:T(8,128)(2,1)S(1)} collective-permute-done((bf16[16,2048]{1,0:T(8,128)(2,1)S(1)}, bf16[16,2048]{1,0:T(8,128)(2,1)S(1)}, u32[]{:S(2)}, u32[]{:S(2)}) %collective-permute-start.5) | collective-permute-done | bytes 65568 | tf_op jit(solution)/shard_map/ppermute | solution.py:133
  9.4 0.4 shard_map.98
  9.8 1.6 %collective-permute-start.7 = (bf16[64,768]{1,0:T(8,128)(2,1)S(1)}, bf16[64,768]{1,0:T(8,128)(2,1)S(1)}, u32[]{:S(2)}, u32[]{:S(2)}) collective-permute-start(bf16[64,768]{1,0:T(8,128)(2,1)S(1)} %shard_map.98), channel_id=1, source_target_pairs={{0,1},{1,0},{2,3},{3,2},{4,5},{5,4},{6,7},{7,6},{8,9},{9,8},{10,11... | collective-permute-start | bytes 294920 | tf_op jit(solution)/shard_map/ppermute | solution.py:133
  11.4 0.7 %shard_map.94.refs_5_ = bf16[64,768]{1,0:T(8,128)(2,1)S(1)} custom-call(bf16[16,2048]{1,0:T(8,128)(2,1)S(1)} %copy-done.3, bf16[16,2048]{1,0:T(8,128)(2,1)S(1)} %collective-permute-done.refs_1_, bf16[16,2048]{1,0:T(8,128)(2,1)S(1)} %collective-permute-done.1.refs_2_, bf16[16,2048]{1,0:T(8,128)(2,1)S(1)} %collective-permute-done.2.refs_3_, ...), custom_call_target="tpu_custom_call" | custom-call | flops 201326592 | bytes 3145728 | tf_op jit(solution)/shard_map/pallas_call | solution.py:137
  12.1 0.5 shard_map.105
  12.6 0.6 %collective-permute-start.10 = (bf16[64,512]{1,0:T(8,128)(2,1)S(1)}, bf16[64,512]{1,0:T(8,128)(2,1)S(1)}, u32[]{:S(2)}, u32[]{:S(2)}) collective-permute-start(bf16[64,512]{1,0:T(8,128)(2,1)S(1)} %shard_map.105), channel_id=1, source_target_pairs={{0,1},{1,0},{2,3},{3,2},{4,5},{5,4},{6,7},{7,6},{8,9},{9,8},{10,11... | collective-permute-start | bytes 196616 | tf_op jit(solution)/shard_map/ppermute | solution.py:133
  13.1 0.4 shard_map.95
  13.6 1.6 %collective-permute-start.6 = (bf16[64,512]{1,0:T(8,128)(2,1)S(1)}, bf16[64,512]{1,0:T(8,128)(2,1)S(1)}, u32[]{:S(2)}, u32[]{:S(2)}) collective-permute-start(bf16[64,512]{1,0:T(8,128)(2,1)S(1)} %shard_map.95), channel_id=1, source_target_pairs={{0,1},{1,0},{2,3},{3,2},{4,5},{5,4},{6,7},{7,6},{8,9},{9,8},{10,11... | collective-permute-start | bytes 196616 | tf_op jit(solution)/shard_map/ppermute | solution.py:133
  15.2 0.6 %shard_map.104.near = bf16[64,512]{1,0:T(8,128)(2,1)S(1)} custom-call(bf16[16,2048]{1,0:T(8,128)(2,1)S(1)} %copy-done.3, bf16[16,2048]{1,0:T(8,128)(2,1)S(1)} %collective-permute-done.refs_1_, bf16[16,2048]{1,0:T(8,128)(2,1)S(1)} %collective-permute-done.1.refs_2_, bf16[16,2048]{1,0:T(8,128)(2,1)S(1)} %collective-permute-done.2.refs_3_, ...), custom_call_target="tpu_custom_call" | custom-call | flops 134217728 | bytes 2097152 | tf_op jit(solution)/shard_map/pallas_call | solution.py:137
  15.8 0.6 %shard_map.96.near = bf16[64,512]{1,0:T(8,128)(2,1)S(1)} custom-call(bf16[16,2048]{1,0:T(8,128)(2,1)S(1)} %copy-done.3, bf16[16,2048]{1,0:T(8,128)(2,1)S(1)} %collective-permute-done.refs_1_, bf16[16,2048]{1,0:T(8,128)(2,1)S(1)} %collective-permute-done.1.refs_2_, bf16[16,2048]{1,0:T(8,128)(2,1)S(1)} %collective-permute-done.2.refs_3_, ...), custom_call_target="tpu_custom_call" | custom-call | flops 134217728 | bytes 2097152 | tf_op jit(solution)/shard_map/pallas_call | solution.py:137
  16.4 0.6 %shard_map.93.near = bf16[64,512]{1,0:T(8,128)(2,1)S(1)} custom-call(bf16[16,2048]{1,0:T(8,128)(2,1)S(1)} %copy-done.3, bf16[16,2048]{1,0:T(8,128)(2,1)S(1)} %collective-permute-done.refs_1_, bf16[16,2048]{1,0:T(8,128)(2,1)S(1)} %collective-permute-done.1.refs_2_, bf16[16,2048]{1,0:T(8,128)(2,1)S(1)} %collective-permute-done.2.refs_3_, ...), custom_call_target="tpu_custom_call" | custom-call | flops 134217728 | bytes 2097152 | tf_op jit(solution)/shard_map/pallas_call | solution.py:137
  17.1 2.7 %collective-permute-start.9 = (bf16[64,768]{1,0:T(8,128)(2,1)S(1)}, bf16[64,768]{1,0:T(8,128)(2,1)S(1)}, u32[]{:S(2)}, u32[]{:S(2)}) collective-permute-start(bf16[64,768]{1,0:T(8,128)(2,1)S(1)} %get-tuple-element.59), channel_id=1, source_target_pairs={{0,4},{1,5},{2,6},{3,7},{4,0},{5,1},{6,2},{7,3},{8,12},{9,13},{10,... | collective-permute-start | bytes 294920 | tf_op jit(solution)/shard_map/ppermute | solution.py:133
  19.8 1.4 %collective-permute-start.11 = (bf16[64,768]{1,0:T(8,128)(2,1)S(1)}, bf16[64,768]{1,0:T(8,128)(2,1)S(1)}, u32[]{:S(2)}, u32[]{:S(2)}) collective-permute-start(bf16[64,768]{1,0:T(8,128)(2,1)S(1)} %shard_map.106), channel_id=1, source_target_pairs={{0,6},{1,7},{2,4},{3,5},{4,2},{5,3},{6,0},{7,1},{8,14},{9,15},{10,... | collective-permute-start | bytes 294920 | tf_op jit(solution)/shard_map/ppermute | solution.py:133
  21.2 0.3 collective-permute-start.12
  21.5 0.4 shard_map.103
  22.0 0.5 collective-permute-start.8
  22.5 0.2 shard_map.102.refs_0_
  22.7 0.6 %shard_map.101.near = bf16[64,512]{1,0:T(8,128)(2,1)S(1)} custom-call(bf16[16,2048]{1,0:T(8,128)(2,1)S(1)} %copy-done.3, bf16[16,2048]{1,0:T(8,128)(2,1)S(1)} %collective-permute-done.refs_1_, bf16[16,2048]{1,0:T(8,128)(2,1)S(1)} %collective-permute-done.1.refs_2_, bf16[16,2048]{1,0:T(8,128)(2,1)S(1)} %collective-permute-done.2.refs_3_, ...), custom_call_target="tpu_custom_call" | custom-call | flops 134217728 | bytes 2097152 | tf_op jit(solution)/shard_map/pallas_call | solution.py:137
  23.4 2.9 %collective-permute-done.8.far = bf16[64,512]{1,0:T(8,128)(2,1)S(1)} collective-permute-done((bf16[64,512]{1,0:T(8,128)(2,1)S(1)}, bf16[64,512]{1,0:T(8,128)(2,1)S(1)}, u32[]{:S(2)}, u32[]{:S(2)}) %collective-permute-start.8) | collective-permute-done | bytes 65568 | tf_op jit(solution)/shard_map/ppermute | solution.py:133
  26.3 0.7 %collective-permute-done.9.refs_0_ = bf16[64,768]{1,0:T(8,128)(2,1)S(1)} collective-permute-done((bf16[64,768]{1,0:T(8,128)(2,1)S(1)}, bf16[64,768]{1,0:T(8,128)(2,1)S(1)}, u32[]{:S(2)}, u32[]{:S(2)}) %collective-permute-start.9) | collective-permute-done | bytes 98336 | tf_op jit(solution)/shard_map/ppermute | solution.py:133
  27.0 0.5 collective-permute-done.12.refs_2_
  27.5 1.1 %shard_map.107.refs_0_.refs_5_.refs_2_.refs_7_ = bf16[64,768]{1,0:T(8,128)(2,1)S(1)} custom-call(bf16[64,512]{1,0:T(8,128)(2,1)S(1)} %shard_map.101.near, bf16[64,512]{1,0:T(8,128)(2,1)S(1)} %collective-permute-done.8.far, bf16[64,256]{1,0:T(8,128)(2,1)S(1)} %get-tuple-element.49.pair, bf16[64,768]{1,0:T(8,128)(2,1)S(1)} %collective-permute-done.9.refs_0_, ...), custom_call_target="tpu_custom_call" | custom-call | flops 25165824 | bytes 786432 | tf_op jit(solution)/shard_map/pallas_call | solution.py:137
  28.6 1.7 %collective-permute-start.13 = (bf16[64,768]{1,0:T(8,128)(2,1)S(1)}, bf16[64,768]{1,0:T(8,128)(2,1)S(1)}, u32[]{:S(2)}, u32[]{:S(2)}) collective-permute-start(bf16[64,768]{1,0:T(8,128)(2,1)S(1)} %shard_map.107.refs_0_.refs_5_.refs_2_.refs_7_), channel_id=1, source_target_pairs={{0,2},{1,3},{2,0},{3,1},{4,6},{5,7},{6,4},{7,5},{8,10},{9,11},{10,... | collective-permute-start | bytes 294920 | tf_op jit(solution)/shard_map/ppermute | solution.py:133
  30.2 2.3 %collective-permute-start.16 = (bf16[64,768]{1,0:T(8,128)(2,1)S(1)}, bf16[64,768]{1,0:T(8,128)(2,1)S(1)}, u32[]{:S(2)}, u32[]{:S(2)}) collective-permute-start(bf16[64,768]{1,0:T(8,128)(2,1)S(1)} %shard_map.107.refs_0_.refs_5_.refs_2_.refs_7_), channel_id=1, source_target_pairs={{0,4},{1,5},{2,6},{3,7},{4,0},{5,1},{6,2},{7,3},{8,12},{9,13},{10,... | collective-permute-start | bytes 294920 | tf_op jit(solution)/shard_map/ppermute | solution.py:133
  32.6 1.1 %collective-permute-start.15 = (bf16[64,768]{1,0:T(8,128)(2,1)S(1)}, bf16[64,768]{1,0:T(8,128)(2,1)S(1)}, u32[]{:S(2)}, u32[]{:S(2)}) collective-permute-start(bf16[64,768]{1,0:T(8,128)(2,1)S(1)} %shard_map.107.refs_0_.refs_5_.refs_2_.refs_7_), channel_id=1, source_target_pairs={{0,6},{1,7},{2,4},{3,5},{4,2},{5,3},{6,0},{7,1},{8,14},{9,15},{10,... | collective-permute-start | bytes 294920 | tf_op jit(solution)/shard_map/ppermute | solution.py:133
  33.7 0.5 collective-permute-start.14
  34.2 3.6 %shard_map.109 = (bf16[2048,2048]{1,0:T(8,128)(2,1)}, bf16[2048,2048]{1,0:T(8,128)(2,1)}, f32[64,2048]{1,0:T(8,128)S(1)}, f32[64,2048]{1,0:T(8,128)S(1)}) custom-call(bf16[2048,64]{1,0:T(8,128)(2,1)S(1)} %shard_map.102.refs_0_, bf16[16,2048]{1,0:T(8,128)(2,1)S(1)} %copy-done.2, bf16[16,2048]{1,0:T(8,128)(2,1)S(1)} %collective-permute-done.3.refs_5_.refs_1_.refs_2_, ...), custom_call_target="tpu_custom_call" | custom-call | flops 536870912 | bytes 8388608 | tf_op jit(solution)/shard_map/pallas_call | solution.py:137
  37.8 2.8 %collective-permute-done.15.refs_0_.refs_5_.refs_3_.refs_8_ = bf16[64,768]{1,0:T(8,128)(2,1)S(1)} collective-permute-done((bf16[64,768]{1,0:T(8,128)(2,1)S(1)}, bf16[64,768]{1,0:T(8,128)(2,1)S(1)}, u32[]{:S(2)}, u32[]{:S(2)}) %collective-permute-start.15) | collective-permute-done | bytes 98336 | tf_op jit(solution)/shard_map/ppermute | solution.py:133
  40.7 0.5 collective-permute-start.17
  41.2 3.2 %shard_map.111 = (bf16[2048,2048]{1,0:T(8,128)(2,1)}, bf16[2048,2048]{1,0:T(8,128)(2,1)}, f32[64,2048]{1,0:T(8,128)S(1)}, f32[64,2048]{1,0:T(8,128)S(1)}) custom-call(bf16[2048,64]{1,0:T(8,128)(2,1)S(1)} %shard_map.102.refs_0_, bf16[16,2048]{1,0:T(8,128)(2,1)S(1)} %copy-done.2, ...), custom_call_target="tpu_custom_call", output_to_operand_aliasing={{0}: (11, {}), {1}: (12, {})} | custom-call | flops 536870912 | bytes 8388608 | tf_op jit(solution)/shard_map/pallas_call | solution.py:137
  44.4 1.1 %shard_map.112 = (f32[64,2048]{1,0:T(8,128)S(1)}, f32[64,2048]{1,0:T(8,128)S(1)}) custom-call(bf16[64,1280]{1,0:T(8,128)(2,1)S(1)} %collective-permute-done.14.refs_0_.refs_5_, bf16[2048,2048]{1,0:T(8,128)(2,1)S(1)} %copy-done.1, bf16[2048,2048]{1,0:T(8,128)(2,1)S(1)} %copy-done, f32[64,2048]{1,0:T(8,128)S(1)} %get-tuple-element.70.refs_3_, ...), custom_call_target="tpu_custom_call" | custom-call | flops 268435456 | bytes 4194304 | tf_op jit(solution)/shard_map/pallas_call | solution.py:137
  45.6 0.5 collective-permute-done.17.refs_1_.refs_6_
  46.0 1.4 %shard_map.113 = (bf16[64,2048]{1,0:T(8,128)(2,1)S(1)}, bf16[64,2048]{1,0:T(8,128)(2,1)S(1)}) custom-call(bf16[64,1280]{1,0:T(8,128)(2,1)S(1)} %collective-permute-done.14.refs_0_.refs_5_, bf16[64,1280]{1,0:T(8,128)(2,1)S(1)} %collective-permute-done.17.refs_1_.refs_6_, bf16[64,768]{1,0:T(8,128)(2,1)S(1)} %shard_map.107.refs_0_.refs_5_.refs_2_.refs_7_, ...), custom_call_target="tpu_custom_call" | custom-call | flops 570425344 | bytes 8912896 | tf_op jit(solution)/shard_map/pallas_call | solution.py:137
  47.5 0.1 collective-permute-start.18
  47.6 1.5 %collective-permute-done.18.far = bf16[64,2048]{1,0:T(8,128)(2,1)S(1)} collective-permute-done((bf16[64,2048]{1,0:T(8,128)(2,1)S(1)}, bf16[64,2048]{1,0:T(8,128)(2,1)S(1)}, u32[]{:S(2)}, u32[]{:S(2)}) %collective-permute-start.18) | collective-permute-done | bytes 262176 | tf_op jit(solution)/shard_map/ppermute | solution.py:133
  49.1 0.1 shard_map.114
  49.2 1.4 %collective-permute-start.19 = (bf16[32,2048]{1,0:T(8,128)(2,1)S(1)}, bf16[32,2048]{1,0:T(8,128)(2,1)S(1)}, u32[]{:S(2)}, u32[]{:S(2)}) collective-permute-start(bf16[32,2048]{1,0:T(8,128)(2,1)S(1)} %get-tuple-element.77), channel_id=1, source_target_pairs={{0,16},{8,24},{16,0},{24,8},{1,17},{9,25},{17,1},{25,9},{2,18},{10... | collective-permute-start | bytes 393224 | tf_op jit(solution)/shard_map/ppermute | solution.py:133
  50.5 4.6 %shard_map.116 = (bf16[2048,2048]{1,0:T(8,128)(2,1)}, bf16[2048,2048]{1,0:T(8,128)(2,1)}, bf16[2048,256]{1,0:T(8,128)(2,1)}) custom-call(bf16[2048,64]{1,0:T(8,128)(2,1)S(1)} %shard_map.102.refs_0_, bf16[16,2048]{1,0:T(8,128)(2,1)S(1)} %copy-done.2, ...), custom_call_target="tpu_custom_call", output_to_operand_aliasing={{0}: (11, {}), {1}: (12, {})} | custom-call | flops 1073741824 | bytes 16777216 | tf_op jit(solution)/shard_map/pallas_call | solution.py:137
  55.1 0.7 %shard_map.115 = (bf16[16,2048]{1,0:T(8,128)(2,1)}, bf16[16,2048]{1,0:T(8,128)(2,1)}) custom-call(bf16[32,2048]{1,0:T(8,128)(2,1)S(1)} %get-tuple-element.76.refs_0_, bf16[32,2048]{1,0:T(8,128)(2,1)S(1)} %collective-permute-done.19.refs_1_), custom_call_target="tpu_custom_call" | custom-call | flops 262144 | bytes 524288 | tf_op jit(solution)/shard_map/pallas_call | solution.py:137
  (25 shorter events, 0.2 us)
Async XLA Ops:
  0.6 7.5 %copy-start.3 = (bf16[16,2048]{1,0:T(8,128)(2,1)S(1)}, bf16[16,2048]{1,0:T(8,128)(2,1)}, u32[]{:S(2)}) copy-start(bf16[16,2048]{1,0:T(8,128)(2,1)} %refs_0_.18) | copy-start | bytes 196612
  0.6 5.6 %copy-start.2 = (bf16[16,2048]{1,0:T(8,128)(2,1)S(1)}, bf16[16,2048]{1,0:T(8,128)(2,1)}, u32[]{:S(2)}) copy-start(bf16[16,2048]{1,0:T(8,128)(2,1)} %refs_1_.7) | copy-start | bytes 196612
  0.7 7.5 %copy-start.1 = (bf16[2048,2048]{1,0:T(8,128)(2,1)S(1)}, bf16[2048,2048]{1,0:T(8,128)(2,1)}, u32[]{:S(2)}) copy-start(bf16[2048,2048]{1,0:T(8,128)(2,1)} %refs_6_.1) | copy-start | bytes 25165828
  0.7 5.6 %collective-permute-start.1 = (bf16[16,2048]{1,0:T(8,128)(2,1)}, bf16[16,2048]{1,0:T(8,128)(2,1)S(1)}, u32[]{:S(2)}, u32[]{:S(2)}) collective-permute-start(bf16[16,2048]{1,0:T(8,128)(2,1)} %refs_0_.18), channel_id=1, source_target_pairs={{0,16},{8,24},{16,0},{24,8},{1,17},{9,25},{17,1},{25,9},{2,18},{10... | collective-permute-start | bytes 196616 | tf_op jit(solution)/shard_map/ppermute | solution.py:133
  3.7 4.5 %collective-permute-start.4 = (bf16[16,2048]{1,0:T(8,128)(2,1)}, bf16[16,2048]{1,0:T(8,128)(2,1)S(1)}, u32[]{:S(2)}, u32[]{:S(2)}) collective-permute-start(bf16[16,2048]{1,0:T(8,128)(2,1)} %refs_1_.7), channel_id=1, source_target_pairs={{0,16},{8,24},{16,0},{24,8},{1,17},{9,25},{17,1},{25,9},{2,18},{10... | collective-permute-start | bytes 196616 | tf_op jit(solution)/shard_map/ppermute | solution.py:133
  3.7 4.4 %collective-permute-start = (bf16[16,2048]{1,0:T(8,128)(2,1)}, bf16[16,2048]{1,0:T(8,128)(2,1)S(1)}, u32[]{:S(2)}, u32[]{:S(2)}) collective-permute-start(bf16[16,2048]{1,0:T(8,128)(2,1)} %refs_0_.18), channel_id=1, source_target_pairs={{0,8},{8,0},{16,24},{24,16},{1,9},{9,1},{17,25},{25,17},{2,10},{10... | collective-permute-start | bytes 196616 | tf_op jit(solution)/shard_map/ppermute | solution.py:133
  5.0 4.4 %copy-start = (bf16[2048,2048]{1,0:T(8,128)(2,1)S(1)}, bf16[2048,2048]{1,0:T(8,128)(2,1)}, u32[]{:S(2)}) copy-start(bf16[2048,2048]{1,0:T(8,128)(2,1)} %refs_7_.5) | copy-start | bytes 25165828
  6.3 1.9 %collective-permute-start.2 = (bf16[16,2048]{1,0:T(8,128)(2,1)S(1)}, bf16[16,2048]{1,0:T(8,128)(2,1)S(1)}, u32[]{:S(2)}, u32[]{:S(2)}) collective-permute-start(bf16[16,2048]{1,0:T(8,128)(2,1)S(1)} %collective-permute-done.1.refs_2_), channel_id=1, source_target_pairs={{0,8},{8,0},{16,24},{24,16},{1,9},{9,1},{17,25},{25,17},{2,10},{10... | collective-permute-start | bytes 196616 | tf_op jit(solution)/shard_map/ppermute | solution.py:133
  6.3 2.4 %collective-permute-start.3 = (bf16[16,2048]{1,0:T(8,128)(2,1)S(1)}, bf16[16,2048]{1,0:T(8,128)(2,1)S(1)}, u32[]{:S(2)}, u32[]{:S(2)}) collective-permute-start(bf16[16,2048]{1,0:T(8,128)(2,1)S(1)} %copy-done.2), channel_id=1, source_target_pairs={{0,8},{8,0},{16,24},{24,16},{1,9},{9,1},{17,25},{25,17},{2,10},{10... | collective-permute-start | bytes 196616 | tf_op jit(solution)/shard_map/ppermute | solution.py:133
  8.1 1.3 %collective-permute-start.5 = (bf16[16,2048]{1,0:T(8,128)(2,1)S(1)}, bf16[16,2048]{1,0:T(8,128)(2,1)S(1)}, u32[]{:S(2)}, u32[]{:S(2)}) collective-permute-start(bf16[16,2048]{1,0:T(8,128)(2,1)S(1)} %collective-permute-done.4.refs_6_.refs_2_.refs_3_), channel_id=1, source_target_pairs={{0,8},{8,0},{16,24},{24,16},{1,9},{9,1},{17,25},{25,17},{2,10},{10... | collective-permute-start | bytes 196616 | tf_op jit(solution)/shard_map/ppermute | solution.py:133
  9.8 7.2 %collective-permute-start.7 = (bf16[64,768]{1,0:T(8,128)(2,1)S(1)}, bf16[64,768]{1,0:T(8,128)(2,1)S(1)}, u32[]{:S(2)}, u32[]{:S(2)}) collective-permute-start(bf16[64,768]{1,0:T(8,128)(2,1)S(1)} %shard_map.98), channel_id=1, source_target_pairs={{0,1},{1,0},{2,3},{3,2},{4,5},{5,4},{6,7},{7,6},{8,9},{9,8},{10,11... | collective-permute-start | bytes 294920 | tf_op jit(solution)/shard_map/ppermute | solution.py:133
  12.6 7.2 %collective-permute-start.10 = (bf16[64,512]{1,0:T(8,128)(2,1)S(1)}, bf16[64,512]{1,0:T(8,128)(2,1)S(1)}, u32[]{:S(2)}, u32[]{:S(2)}) collective-permute-start(bf16[64,512]{1,0:T(8,128)(2,1)S(1)} %shard_map.105), channel_id=1, source_target_pairs={{0,1},{1,0},{2,3},{3,2},{4,5},{5,4},{6,7},{7,6},{8,9},{9,8},{10,11... | collective-permute-start | bytes 196616 | tf_op jit(solution)/shard_map/ppermute | solution.py:133
  13.6 7.6 %collective-permute-start.6 = (bf16[64,512]{1,0:T(8,128)(2,1)S(1)}, bf16[64,512]{1,0:T(8,128)(2,1)S(1)}, u32[]{:S(2)}, u32[]{:S(2)}) collective-permute-start(bf16[64,512]{1,0:T(8,128)(2,1)S(1)} %shard_map.95), channel_id=1, source_target_pairs={{0,1},{1,0},{2,3},{3,2},{4,5},{5,4},{6,7},{7,6},{8,9},{9,8},{10,11... | collective-permute-start | bytes 196616 | tf_op jit(solution)/shard_map/ppermute | solution.py:133
  17.1 9.9 %collective-permute-start.9 = (bf16[64,768]{1,0:T(8,128)(2,1)S(1)}, bf16[64,768]{1,0:T(8,128)(2,1)S(1)}, u32[]{:S(2)}, u32[]{:S(2)}) collective-permute-start(bf16[64,768]{1,0:T(8,128)(2,1)S(1)} %get-tuple-element.59), channel_id=1, source_target_pairs={{0,4},{1,5},{2,6},{3,7},{4,0},{5,1},{6,2},{7,3},{8,12},{9,13},{10,... | collective-permute-start | bytes 294920 | tf_op jit(solution)/shard_map/ppermute | solution.py:133
  19.8 7.2 %collective-permute-start.11 = (bf16[64,768]{1,0:T(8,128)(2,1)S(1)}, bf16[64,768]{1,0:T(8,128)(2,1)S(1)}, u32[]{:S(2)}, u32[]{:S(2)}) collective-permute-start(bf16[64,768]{1,0:T(8,128)(2,1)S(1)} %shard_map.106), channel_id=1, source_target_pairs={{0,6},{1,7},{2,4},{3,5},{4,2},{5,3},{6,0},{7,1},{8,14},{9,15},{10,... | collective-permute-start | bytes 294920 | tf_op jit(solution)/shard_map/ppermute | solution.py:133
  21.2 6.3 %collective-permute-start.12 = (bf16[64,768]{1,0:T(8,128)(2,1)S(1)}, bf16[64,768]{1,0:T(8,128)(2,1)S(1)}, u32[]{:S(2)}, u32[]{:S(2)}) collective-permute-start(bf16[64,768]{1,0:T(8,128)(2,1)S(1)} %shard_map.100), channel_id=1, source_target_pairs={{0,2},{1,3},{2,0},{3,1},{4,6},{5,7},{6,4},{7,5},{8,10},{9,11},{10,... | collective-permute-start | bytes 294920 | tf_op jit(solution)/shard_map/ppermute | solution.py:133
  22.0 4.3 %collective-permute-start.8 = (bf16[64,512]{1,0:T(8,128)(2,1)S(1)}, bf16[64,512]{1,0:T(8,128)(2,1)S(1)}, u32[]{:S(2)}, u32[]{:S(2)}) collective-permute-start(bf16[64,512]{1,0:T(8,128)(2,1)S(1)} %shard_map.103), channel_id=1, source_target_pairs={{0,1},{1,0},{2,3},{3,2},{4,5},{5,4},{6,7},{7,6},{8,9},{9,8},{10,11... | collective-permute-start | bytes 196616 | tf_op jit(solution)/shard_map/ppermute | solution.py:133
  28.6 5.0 %collective-permute-start.13 = (bf16[64,768]{1,0:T(8,128)(2,1)S(1)}, bf16[64,768]{1,0:T(8,128)(2,1)S(1)}, u32[]{:S(2)}, u32[]{:S(2)}) collective-permute-start(bf16[64,768]{1,0:T(8,128)(2,1)S(1)} %shard_map.107.refs_0_.refs_5_.refs_2_.refs_7_), channel_id=1, source_target_pairs={{0,2},{1,3},{2,0},{3,1},{4,6},{5,7},{6,4},{7,5},{8,10},{9,11},{10,... | collective-permute-start | bytes 294920 | tf_op jit(solution)/shard_map/ppermute | solution.py:133
  30.2 7.6 %collective-permute-start.16 = (bf16[64,768]{1,0:T(8,128)(2,1)S(1)}, bf16[64,768]{1,0:T(8,128)(2,1)S(1)}, u32[]{:S(2)}, u32[]{:S(2)}) collective-permute-start(bf16[64,768]{1,0:T(8,128)(2,1)S(1)} %shard_map.107.refs_0_.refs_5_.refs_2_.refs_7_), channel_id=1, source_target_pairs={{0,4},{1,5},{2,6},{3,7},{4,0},{5,1},{6,2},{7,3},{8,12},{9,13},{10,... | collective-permute-start | bytes 294920 | tf_op jit(solution)/shard_map/ppermute | solution.py:133
  32.6 8.1 %collective-permute-start.15 = (bf16[64,768]{1,0:T(8,128)(2,1)S(1)}, bf16[64,768]{1,0:T(8,128)(2,1)S(1)}, u32[]{:S(2)}, u32[]{:S(2)}) collective-permute-start(bf16[64,768]{1,0:T(8,128)(2,1)S(1)} %shard_map.107.refs_0_.refs_5_.refs_2_.refs_7_), channel_id=1, source_target_pairs={{0,6},{1,7},{2,4},{3,5},{4,2},{5,3},{6,0},{7,1},{8,14},{9,15},{10,... | collective-permute-start | bytes 294920 | tf_op jit(solution)/shard_map/ppermute | solution.py:133
  33.7 10.8 %collective-permute-start.14 = (bf16[64,1280]{1,0:T(8,128)(2,1)S(1)}, bf16[64,1280]{1,0:T(8,128)(2,1)S(1)}, u32[]{:S(2)}, u32[]{:S(2)}) collective-permute-start(bf16[64,1280]{1,0:T(8,128)(2,1)S(1)} %shard_map.108), channel_id=1, source_target_pairs={{0,1},{1,0},{2,3},{3,2},{4,5},{5,4},{6,7},{7,6},{8,9},{9,8},{10,11... | collective-permute-start | bytes 491528 | tf_op jit(solution)/shard_map/ppermute | solution.py:133
  40.7 5.4 %collective-permute-start.17 = (bf16[64,1280]{1,0:T(8,128)(2,1)S(1)}, bf16[64,1280]{1,0:T(8,128)(2,1)S(1)}, u32[]{:S(2)}, u32[]{:S(2)}) collective-permute-start(bf16[64,1280]{1,0:T(8,128)(2,1)S(1)} %shard_map.110), channel_id=1, source_target_pairs={{0,1},{1,0},{2,3},{3,2},{4,5},{5,4},{6,7},{7,6},{8,9},{9,8},{10,11... | collective-permute-start | bytes 491528 | tf_op jit(solution)/shard_map/ppermute | solution.py:133
  47.5 1.6 %collective-permute-start.18 = (bf16[64,2048]{1,0:T(8,128)(2,1)S(1)}, bf16[64,2048]{1,0:T(8,128)(2,1)S(1)}, u32[]{:S(2)}, u32[]{:S(2)}) collective-permute-start(bf16[64,2048]{1,0:T(8,128)(2,1)S(1)} %get-tuple-element.75), channel_id=1, source_target_pairs={{0,8},{8,0},{16,24},{24,16},{1,9},{9,1},{17,25},{25,17},{2,10},{10... | collective-permute-start | bytes 786440 | tf_op jit(solution)/shard_map/ppermute | solution.py:133
  49.2 6.0 %collective-permute-start.19 = (bf16[32,2048]{1,0:T(8,128)(2,1)S(1)}, bf16[32,2048]{1,0:T(8,128)(2,1)S(1)}, u32[]{:S(2)}, u32[]{:S(2)}) collective-permute-start(bf16[32,2048]{1,0:T(8,128)(2,1)S(1)} %get-tuple-element.77), channel_id=1, source_target_pairs={{0,16},{8,24},{16,0},{24,8},{1,17},{9,25},{17,1},{25,9},{2,18},{10... | collective-permute-start | bytes 393224 | tf_op jit(solution)/shard_map/ppermute | solution.py:133

commit v6 on v4

--- a/solution.py
+++ b/solution.py
@@ -331,24 +331,32 @@
     tile = 256
     for at, (part, left, b) in enumerate(blocks):
         att = parts[part][:, left : left + cols].T
-        for first in range(0, gwo.shape[1], tile):
-            span = slice(first, first + tile)
-            gwo_v[at, :, span] = jnp.dot(att, grad_panel[:, span], preferred_element_type=F32).astype(BF)
-        send(gwo_v.at[at], gwo.at[block_of(b, cols), :])
+        half = cols // 2
+        for top in (0, half):
+            for first in range(0, gwo.shape[1], tile):
+                span = slice(first, first + tile)
+                gwo_v[at, top : top + half, span] = jnp.dot(
+                    att[top : top + half, :], grad_panel[:, span], preferred_element_type=F32
+                ).astype(BF)
+            me = lax.axis_index("wide") ^ b
+            rows = pl.ds(pl.multiple_of(me * cols + top, half), half)
+            send(gwo_v.at[at, pl.ds(top, half), :], gwo.at[rows, :])
         grad = parts[part][:, left + cols : left + 2 * cols]
-        for first in range(0, gwq.shape[0], tile):
-            span = slice(first, first + tile)
-            gwq_v[at, span, :] = jnp.dot(turned[span, :], grad, preferred_element_type=F32).astype(BF)
-        send(gwq_v.at[at], gwq.at[:, block_of(b, cols)])
+        half = gwq.shape[0] // 2
+        for top in (0, half):
+            for first in range(top, top + half, tile):
+                span = slice(first, first + tile)
+                gwq_v[at, span, :] = jnp.dot(turned[span, :], grad, preferred_element_type=F32).astype(BF)
+            send(gwq_v.at[at, pl.ds(top, half), :], gwq.at[pl.ds(top, half), block_of(b, cols)])
     return copies
 
 
-def block_kernel(blocks, cols, narrow, count, has_before, *refs):
+def block_kernel(blocks, written, cols, narrow, count, has_before, *refs):
     turned, grads, parts, refs = refs[0], refs[1 : 1 + narrow], refs[1 + narrow : 1 + narrow + count], refs[1 + narrow + count :]
     wq, wo = refs[:2]
     before, outs = (refs[2:4], refs[6:]) if has_before else ((), refs[2:])
     gwq, gwo, out_sum, grad_sum, gwq_v, gwo_v, sems = outs
-    copies = send_weight_grads(blocks, cols, turned, grads, parts, gwq, gwo, gwq_v, gwo_v, sems)
+    copies = send_weight_grads(blocks + written, cols, turned, grads, parts, gwq, gwo, gwq_v, gwo_v, sems)
     accumulate(blocks, cols, parts, wq, wo, before, out_sum, grad_sum)
     for copy in copies:
         copy.wait()
@@ -357,10 +365,10 @@
 def weight_grad_kernel(blocks, cols, narrow, count, *refs):
     turned, grads, parts = refs[0], refs[1 : 1 + narrow], refs[1 + narrow : 1 + narrow + count]
     gwq, gwo, gwkv, gwkv_v, gwq_v, gwo_v, sems = refs[3 + narrow + count :]
+    copies = send_weight_grads(blocks, cols, turned, grads, parts, gwq, gwo, gwq_v, gwo_v, sems)
     gwkv_v[...] = jnp.dot(turned[...], kv_total(parts), preferred_element_type=F32).astype(BF)
-    last = pltpu.make_async_copy(gwkv_v, gwkv, sems.at[2 * len(blocks)])
+    last = pltpu.make_async_copy(gwkv_v, gwkv, sems.at[len(copies)])
     last.start()
-    copies = send_weight_grads(blocks, cols, turned, grads, parts, gwq, gwo, gwq_v, gwo_v, sems)
     for copy in copies + [last]:
         copy.wait()
 
@@ -524,24 +532,23 @@
         2 * rows * wide * full.shape[1],
     )
     width = 2 * cols
-    same = {0: own, **{d: swap(own, "wide", wide, d) for d in near_blocks[:-1]}}
-    width = 2 * cols
     sum_shapes = [jax.ShapeDtypeStruct((rows, features), F32)] * 2
     grad_shapes = [jax.ShapeDtypeStruct(w.shape, BF) for w in (w_query, w_output)]
 
     def grad_scratch(blocks):
         return [pltpu.VMEM((len(blocks), features, cols), BF), pltpu.VMEM((len(blocks), cols, features), BF), sems]
 
-    def block_terms(distances, before=()):
+    def block_terms(distances, before=(), more=(), written=()):
         blocks = [(i, 0, d) for i, d in enumerate(distances)]
-        ins = (turned, *grad_pieces, *[same[d] for d in distances], w_query, w_output, *before)
+        parts = [*[same[d] for d in distances], *more]
+        ins = (turned, *grad_pieces, *parts, w_query, w_output, *before)
         return call(
-            functools.partial(block_kernel, blocks, cols, narrow, len(blocks), bool(before)),
+            functools.partial(block_kernel, blocks, list(written), cols, narrow, len(parts), bool(before)),
             ins,
-            [VMEM] * (3 + narrow + len(blocks)) + ([VMEM] * 2 + [ANY] * 2 if before else []),
+            [VMEM] * (3 + narrow + len(parts)) + ([VMEM] * 2 + [ANY] * 2 if before else []),
             grad_shapes + sum_shapes,
             [ANY] * 2 + [VMEM] * 2,
-            grad_scratch(blocks),
+            grad_scratch([*blocks, *written]),
             20 * MIB,
             8 * rows * features * cols * len(blocks),
             8 * features * cols * len(blocks),
@@ -568,8 +575,9 @@
             4 * rows * full.shape[1] * len(group),
         )
         joined.append(swap(together, "wide", wide, 1))
-    *grads, out_sum, grad_sum = block_terms(rest, (out_sum, grad_sum, *grads))
     blocks = [[(i, width * at, d + 1) for at, d in enumerate(group)] for i, group in enumerate(groups)]
+    written = [(len(rest), *blocks[0][0][1:])]
+    *grads, out_sum, grad_sum = block_terms(rest, (out_sum, grad_sum, *grads), [joined[0]], written)
     out_sum, grad_sum = call(
         functools.partial(back_kernel, blocks[0], cols, 1),
         (joined[0], w_query, w_output, out_sum, grad_sum),
@@ -608,7 +616,7 @@
         12 * rows * features,
     )
     sums = [sums[0]] + [swap(sums[i], "narrow", narrow, 2 * i) for i in range(1, narrow // 2)]
-    blocks = blocks[0] + blocks[1]
+    blocks = blocks[0][1:] + blocks[1]
     ins = (turned, *grad_pieces, *parts, *grads)
     grad_wq, grad_wo, grad_wkv = call(
         functools.partial(weight_grad_kernel, blocks, cols, narrow, len(parts)),

time: 55.2 us -> 54.9 us (level)
  Pallas kernels: 22.8 us -> 21.2 us
  waiting for transfers between devices: 11.9 us -> 13.3 us
    pallas_call x25, Pallas kernels: 22.8 us -> 21.2 us  [call(): pl.pallas_call(kernel, out_shape=outs, in_specs=in_specs, out_specs=out_s...]
    ppermute x20, waiting for transfers between devices: 11.9 us -> 13.3 us  [swap(): return lax.ppermute(value, axis, [(i, i ^ distance) for i in range(size)])]
  transfers between devices with their start and end apart: 20 -> 20, of which waited for: 9 -> 10; matrix products, arithmetic and copies ran while one was open for 0% -> 0% of each run, Pallas kernels for 35% -> 32%
where the time goes in v6:
time: 54.9 us; the launch traced here: 54.8 us
  Pallas kernels  21.2 us (39%)
  starting transfers between devices  19.4 us (35%)
  waiting for transfers between devices  13.3 us (24%)
  between operations  0.84 us (2%)
    pallas_call x25, Pallas kernels, call(): pl.pallas_call(kernel, out_shape=outs, in_specs=in_specs, out_specs=out_s...  21.2 us
    ppermute x20, starting transfers between devices, swap(): return lax.ppermute(value, axis, [(i, i ^ distance) for i in range(size)])  19.4 us
    ppermute x20, waiting for transfers between devices, swap(): return lax.ppermute(value, axis, [(i, i ^ distance) for i in range(size)])  13.3 us
  transfers between devices with their start and end apart: 20, of which 10 were waited for; matrix products, arithmetic and copies ran while one was open for 0% of the time, Pallas kernels for 32%

profile of v6, /device:TPU:0, one launch (start us, length us, event | category | flops | bytes accessed | tf_op | source)
XLA Modules:
  0.0 54.8 jit_solution(6190230072574857312)
XLA Ops:
  0.7 3.0 %collective-permute-start.1 = (bf16[16,2048]{1,0:T(8,128)(2,1)}, bf16[16,2048]{1,0:T(8,128)(2,1)S(1)}, u32[]{:S(2)}, u32[]{:S(2)}) collective-permute-start(bf16[16,2048]{1,0:T(8,128)(2,1)} %refs_0_.18), channel_id=1, source_target_pairs={{0,16},{8,24},{16,0},{24,8},{1,17},{9,25},{17,1},{25,9},{2,18},{10... | collective-permute-start | bytes 196616 | tf_op jit(solution)/shard_map/ppermute | solution.py:133
  3.7 0.1 collective-permute-start.4
  3.7 1.2 %shard_map.92.refs_5_.refs_8_ = bf16[2048,256]{1,0:T(8,128)(2,1)S(1)} custom-call(bf16[2048,256]{1,0:T(8,128)(2,1)} %source.1, bf16[2048,2048]{1,0:T(8,128)(2,1)} %refs_6_.1, bf16[2048,2048]{1,0:T(8,128)(2,1)} %refs_7_.3), custom_call_target="tpu_custom_call" | custom-call | bytes 17825792 | tf_op jit(solution)/shard_map/pallas_call | solution.py:137
  5.0 0.0 copy-start
  5.0 1.3 %collective-permute-done.1.refs_2_ = bf16[16,2048]{1,0:T(8,128)(2,1)S(1)} collective-permute-done((bf16[16,2048]{1,0:T(8,128)(2,1)}, bf16[16,2048]{1,0:T(8,128)(2,1)S(1)}, u32[]{:S(2)}, u32[]{:S(2)}) %collective-permute-start.1) | collective-permute-done | bytes 65568 | tf_op jit(solution)/shard_map/ppermute | solution.py:133
  6.3 0.5 collective-permute-start.3
  6.8 1.4 %collective-permute-done.4.refs_6_.refs_2_.refs_3_ = bf16[16,2048]{1,0:T(8,128)(2,1)S(1)} collective-permute-done((bf16[16,2048]{1,0:T(8,128)(2,1)}, bf16[16,2048]{1,0:T(8,128)(2,1)S(1)}, u32[]{:S(2)}, u32[]{:S(2)}) %collective-permute-start.4) | collective-permute-done | bytes 65568 | tf_op jit(solution)/shard_map/ppermute | solution.py:133
  8.2 0.5 shard_map.97
  8.7 0.7 %collective-permute-done.5.refs_7_.refs_3_.refs_4_ = bf16[16,2048]{1,0:T(8,128)(2,1)S(1)} collective-permute-done((bf16[16,2048]{1,0:T(8,128)(2,1)S(1)}, bf16[16,2048]{1,0:T(8,128)(2,1)S(1)}, u32[]{:S(2)}, u32[]{:S(2)}) %collective-permute-start.5) | collective-permute-done | bytes 65568 | tf_op jit(solution)/shard_map/ppermute | solution.py:133
  9.4 0.4 shard_map.98
  9.8 1.6 %collective-permute-start.7 = (bf16[64,768]{1,0:T(8,128)(2,1)S(1)}, bf16[64,768]{1,0:T(8,128)(2,1)S(1)}, u32[]{:S(2)}, u32[]{:S(2)}) collective-permute-start(bf16[64,768]{1,0:T(8,128)(2,1)S(1)} %shard_map.98), channel_id=1, source_target_pairs={{0,1},{1,0},{2,3},{3,2},{4,5},{5,4},{6,7},{7,6},{8,9},{9,8},{10,11... | collective-permute-start | bytes 294920 | tf_op jit(solution)/shard_map/ppermute | solution.py:133
  11.4 0.7 %shard_map.94.refs_5_ = bf16[64,768]{1,0:T(8,128)(2,1)S(1)} custom-call(bf16[16,2048]{1,0:T(8,128)(2,1)S(1)} %copy-done.3, bf16[16,2048]{1,0:T(8,128)(2,1)S(1)} %collective-permute-done.refs_1_, bf16[16,2048]{1,0:T(8,128)(2,1)S(1)} %collective-permute-done.1.refs_2_, bf16[16,2048]{1,0:T(8,128)(2,1)S(1)} %collective-permute-done.2.refs_3_, ...), custom_call_target="tpu_custom_call" | custom-call | flops 201326592 | bytes 3145728 | tf_op jit(solution)/shard_map/pallas_call | solution.py:137
  12.1 0.5 shard_map.105
  12.6 0.6 %collective-permute-start.10 = (bf16[64,512]{1,0:T(8,128)(2,1)S(1)}, bf16[64,512]{1,0:T(8,128)(2,1)S(1)}, u32[]{:S(2)}, u32[]{:S(2)}) collective-permute-start(bf16[64,512]{1,0:T(8,128)(2,1)S(1)} %shard_map.105), channel_id=1, source_target_pairs={{0,1},{1,0},{2,3},{3,2},{4,5},{5,4},{6,7},{7,6},{8,9},{9,8},{10,11... | collective-permute-start | bytes 196616 | tf_op jit(solution)/shard_map/ppermute | solution.py:133
  13.1 0.4 shard_map.95
  13.6 1.6 %collective-permute-start.6 = (bf16[64,512]{1,0:T(8,128)(2,1)S(1)}, bf16[64,512]{1,0:T(8,128)(2,1)S(1)}, u32[]{:S(2)}, u32[]{:S(2)}) collective-permute-start(bf16[64,512]{1,0:T(8,128)(2,1)S(1)} %shard_map.95), channel_id=1, source_target_pairs={{0,1},{1,0},{2,3},{3,2},{4,5},{5,4},{6,7},{7,6},{8,9},{9,8},{10,11... | collective-permute-start | bytes 196616 | tf_op jit(solution)/shard_map/ppermute | solution.py:133
  15.2 0.6 %shard_map.104.near = bf16[64,512]{1,0:T(8,128)(2,1)S(1)} custom-call(bf16[16,2048]{1,0:T(8,128)(2,1)S(1)} %copy-done.3, bf16[16,2048]{1,0:T(8,128)(2,1)S(1)} %collective-permute-done.refs_1_, bf16[16,2048]{1,0:T(8,128)(2,1)S(1)} %collective-permute-done.1.refs_2_, bf16[16,2048]{1,0:T(8,128)(2,1)S(1)} %collective-permute-done.2.refs_3_, ...), custom_call_target="tpu_custom_call" | custom-call | flops 134217728 | bytes 2097152 | tf_op jit(solution)/shard_map/pallas_call | solution.py:137
  15.8 0.6 %shard_map.96.near = bf16[64,512]{1,0:T(8,128)(2,1)S(1)} custom-call(bf16[16,2048]{1,0:T(8,128)(2,1)S(1)} %copy-done.3, bf16[16,2048]{1,0:T(8,128)(2,1)S(1)} %collective-permute-done.refs_1_, bf16[16,2048]{1,0:T(8,128)(2,1)S(1)} %collective-permute-done.1.refs_2_, bf16[16,2048]{1,0:T(8,128)(2,1)S(1)} %collective-permute-done.2.refs_3_, ...), custom_call_target="tpu_custom_call" | custom-call | flops 134217728 | bytes 2097152 | tf_op jit(solution)/shard_map/pallas_call | solution.py:137
  16.4 0.6 %shard_map.93.near = bf16[64,512]{1,0:T(8,128)(2,1)S(1)} custom-call(bf16[16,2048]{1,0:T(8,128)(2,1)S(1)} %copy-done.3, bf16[16,2048]{1,0:T(8,128)(2,1)S(1)} %collective-permute-done.refs_1_, bf16[16,2048]{1,0:T(8,128)(2,1)S(1)} %collective-permute-done.1.refs_2_, bf16[16,2048]{1,0:T(8,128)(2,1)S(1)} %collective-permute-done.2.refs_3_, ...), custom_call_target="tpu_custom_call" | custom-call | flops 134217728 | bytes 2097152 | tf_op jit(solution)/shard_map/pallas_call | solution.py:137
  17.1 3.7 %collective-permute-start.9 = (bf16[64,768]{1,0:T(8,128)(2,1)S(1)}, bf16[64,768]{1,0:T(8,128)(2,1)S(1)}, u32[]{:S(2)}, u32[]{:S(2)}) collective-permute-start(bf16[64,768]{1,0:T(8,128)(2,1)S(1)} %get-tuple-element.59), channel_id=1, source_target_pairs={{0,6},{1,7},{2,4},{3,5},{4,2},{5,3},{6,0},{7,1},{8,14},{9,15},{10,... | collective-permute-start | bytes 294920 | tf_op jit(solution)/shard_map/ppermute | solution.py:133
  20.8 0.1 collective-permute-start.11
  20.9 0.8 %collective-permute-start.12 = (bf16[64,768]{1,0:T(8,128)(2,1)S(1)}, bf16[64,768]{1,0:T(8,128)(2,1)S(1)}, u32[]{:S(2)}, u32[]{:S(2)}) collective-permute-start(bf16[64,768]{1,0:T(8,128)(2,1)S(1)} %shard_map.100), channel_id=1, source_target_pairs={{0,2},{1,3},{2,0},{3,1},{4,6},{5,7},{6,4},{7,5},{8,10},{9,11},{10,... | collective-permute-start | bytes 294920 | tf_op jit(solution)/shard_map/ppermute | solution.py:133
  21.8 0.4 shard_map.103
  22.2 0.6 %collective-permute-start.8 = (bf16[64,512]{1,0:T(8,128)(2,1)S(1)}, bf16[64,512]{1,0:T(8,128)(2,1)S(1)}, u32[]{:S(2)}, u32[]{:S(2)}) collective-permute-start(bf16[64,512]{1,0:T(8,128)(2,1)S(1)} %shard_map.103), channel_id=1, source_target_pairs={{0,1},{1,0},{2,3},{3,2},{4,5},{5,4},{6,7},{7,6},{8,9},{9,8},{10,11... | collective-permute-start | bytes 196616 | tf_op jit(solution)/shard_map/ppermute | solution.py:133
  22.8 0.2 shard_map.102.refs_0_
  23.0 0.6 %shard_map.101.near = bf16[64,512]{1,0:T(8,128)(2,1)S(1)} custom-call(bf16[16,2048]{1,0:T(8,128)(2,1)S(1)} %copy-done.3, bf16[16,2048]{1,0:T(8,128)(2,1)S(1)} %collective-permute-done.refs_1_, bf16[16,2048]{1,0:T(8,128)(2,1)S(1)} %collective-permute-done.1.refs_2_, bf16[16,2048]{1,0:T(8,128)(2,1)S(1)} %collective-permute-done.2.refs_3_, ...), custom_call_target="tpu_custom_call" | custom-call | flops 134217728 | bytes 2097152 | tf_op jit(solution)/shard_map/pallas_call | solution.py:137
  23.6 2.9 %collective-permute-done.8.far = bf16[64,512]{1,0:T(8,128)(2,1)S(1)} collective-permute-done((bf16[64,512]{1,0:T(8,128)(2,1)S(1)}, bf16[64,512]{1,0:T(8,128)(2,1)S(1)}, u32[]{:S(2)}, u32[]{:S(2)}) %collective-permute-start.8) | collective-permute-done | bytes 65568 | tf_op jit(solution)/shard_map/ppermute | solution.py:133
  26.5 2.0 %collective-permute-done.11.refs_1_ = bf16[64,768]{1,0:T(8,128)(2,1)S(1)} collective-permute-done((bf16[64,768]{1,0:T(8,128)(2,1)S(1)}, bf16[64,768]{1,0:T(8,128)(2,1)S(1)}, u32[]{:S(2)}, u32[]{:S(2)}) %collective-permute-start.11) | collective-permute-done | bytes 98336 | tf_op jit(solution)/shard_map/ppermute | solution.py:133
  28.5 1.1 %shard_map.107.refs_0_.refs_5_.refs_2_.refs_7_ = bf16[64,768]{1,0:T(8,128)(2,1)S(1)} custom-call(bf16[64,512]{1,0:T(8,128)(2,1)S(1)} %shard_map.101.near, bf16[64,512]{1,0:T(8,128)(2,1)S(1)} %collective-permute-done.8.far, bf16[64,256]{1,0:T(8,128)(2,1)S(1)} %get-tuple-element.49.pair, bf16[64,768]{1,0:T(8,128)(2,1)S(1)} %collective-permute-done.9.refs_0_, ...), custom_call_target="tpu_custom_call" | custom-call | flops 25165824 | bytes 786432 | tf_op jit(solution)/shard_map/pallas_call | solution.py:137
  29.6 0.6 %collective-permute-start.13 = (bf16[64,768]{1,0:T(8,128)(2,1)S(1)}, bf16[64,768]{1,0:T(8,128)(2,1)S(1)}, u32[]{:S(2)}, u32[]{:S(2)}) collective-permute-start(bf16[64,768]{1,0:T(8,128)(2,1)S(1)} %shard_map.107.refs_0_.refs_5_.refs_2_.refs_7_), channel_id=1, source_target_pairs={{0,2},{1,3},{2,0},{3,1},{4,6},{5,7},{6,4},{7,5},{8,10},{9,11},{10,... | collective-permute-start | bytes 294920 | tf_op jit(solution)/shard_map/ppermute | solution.py:133
  30.2 2.6 %collective-permute-start.16 = (bf16[64,768]{1,0:T(8,128)(2,1)S(1)}, bf16[64,768]{1,0:T(8,128)(2,1)S(1)}, u32[]{:S(2)}, u32[]{:S(2)}) collective-permute-start(bf16[64,768]{1,0:T(8,128)(2,1)S(1)} %shard_map.107.refs_0_.refs_5_.refs_2_.refs_7_), channel_id=1, source_target_pairs={{0,4},{1,5},{2,6},{3,7},{4,0},{5,1},{6,2},{7,3},{8,12},{9,13},{10,... | collective-permute-start | bytes 294920 | tf_op jit(solution)/shard_map/ppermute | solution.py:133
  32.8 1.3 %collective-permute-start.15 = (bf16[64,768]{1,0:T(8,128)(2,1)S(1)}, bf16[64,768]{1,0:T(8,128)(2,1)S(1)}, u32[]{:S(2)}, u32[]{:S(2)}) collective-permute-start(bf16[64,768]{1,0:T(8,128)(2,1)S(1)} %shard_map.107.refs_0_.refs_5_.refs_2_.refs_7_), channel_id=1, source_target_pairs={{0,6},{1,7},{2,4},{3,5},{4,2},{5,3},{6,0},{7,1},{8,14},{9,15},{10,... | collective-permute-start | bytes 294920 | tf_op jit(solution)/shard_map/ppermute | solution.py:133
  34.1 0.7 %collective-permute-done.13.refs_1_.refs_6_.refs_5_.refs_10_ = bf16[64,768]{1,0:T(8,128)(2,1)S(1)} collective-permute-done((bf16[64,768]{1,0:T(8,128)(2,1)S(1)}, bf16[64,768]{1,0:T(8,128)(2,1)S(1)}, u32[]{:S(2)}, u32[]{:S(2)}) %collective-permute-start.13) | collective-permute-done | bytes 98336 | tf_op jit(solution)/shard_map/ppermute | solution.py:133
  34.8 0.5 collective-permute-start.14
  35.3 2.6 %shard_map.109 = (bf16[2048,2048]{1,0:T(8,128)(2,1)}, bf16[2048,2048]{1,0:T(8,128)(2,1)}, f32[64,2048]{1,0:T(8,128)S(1)}, f32[64,2048]{1,0:T(8,128)S(1)}) custom-call(bf16[2048,64]{1,0:T(8,128)(2,1)S(1)} %shard_map.102.refs_0_, bf16[16,2048]{1,0:T(8,128)(2,1)S(1)} %copy-done.2, bf16[16,2048]{1,0:T(8,128)(2,1)S(1)} %collective-permute-done.3.refs_5_.refs_1_.refs_2_, ...), custom_call_target="tpu_custom_call" | custom-call | flops 536870912 | bytes 8388608 | tf_op jit(solution)/shard_map/pallas_call | solution.py:137
  37.9 2.0 %collective-permute-done.16.refs_1_.refs_6_.refs_4_.refs_9_ = bf16[64,768]{1,0:T(8,128)(2,1)S(1)} collective-permute-done((bf16[64,768]{1,0:T(8,128)(2,1)S(1)}, bf16[64,768]{1,0:T(8,128)(2,1)S(1)}, u32[]{:S(2)}, u32[]{:S(2)}) %collective-permute-start.16) | collective-permute-done | bytes 98336 | tf_op jit(solution)/shard_map/ppermute | solution.py:133
  40.0 0.5 collective-permute-start.17
  40.5 3.6 %shard_map.111 = (bf16[2048,2048]{1,0:T(8,128)(2,1)}, bf16[2048,2048]{1,0:T(8,128)(2,1)}, f32[64,2048]{1,0:T(8,128)S(1)}, f32[64,2048]{1,0:T(8,128)S(1)}) custom-call(bf16[2048,64]{1,0:T(8,128)(2,1)S(1)} %shard_map.102.refs_0_, bf16[16,2048]{1,0:T(8,128)(2,1)S(1)} %copy-done.2, ...), custom_call_target="tpu_custom_call", output_to_operand_aliasing={{0}: (12, {}), {1}: (13, {})} | custom-call | flops 536870912 | bytes 8388608 | tf_op jit(solution)/shard_map/pallas_call | solution.py:137
  44.1 1.1 %shard_map.112 = (f32[64,2048]{1,0:T(8,128)S(1)}, f32[64,2048]{1,0:T(8,128)S(1)}) custom-call(bf16[64,1280]{1,0:T(8,128)(2,1)S(1)} %collective-permute-done.14.refs_7_.refs_0_.refs_5_, bf16[2048,2048]{1,0:T(8,128)(2,1)S(1)} %copy-done.1, bf16[2048,2048]{1,0:T(8,128)(2,1)S(1)} %copy-done, f32[64,2048]{1,0:T(8,128)S(1)} %get-tuple-element.70.refs_3_, ...), custom_call_target="tpu_custom_call" | custom-call | flops 268435456 | bytes 4194304 | tf_op jit(solution)/shard_map/pallas_call | solution.py:137
  45.3 0.1 collective-permute-done.17.refs_1_.refs_6_
  45.4 1.4 %shard_map.113 = (bf16[64,2048]{1,0:T(8,128)(2,1)S(1)}, bf16[64,2048]{1,0:T(8,128)(2,1)S(1)}) custom-call(bf16[64,1280]{1,0:T(8,128)(2,1)S(1)} %collective-permute-done.14.refs_7_.refs_0_.refs_5_, bf16[64,1280]{1,0:T(8,128)(2,1)S(1)} %collective-permute-done.17.refs_1_.refs_6_, bf16[64,768]{1,0:T(8,128)(2,1)S(1)} %shard_map.107.refs_0_.refs_5_.refs_2_.refs_7_, ...), custom_call_target="tpu_custom_call" | custom-call | flops 570425344 | bytes 8912896 | tf_op jit(solution)/shard_map/pallas_call | solution.py:137
  46.8 0.1 collective-permute-start.18
  46.9 1.5 %collective-permute-done.18.far = bf16[64,2048]{1,0:T(8,128)(2,1)S(1)} collective-permute-done((bf16[64,2048]{1,0:T(8,128)(2,1)S(1)}, bf16[64,2048]{1,0:T(8,128)(2,1)S(1)}, u32[]{:S(2)}, u32[]{:S(2)}) %collective-permute-start.18) | collective-permute-done | bytes 262176 | tf_op jit(solution)/shard_map/ppermute | solution.py:133
  48.4 0.1 shard_map.114
  48.5 1.3 %collective-permute-start.19 = (bf16[32,2048]{1,0:T(8,128)(2,1)S(1)}, bf16[32,2048]{1,0:T(8,128)(2,1)S(1)}, u32[]{:S(2)}, u32[]{:S(2)}) collective-permute-start(bf16[32,2048]{1,0:T(8,128)(2,1)S(1)} %get-tuple-element.77), channel_id=1, source_target_pairs={{0,16},{8,24},{16,0},{24,8},{1,17},{9,25},{17,1},{25,9},{2,18},{10... | collective-permute-start | bytes 393224 | tf_op jit(solution)/shard_map/ppermute | solution.py:133
  49.8 3.6 %shard_map.116 = (bf16[2048,2048]{1,0:T(8,128)(2,1)}, bf16[2048,2048]{1,0:T(8,128)(2,1)}, bf16[2048,256]{1,0:T(8,128)(2,1)}) custom-call(bf16[2048,64]{1,0:T(8,128)(2,1)S(1)} %shard_map.102.refs_0_, bf16[16,2048]{1,0:T(8,128)(2,1)S(1)} %copy-done.2, ...), custom_call_target="tpu_custom_call", output_to_operand_aliasing={{0}: (11, {}), {1}: (12, {})} | custom-call | flops 805306368 | bytes 12582912 | tf_op jit(solution)/shard_map/pallas_call | solution.py:137
  53.4 0.7 %collective-permute-done.19.refs_1_ = bf16[32,2048]{1,0:T(8,128)(2,1)S(1)} collective-permute-done((bf16[32,2048]{1,0:T(8,128)(2,1)S(1)}, bf16[32,2048]{1,0:T(8,128)(2,1)S(1)}, u32[]{:S(2)}, u32[]{:S(2)}) %collective-permute-start.19) | collective-permute-done | bytes 131104 | tf_op jit(solution)/shard_map/ppermute | solution.py:133
  54.1 0.7 %shard_map.115 = (bf16[16,2048]{1,0:T(8,128)(2,1)}, bf16[16,2048]{1,0:T(8,128)(2,1)}) custom-call(bf16[32,2048]{1,0:T(8,128)(2,1)S(1)} %get-tuple-element.76.refs_0_, bf16[32,2048]{1,0:T(8,128)(2,1)S(1)} %collective-permute-done.19.refs_1_), custom_call_target="tpu_custom_call" | custom-call | flops 262144 | bytes 524288 | tf_op jit(solution)/shard_map/pallas_call | solution.py:137
  (25 shorter events, 0.2 us)
Async XLA Ops:
  0.6 7.5 %copy-start.3 = (bf16[16,2048]{1,0:T(8,128)(2,1)S(1)}, bf16[16,2048]{1,0:T(8,128)(2,1)}, u32[]{:S(2)}) copy-start(bf16[16,2048]{1,0:T(8,128)(2,1)} %refs_0_.18) | copy-start | bytes 196612
  0.6 5.6 %copy-start.2 = (bf16[16,2048]{1,0:T(8,128)(2,1)S(1)}, bf16[16,2048]{1,0:T(8,128)(2,1)}, u32[]{:S(2)}) copy-start(bf16[16,2048]{1,0:T(8,128)(2,1)} %refs_1_.7) | copy-start | bytes 196612
  0.7 7.5 %copy-start.1 = (bf16[2048,2048]{1,0:T(8,128)(2,1)S(1)}, bf16[2048,2048]{1,0:T(8,128)(2,1)}, u32[]{:S(2)}) copy-start(bf16[2048,2048]{1,0:T(8,128)(2,1)} %refs_6_.1) | copy-start | bytes 25165828
  0.7 5.6 %collective-permute-start.1 = (bf16[16,2048]{1,0:T(8,128)(2,1)}, bf16[16,2048]{1,0:T(8,128)(2,1)S(1)}, u32[]{:S(2)}, u32[]{:S(2)}) collective-permute-start(bf16[16,2048]{1,0:T(8,128)(2,1)} %refs_0_.18), channel_id=1, source_target_pairs={{0,16},{8,24},{16,0},{24,8},{1,17},{9,25},{17,1},{25,9},{2,18},{10... | collective-permute-start | bytes 196616 | tf_op jit(solution)/shard_map/ppermute | solution.py:133
  3.7 4.5 %collective-permute-start.4 = (bf16[16,2048]{1,0:T(8,128)(2,1)}, bf16[16,2048]{1,0:T(8,128)(2,1)S(1)}, u32[]{:S(2)}, u32[]{:S(2)}) collective-permute-start(bf16[16,2048]{1,0:T(8,128)(2,1)} %refs_1_.7), channel_id=1, source_target_pairs={{0,16},{8,24},{16,0},{24,8},{1,17},{9,25},{17,1},{25,9},{2,18},{10... | collective-permute-start | bytes 196616 | tf_op jit(solution)/shard_map/ppermute | solution.py:133
  3.7 4.4 %collective-permute-start = (bf16[16,2048]{1,0:T(8,128)(2,1)}, bf16[16,2048]{1,0:T(8,128)(2,1)S(1)}, u32[]{:S(2)}, u32[]{:S(2)}) collective-permute-start(bf16[16,2048]{1,0:T(8,128)(2,1)} %refs_0_.18), channel_id=1, source_target_pairs={{0,8},{8,0},{16,24},{24,16},{1,9},{9,1},{17,25},{25,17},{2,10},{10... | collective-permute-start | bytes 196616 | tf_op jit(solution)/shard_map/ppermute | solution.py:133
  5.0 4.4 %copy-start = (bf16[2048,2048]{1,0:T(8,128)(2,1)S(1)}, bf16[2048,2048]{1,0:T(8,128)(2,1)}, u32[]{:S(2)}) copy-start(bf16[2048,2048]{1,0:T(8,128)(2,1)} %refs_7_.3) | copy-start | bytes 25165828
  6.3 1.9 %collective-permute-start.2 = (bf16[16,2048]{1,0:T(8,128)(2,1)S(1)}, bf16[16,2048]{1,0:T(8,128)(2,1)S(1)}, u32[]{:S(2)}, u32[]{:S(2)}) collective-permute-start(bf16[16,2048]{1,0:T(8,128)(2,1)S(1)} %collective-permute-done.1.refs_2_), channel_id=1, source_target_pairs={{0,8},{8,0},{16,24},{24,16},{1,9},{9,1},{17,25},{25,17},{2,10},{10... | collective-permute-start | bytes 196616 | tf_op jit(solution)/shard_map/ppermute | solution.py:133
  6.3 2.4 %collective-permute-start.3 = (bf16[16,2048]{1,0:T(8,128)(2,1)S(1)}, bf16[16,2048]{1,0:T(8,128)(2,1)S(1)}, u32[]{:S(2)}, u32[]{:S(2)}) collective-permute-start(bf16[16,2048]{1,0:T(8,128)(2,1)S(1)} %copy-done.2), channel_id=1, source_target_pairs={{0,8},{8,0},{16,24},{24,16},{1,9},{9,1},{17,25},{25,17},{2,10},{10... | collective-permute-start | bytes 196616 | tf_op jit(solution)/shard_map/ppermute | solution.py:133
  8.1 1.3 %collective-permute-start.5 = (bf16[16,2048]{1,0:T(8,128)(2,1)S(1)}, bf16[16,2048]{1,0:T(8,128)(2,1)S(1)}, u32[]{:S(2)}, u32[]{:S(2)}) collective-permute-start(bf16[16,2048]{1,0:T(8,128)(2,1)S(1)} %collective-permute-done.4.refs_6_.refs_2_.refs_3_), channel_id=1, source_target_pairs={{0,8},{8,0},{16,24},{24,16},{1,9},{9,1},{17,25},{25,17},{2,10},{10... | collective-permute-start | bytes 196616 | tf_op jit(solution)/shard_map/ppermute | solution.py:133
  9.8 7.2 %collective-permute-start.7 = (bf16[64,768]{1,0:T(8,128)(2,1)S(1)}, bf16[64,768]{1,0:T(8,128)(2,1)S(1)}, u32[]{:S(2)}, u32[]{:S(2)}) collective-permute-start(bf16[64,768]{1,0:T(8,128)(2,1)S(1)} %shard_map.98), channel_id=1, source_target_pairs={{0,1},{1,0},{2,3},{3,2},{4,5},{5,4},{6,7},{7,6},{8,9},{9,8},{10,11... | collective-permute-start | bytes 294920 | tf_op jit(solution)/shard_map/ppermute | solution.py:133
  12.6 8.2 %collective-permute-start.10 = (bf16[64,512]{1,0:T(8,128)(2,1)S(1)}, bf16[64,512]{1,0:T(8,128)(2,1)S(1)}, u32[]{:S(2)}, u32[]{:S(2)}) collective-permute-start(bf16[64,512]{1,0:T(8,128)(2,1)S(1)} %shard_map.105), channel_id=1, source_target_pairs={{0,1},{1,0},{2,3},{3,2},{4,5},{5,4},{6,7},{7,6},{8,9},{9,8},{10,11... | collective-permute-start | bytes 196616 | tf_op jit(solution)/shard_map/ppermute | solution.py:133
  13.6 7.3 %collective-permute-start.6 = (bf16[64,512]{1,0:T(8,128)(2,1)S(1)}, bf16[64,512]{1,0:T(8,128)(2,1)S(1)}, u32[]{:S(2)}, u32[]{:S(2)}) collective-permute-start(bf16[64,512]{1,0:T(8,128)(2,1)S(1)} %shard_map.95), channel_id=1, source_target_pairs={{0,1},{1,0},{2,3},{3,2},{4,5},{5,4},{6,7},{7,6},{8,9},{9,8},{10,11... | collective-permute-start | bytes 196616 | tf_op jit(solution)/shard_map/ppermute | solution.py:133
  17.1 9.4 %collective-permute-start.9 = (bf16[64,768]{1,0:T(8,128)(2,1)S(1)}, bf16[64,768]{1,0:T(8,128)(2,1)S(1)}, u32[]{:S(2)}, u32[]{:S(2)}) collective-permute-start(bf16[64,768]{1,0:T(8,128)(2,1)S(1)} %get-tuple-element.59), channel_id=1, source_target_pairs={{0,6},{1,7},{2,4},{3,5},{4,2},{5,3},{6,0},{7,1},{8,14},{9,15},{10,... | collective-permute-start | bytes 294920 | tf_op jit(solution)/shard_map/ppermute | solution.py:133
  20.8 7.7 %collective-permute-start.11 = (bf16[64,768]{1,0:T(8,128)(2,1)S(1)}, bf16[64,768]{1,0:T(8,128)(2,1)S(1)}, u32[]{:S(2)}, u32[]{:S(2)}) collective-permute-start(bf16[64,768]{1,0:T(8,128)(2,1)S(1)} %shard_map.106), channel_id=1, source_target_pairs={{0,4},{1,5},{2,6},{3,7},{4,0},{5,1},{6,2},{7,3},{8,12},{9,13},{10,... | collective-permute-start | bytes 294920 | tf_op jit(solution)/shard_map/ppermute | solution.py:133
  20.9 7.6 %collective-permute-start.12 = (bf16[64,768]{1,0:T(8,128)(2,1)S(1)}, bf16[64,768]{1,0:T(8,128)(2,1)S(1)}, u32[]{:S(2)}, u32[]{:S(2)}) collective-permute-start(bf16[64,768]{1,0:T(8,128)(2,1)S(1)} %shard_map.100), channel_id=1, source_target_pairs={{0,2},{1,3},{2,0},{3,1},{4,6},{5,7},{6,4},{7,5},{8,10},{9,11},{10,... | collective-permute-start | bytes 294920 | tf_op jit(solution)/shard_map/ppermute | solution.py:133
  22.2 4.3 %collective-permute-start.8 = (bf16[64,512]{1,0:T(8,128)(2,1)S(1)}, bf16[64,512]{1,0:T(8,128)(2,1)S(1)}, u32[]{:S(2)}, u32[]{:S(2)}) collective-permute-start(bf16[64,512]{1,0:T(8,128)(2,1)S(1)} %shard_map.103), channel_id=1, source_target_pairs={{0,1},{1,0},{2,3},{3,2},{4,5},{5,4},{6,7},{7,6},{8,9},{9,8},{10,11... | collective-permute-start | bytes 196616 | tf_op jit(solution)/shard_map/ppermute | solution.py:133
  29.6 5.1 %collective-permute-start.13 = (bf16[64,768]{1,0:T(8,128)(2,1)S(1)}, bf16[64,768]{1,0:T(8,128)(2,1)S(1)}, u32[]{:S(2)}, u32[]{:S(2)}) collective-permute-start(bf16[64,768]{1,0:T(8,128)(2,1)S(1)} %shard_map.107.refs_0_.refs_5_.refs_2_.refs_7_), channel_id=1, source_target_pairs={{0,2},{1,3},{2,0},{3,1},{4,6},{5,7},{6,4},{7,5},{8,10},{9,11},{10,... | collective-permute-start | bytes 294920 | tf_op jit(solution)/shard_map/ppermute | solution.py:133
  30.2 9.7 %collective-permute-start.16 = (bf16[64,768]{1,0:T(8,128)(2,1)S(1)}, bf16[64,768]{1,0:T(8,128)(2,1)S(1)}, u32[]{:S(2)}, u32[]{:S(2)}) collective-permute-start(bf16[64,768]{1,0:T(8,128)(2,1)S(1)} %shard_map.107.refs_0_.refs_5_.refs_2_.refs_7_), channel_id=1, source_target_pairs={{0,4},{1,5},{2,6},{3,7},{4,0},{5,1},{6,2},{7,3},{8,12},{9,13},{10,... | collective-permute-start | bytes 294920 | tf_op jit(solution)/shard_map/ppermute | solution.py:133
  32.8 7.2 %collective-permute-start.15 = (bf16[64,768]{1,0:T(8,128)(2,1)S(1)}, bf16[64,768]{1,0:T(8,128)(2,1)S(1)}, u32[]{:S(2)}, u32[]{:S(2)}) collective-permute-start(bf16[64,768]{1,0:T(8,128)(2,1)S(1)} %shard_map.107.refs_0_.refs_5_.refs_2_.refs_7_), channel_id=1, source_target_pairs={{0,6},{1,7},{2,4},{3,5},{4,2},{5,3},{6,0},{7,1},{8,14},{9,15},{10,... | collective-permute-start | bytes 294920 | tf_op jit(solution)/shard_map/ppermute | solution.py:133
  34.8 5.8 %collective-permute-start.14 = (bf16[64,1280]{1,0:T(8,128)(2,1)S(1)}, bf16[64,1280]{1,0:T(8,128)(2,1)S(1)}, u32[]{:S(2)}, u32[]{:S(2)}) collective-permute-start(bf16[64,1280]{1,0:T(8,128)(2,1)S(1)} %shard_map.108), channel_id=1, source_target_pairs={{0,1},{1,0},{2,3},{3,2},{4,5},{5,4},{6,7},{7,6},{8,9},{9,8},{10,11... | collective-permute-start | bytes 491528 | tf_op jit(solution)/shard_map/ppermute | solution.py:133
  40.0 5.4 %collective-permute-start.17 = (bf16[64,1280]{1,0:T(8,128)(2,1)S(1)}, bf16[64,1280]{1,0:T(8,128)(2,1)S(1)}, u32[]{:S(2)}, u32[]{:S(2)}) collective-permute-start(bf16[64,1280]{1,0:T(8,128)(2,1)S(1)} %shard_map.110), channel_id=1, source_target_pairs={{0,1},{1,0},{2,3},{3,2},{4,5},{5,4},{6,7},{7,6},{8,9},{9,8},{10,11... | collective-permute-start | bytes 491528 | tf_op jit(solution)/shard_map/ppermute | solution.py:133
  46.8 1.6 %collective-permute-start.18 = (bf16[64,2048]{1,0:T(8,128)(2,1)S(1)}, bf16[64,2048]{1,0:T(8,128)(2,1)S(1)}, u32[]{:S(2)}, u32[]{:S(2)}) collective-permute-start(bf16[64,2048]{1,0:T(8,128)(2,1)S(1)} %get-tuple-element.75), channel_id=1, source_target_pairs={{0,8},{8,0},{16,24},{24,16},{1,9},{9,1},{17,25},{25,17},{2,10},{10... | collective-permute-start | bytes 786440 | tf_op jit(solution)/shard_map/ppermute | solution.py:133
  48.5 5.6 %collective-permute-start.19 = (bf16[32,2048]{1,0:T(8,128)(2,1)S(1)}, bf16[32,2048]{1,0:T(8,128)(2,1)S(1)}, u32[]{:S(2)}, u32[]{:S(2)}) collective-permute-start(bf16[32,2048]{1,0:T(8,128)(2,1)S(1)} %get-tuple-element.77), channel_id=1, source_target_pairs={{0,16},{8,24},{16,0},{24,8},{1,17},{9,25},{17,1},{25,9},{2,18},{10... | collective-permute-start | bytes 393224 | tf_op jit(solution)/shard_map/ppermute | solution.py:133
